TPU v7x, 32 devices: a whole 2x2x4 slice. The times are simulated.
32 devices in a mesh: section: 2 (over core), dp: 4 (over z), mp: 4 (over y, x).
Axes of the slice: x: 2, y: 2, z: 4, core: 2. Of those that a mesh axis runs over, the one named last changes fastest.
Arguments:
- inputs: bfloat16 [2, 4, 4, 1024, 512], P('section', None, 'dp', 'mp'), may hold values from -6 to 6
- lengths: int32 [2, 4, 4, 8], P('section', None, 'dp'), may hold values from 1 to 1024, as said below
- routes_self: int32 [2, 4, 4, 1024, 2], P('section', None, 'dp', 'mp'), may hold values from 0 to 7, all different within a row; in each aligned block of 256 rows (0 to 255, 256 to 511, ..., all dimensions but the last counted through in order) at most 128 rows name the same one
- routes_cross: int32 [4, 4, 1024, 2], P(None, 'dp', 'mp'), may hold values from 0 to 7, all different within a row; in each aligned block of 256 rows (0 to 255, 256 to 511, ..., all dimensions but the last counted through in order) at most 128 rows name the same one
- gains: bfloat16 [2, 3, 512], P('section'), may hold values from 0.5 to 1.5
- router_self: bfloat16 [2, 512, 8], P('section'), may hold values from -0.19921875 to 0.19921875
- query_self: bfloat16 [2, 8, 512, 64], P('section', 'mp'), may hold values from -0.25 to 0.25
- keyval_self: bfloat16 [2, 512, 128], P('section'), may hold values from -0.25 to 0.25
- output_self: bfloat16 [2, 8, 64, 512], P('section', 'mp'), may hold values from -3 to 3
- ffn_in: bfloat16 [2, 512, 2048], P('section', None, 'mp'), may hold values from -0.25 to 0.25
- ffn_out: bfloat16 [2, 2048, 512], P('section', 'mp'), may hold values from -0.1875 to 0.1875
- router_cross: bfloat16 [512, 8], replicated, may hold values from -0.19921875 to 0.19921875
- query_cross: bfloat16 [8, 512, 64], P('mp'), may hold values from -0.25 to 0.25
- keyval_cross: bfloat16 [512, 128], replicated, may hold values from -0.25 to 0.25
- output_cross: bfloat16 [8, 64, 512], P('mp'), may hold values from -3 to 3
- cotangent: bfloat16 [4, 4, 1024, 512], P(None, 'dp', 'mp'), may hold values from -6 to 6
Outputs:
- outputs: bfloat16 [2, 4, 4, 1024, 512], P('section', None, 'dp', 'mp')
- grad_inputs: float32 [2, 4, 4, 1024, 512], P('section', None, 'dp', 'mp')
- grad_gains: float32 [2, 3, 512], P(None, None, ('section', 'dp'))
- grad_router_self: float32 [2, 512, 8], P(None, ('section', 'dp'))
- grad_query_self: float32 [2, 8, 512, 64], P(None, 'mp', ('section', 'dp'))
- grad_keyval_self: float32 [2, 512, 128], P(None, ('section', 'dp'))
- grad_output_self: float32 [2, 8, 64, 512], P(None, 'mp', None, ('section', 'dp'))
- grad_ffn_in: float32 [2, 512, 2048], P(None, ('section', 'dp'), 'mp')
- grad_ffn_out: float32 [2, 2048, 512], P(None, 'mp', ('section', 'dp'))
- grad_router_cross: float32 [512, 8], P(('section', 'dp'))
- grad_query_cross: float32 [8, 512, 64], P('mp', ('section', 'dp'))
- grad_keyval_cross: float32 [512, 128], P(('section', 'dp'))
- grad_output_cross: float32 [8, 64, 512], P('mp', None, ('section', 'dp'))
Inputs may be any that keep to these rules, and one draw needn't show every extreme that they name: `routes_self`: in each aligned block of 256 tokens, no expert is named by more than 128 tokens, a bound that some block reaches; a token's two experts differ. `routes_cross`: in each aligned block of 256 tokens, no expert is named by more than 128 tokens, a bound that some block reaches; a token's two experts differ. Each row's 8 lengths sum to 1024.
All inputs are finite; a program needn't handle non-finite values.
Results may differ from a plain program's by a relative error of at most 0.02.
Values may be sent and summed in bfloat16 or wider, within the bound.
No kernel may reach another device: no remote copies, remote signals or barrier semaphores. Data moves between devices by JAX's collectives and lax.ppermute only.
A program may use at most 192 MiB of HBM per device.

v0:
```python
import jax
import jax.numpy as jnp
from jax import lax
from jax.sharding import PartitionSpec as P

FF = 2048


EPS = 1e-05
MASK_VALUE = -1000000000.0
SHARD_DIMS = (2, 1, 2, 1, 3, 1, 2, 0, 1, 0, 2)


def passed_along(value, axis, by):
    length = lax.axis_size(axis)
    pairs = [(i, i + by) for i in range(length) if 0 <= i + by < length]
    return lax.ppermute(value, axis, pairs)


def normalize(values, gain_row):
    center = values - jnp.mean(values, 1, keepdims=True)
    scaled = lax.rsqrt(jnp.mean(center * center, 1, keepdims=True) + EPS)
    unit_rows = center * scaled
    return (unit_rows * gain_row, unit_rows, scaled)


def normalize_back(upstream, unit_rows, scaled, gain_row):
    inner_grad = upstream * gain_row
    result = scaled * (
        inner_grad
        - jnp.mean(inner_grad, 1, keepdims=True)
        - unit_rows * jnp.mean(inner_grad * unit_rows, 1, keepdims=True)
    )
    return (result, jnp.sum(upstream * unit_rows, 0))


def segment_of(where_at, lengths):
    sentence_ends = jnp.cumsum(lengths)
    return jnp.sum((where_at[:, None] >= sentence_ends[None, :]).astype(jnp.int32), 1)


def gate_of(logits, routes):
    experts = logits.shape[1]
    picked = (routes[:, :, None] == lax.broadcasted_iota(jnp.int32, (1, 1, experts), 2)).astype(
        jnp.float32
    )
    chosen = jnp.sum(picked * logits[:, None, :], 2)
    return (jax.nn.softmax(chosen, 1), picked)


def slot_tables(routes, experts, capacity):
    tokens = routes.shape[0]
    flat_routes = routes.reshape(-1)
    onehot = (flat_routes[:, None] == lax.broadcasted_iota(jnp.int32, (1, experts), 1)).astype(
        jnp.int32
    )
    rank_in = jnp.sum((jnp.cumsum(onehot, 0) - onehot) * onehot, 1)
    target = flat_routes * capacity + rank_in
    slot_owner = (
        jnp.full((experts * capacity,), -1, jnp.int32)
        .at[target]
        .set(lax.iota(jnp.int32, 2 * tokens))
    )
    filled = slot_owner >= 0
    return (target, jnp.maximum(slot_owner, 0), filled)


def allowed_of(places_in, query_lengths, key_lengths, causal, key_count):
    key_places = lax.iota(jnp.int32, key_count)
    key_segments = segment_of(key_places, key_lengths)
    query_segments = segment_of(jnp.maximum(places_in, 0).reshape(-1), query_lengths).reshape(
        places_in.shape
    )
    allowed = (places_in[:, :, None] >= 0) & (
        query_segments[:, :, None] == key_segments[None, None, :]
    )
    return allowed & (
        (key_places[None, None, :] <= places_in[:, :, None]) | jnp.logical_not(causal)
    )


def attend(query_rows, key_rows, weights, routes, query_lengths, key_lengths, causal):
    router, w_query, w_keyval, w_output = weights
    tokens, model_width = query_rows.shape
    experts = router.shape[1]
    capacity = tokens // 2
    head_size = w_query.shape[2]
    score_scale = head_size ** (-0.5)
    keyval = jnp.dot(key_rows, w_keyval, preferred_element_type=jnp.float32).astype(jnp.bfloat16)
    keyval_all = lax.all_gather(keyval, "mp", axis=0, tiled=True)
    logits = jnp.dot(query_rows, router, preferred_element_type=jnp.float32)
    gate_values, picked = gate_of(logits, routes)
    target, assign, filled = slot_tables(routes, experts, capacity)
    token_of = assign // 2
    places = lax.axis_index("mp") * tokens + lax.iota(jnp.int32, tokens)
    sent_rows = query_rows[token_of].reshape(experts, capacity, model_width)
    sent_gates = (
        jnp.where(filled, gate_values.reshape(-1)[assign], 0.0)
        .astype(jnp.bfloat16)
        .reshape(experts, capacity)
    )
    sent_places = jnp.where(filled, places[token_of], -1).reshape(experts, capacity)
    rows_in, gates_in, places_in = (
        lax.all_to_all(sent_rows, "mp", split_axis=0, concat_axis=1, tiled=True),
        lax.all_to_all(sent_gates, "mp", split_axis=0, concat_axis=1, tiled=True),
        lax.all_to_all(sent_places, "mp", split_axis=0, concat_axis=1, tiled=True),
    )
    key_count = keyval_all.shape[0]
    allowed = allowed_of(places_in, query_lengths, key_lengths, causal, key_count)
    queries = jnp.einsum(
        "esd,edh->esh", rows_in, w_query, preferred_element_type=jnp.float32
    ).astype(jnp.bfloat16)
    scores = (
        jnp.einsum(
            "esh,kh->esk", queries, keyval_all[:, :head_size], preferred_element_type=jnp.float32
        )
        * score_scale
    )
    scores = jnp.where(allowed, scores, MASK_VALUE)
    row_max = jnp.max(scores, 2, keepdims=True)
    exp_scores = jnp.exp(scores - row_max)
    row_total = jnp.sum(exp_scores, 2, keepdims=True)
    probabilities = (exp_scores / row_total).astype(jnp.bfloat16)
    log_total = row_max + jnp.log(row_total)
    mixture_out = jnp.einsum(
        "esk,kh->esh", probabilities, keyval_all[:, head_size:], preferred_element_type=jnp.float32
    )
    gated_rows = (gates_in.astype(jnp.float32)[:, :, None] * mixture_out).astype(jnp.bfloat16)
    result = jnp.einsum(
        "esh,ehd->esd", gated_rows, w_output, preferred_element_type=jnp.float32
    ).astype(jnp.bfloat16)
    returned = lax.all_to_all(result, "mp", split_axis=1, concat_axis=0, tiled=True)
    output = jnp.sum(
        returned.reshape(experts * capacity, model_width)[target]
        .astype(jnp.float32)
        .reshape(tokens, 2, model_width),
        1,
    )
    residuals = (
        query_rows,
        key_rows,
        gate_values,
        picked,
        target,
        token_of,
        filled,
        rows_in,
        gates_in,
        places_in,
        queries,
        keyval_all,
        log_total,
        mixture_out,
        gated_rows,
    )
    return (output, residuals)


def attend_empty(query_rows, key_rows, weights):
    router, w_query, w_keyval, w_output = weights
    tokens, model_width = query_rows.shape
    experts = router.shape[1]
    capacity = tokens // 2
    used = w_query.shape[0]
    slots = experts * capacity // used
    head_size = w_query.shape[2]
    key_count = key_rows.shape[0] * lax.axis_size("mp")
    kept = (
        query_rows,
        key_rows,
        jnp.zeros((tokens, 2), jnp.float32),
        jnp.zeros((tokens, 2, experts), jnp.float32),
        jnp.zeros((2 * tokens,), jnp.int32),
        jnp.zeros((experts * capacity,), jnp.int32),
        jnp.zeros((experts * capacity,), jnp.bool_),
        jnp.zeros((used, slots, model_width), jnp.bfloat16),
        jnp.zeros((used, slots), jnp.bfloat16),
        jnp.full((used, slots), -1, jnp.int32),
        jnp.zeros((used, slots, head_size), jnp.bfloat16),
        jnp.zeros((key_count, 2 * head_size), jnp.bfloat16),
        jnp.zeros((used, slots, 1), jnp.float32),
        jnp.zeros((used, slots, head_size), jnp.float32),
        jnp.zeros((used, slots, head_size), jnp.bfloat16),
    )
    return (jnp.zeros((tokens, model_width), jnp.float32), kept)


def attend_back(upstream, residuals, weights, query_lengths, key_lengths, causal):
    router, w_query, w_keyval, w_output = weights
    (
        query_rows,
        key_rows,
        gate_values,
        picked,
        target,
        token_of,
        filled,
        rows_in,
        gates_in,
        places_in,
        queries,
        keyval_all,
        log_total,
        mixture_out,
        gated_rows,
    ) = residuals
    tokens, model_width = query_rows.shape
    experts = router.shape[1]
    capacity = tokens // 2
    head_size = w_query.shape[2]
    score_scale = head_size ** (-0.5)
    keys_part = keyval_all[:, :head_size]
    values_part = keyval_all[:, head_size:]
    upstream_rows = upstream.astype(jnp.bfloat16)
    slot_grads = jnp.where(
        filled[:, None], upstream_rows[token_of], jnp.zeros((), jnp.bfloat16)
    ).reshape(experts, capacity, model_width)
    grads_in = lax.all_to_all(slot_grads, "mp", split_axis=0, concat_axis=1, tiled=True)
    grad_gated = jnp.einsum("esd,ehd->esh", grads_in, w_output, preferred_element_type=jnp.float32)
    grad_w_output = jnp.einsum(
        "esh,esd->ehd", gated_rows, grads_in, preferred_element_type=jnp.float32
    )
    grad_mixture = (gates_in.astype(jnp.float32)[:, :, None] * grad_gated).astype(jnp.bfloat16)
    grad_gates_in = jnp.sum(mixture_out * grad_gated, 2).astype(jnp.bfloat16)
    allowed = allowed_of(places_in, query_lengths, key_lengths, causal, keyval_all.shape[0])
    scores = (
        jnp.einsum("esh,kh->esk", queries, keys_part, preferred_element_type=jnp.float32)
        * score_scale
    )
    scores = jnp.where(allowed, scores, MASK_VALUE)
    probabilities = jnp.exp(scores - log_total)
    grad_probs = jnp.einsum(
        "esh,kh->esk", grad_mixture, values_part, preferred_element_type=jnp.float32
    )
    grad_values = jnp.einsum(
        "esk,esh->kh",
        probabilities.astype(jnp.bfloat16),
        grad_mixture,
        preferred_element_type=jnp.float32,
    )
    inner_sum = jnp.sum(probabilities * grad_probs, 2, keepdims=True)
    grad_scores = (probabilities * (grad_probs - inner_sum)).astype(jnp.bfloat16)
    grad_queries = (
        jnp.einsum("esk,kh->esh", grad_scores, keys_part, preferred_element_type=jnp.float32)
        * score_scale
    ).astype(jnp.bfloat16)
    grad_keys = (
        jnp.einsum("esk,esh->kh", grad_scores, queries, preferred_element_type=jnp.float32)
        * score_scale
    )
    grad_w_query = jnp.einsum(
        "esd,esh->edh", rows_in, grad_queries, preferred_element_type=jnp.float32
    )
    grad_rows_in = jnp.einsum(
        "esh,edh->esd", grad_queries, w_query, preferred_element_type=jnp.float32
    ).astype(jnp.bfloat16)
    back_rows, back_gates = (
        lax.all_to_all(grad_rows_in, "mp", split_axis=1, concat_axis=0, tiled=True),
        lax.all_to_all(grad_gates_in, "mp", split_axis=1, concat_axis=0, tiled=True),
    )
    grad_keyval = lax.psum_scatter(
        jnp.concatenate([grad_keys, grad_values], 1), "mp", scatter_dimension=0, tiled=True
    ).astype(jnp.bfloat16)
    grad_query_rows = jnp.sum(
        back_rows.reshape(experts * capacity, model_width)[target]
        .astype(jnp.float32)
        .reshape(tokens, 2, model_width),
        1,
    )
    grad_gates = back_gates.reshape(-1)[target].astype(jnp.float32).reshape(tokens, 2)
    grad_chosen = gate_values * (grad_gates - jnp.sum(gate_values * grad_gates, 1, keepdims=True))
    grad_logits = jnp.sum(picked * grad_chosen[:, :, None], 1)
    grad_router = lax.dot_general(
        query_rows.astype(jnp.float32),
        grad_logits,
        (((0,), (0,)), ((), ())),
        precision=lax.Precision.HIGHEST,
    )
    grad_query_rows = grad_query_rows + lax.dot_general(
        grad_logits,
        router.astype(jnp.float32),
        (((1,), (1,)), ((), ())),
        precision=lax.Precision.HIGHEST,
    )
    grad_w_keyval = lax.dot_general(
        key_rows, grad_keyval, (((0,), (0,)), ((), ())), preferred_element_type=jnp.float32
    )
    grad_key_rows = lax.dot_general(
        grad_keyval, w_keyval, (((1,), (1,)), ((), ())), preferred_element_type=jnp.float32
    )
    return (
        grad_query_rows,
        grad_key_rows,
        (grad_router, grad_w_query, grad_w_keyval, grad_w_output),
    )


def gelu_exact(pre_act):
    return jax.nn.gelu(pre_act, approximate=False)


def hidden_rows(values):
    return lax.all_gather(values, "mp", axis=0, tiled=True)


def hidden_sums(values):
    return lax.psum_scatter(values, "mp", scatter_dimension=0, tiled=True)


def layer_empty(tokens, self_weights, cross_weights, ffn_weights):
    model_width = self_weights[0].shape[0]
    blank_rows = jnp.zeros((tokens, model_width), jnp.bfloat16)
    unit_rows = jnp.zeros((tokens, model_width), jnp.float32)
    scaled = jnp.zeros((tokens, 1), jnp.float32)
    hidden_units = ffn_weights[0].shape[1]
    gathered_count = tokens * (FF // hidden_units)
    unused_self, self_kept = attend_empty(blank_rows, blank_rows, self_weights)
    unused_cross, cross_kept = attend_empty(blank_rows, blank_rows, cross_weights)
    return (
        unit_rows,
        scaled,
        self_kept,
        unit_rows,
        scaled,
        cross_kept,
        unit_rows,
        scaled,
        jnp.zeros((gathered_count, model_width), jnp.bfloat16),
        jnp.zeros((gathered_count, hidden_units), jnp.float32),
        jnp.zeros((gathered_count, hidden_units), jnp.bfloat16),
        unit_rows,
        scaled,
    )


def layer_forward(
    rows_in,
    gain_rows,
    self_weights,
    cross_weights,
    ffn_weights,
    routes_own,
    routes_other,
    own_lengths,
    memory,
    memory_lengths,
    is_decoder,
):
    w_in, w_out = ffn_weights
    decoder_flag = is_decoder.astype(jnp.float32)
    first, unit_a, scaled_a = normalize(rows_in, gain_rows[0])
    first_rows = first.astype(jnp.bfloat16)
    self_out, self_kept = attend(
        first_rows, first_rows, self_weights, routes_own, own_lengths, own_lengths, is_decoder
    )
    after_self = rows_in + self_out
    second, unit_b, scaled_b = normalize(after_self, gain_rows[1])
    second_rows = second.astype(jnp.bfloat16)
    cross_out, cross_kept = attend(
        second_rows,
        memory,
        cross_weights,
        routes_other,
        own_lengths,
        memory_lengths,
        jnp.asarray(False),
    )
    after_cross = after_self + cross_out * decoder_flag
    third, unit_c, scaled_c = normalize(after_cross, gain_rows[2])
    third_rows = third.astype(jnp.bfloat16)
    gathered = hidden_rows(third_rows)
    hidden_pre = jnp.dot(gathered, w_in, preferred_element_type=jnp.float32)
    hidden = gelu_exact(hidden_pre).astype(jnp.bfloat16)
    partial_out = jnp.dot(hidden, w_out, preferred_element_type=jnp.float32)
    ffn_result = hidden_sums(partial_out)
    after_ffn = after_cross + ffn_result
    final, unit_d, scaled_d = normalize(after_ffn, gain_rows[1])
    result = jnp.where(is_decoder, after_ffn, final)
    residuals = (
        unit_a,
        scaled_a,
        self_kept,
        unit_b,
        scaled_b,
        cross_kept,
        unit_c,
        scaled_c,
        gathered,
        hidden_pre,
        hidden,
        unit_d,
        scaled_d,
    )
    return (result, residuals)


def layer_backward(
    upstream,
    residuals,
    gain_rows,
    self_weights,
    cross_weights,
    ffn_weights,
    own_lengths,
    memory_lengths,
    is_decoder,
):
    w_in, w_out = ffn_weights
    decoder_flag = is_decoder.astype(jnp.float32)
    (
        unit_a,
        scaled_a,
        self_kept,
        unit_b,
        scaled_b,
        cross_kept,
        unit_c,
        scaled_c,
        gathered,
        hidden_pre,
        hidden,
        unit_d,
        scaled_d,
    ) = residuals
    back_final, gain_final = normalize_back(upstream, unit_d, scaled_d, gain_rows[1])
    grad_after_ffn = jnp.where(is_decoder, upstream, back_final)
    gain_final = jnp.where(is_decoder, 0.0, gain_final)
    grad_out_rows = grad_after_ffn.astype(jnp.bfloat16)
    grad_gathered = hidden_rows(grad_out_rows)
    grad_w_out = lax.dot_general(
        hidden, grad_gathered, (((0,), (0,)), ((), ())), preferred_element_type=jnp.float32
    )
    grad_hidden = lax.dot_general(
        grad_gathered, w_out, (((1,), (1,)), ((), ())), preferred_element_type=jnp.float32
    )
    unused_value, gelu_pullback = jax.vjp(gelu_exact, hidden_pre)
    grad_pre = gelu_pullback(grad_hidden)[0].astype(jnp.bfloat16)
    grad_w_in = lax.dot_general(
        gathered, grad_pre, (((0,), (0,)), ((), ())), preferred_element_type=jnp.float32
    )
    partial_third = lax.dot_general(
        grad_pre, w_in, (((1,), (1,)), ((), ())), preferred_element_type=jnp.float32
    )
    grad_third = hidden_sums(partial_third)
    back_c, gain_c = normalize_back(grad_third, unit_c, scaled_c, gain_rows[2])
    grad_after_cross = grad_after_ffn + back_c
    cross_query, cross_key, cross_grads = attend_back(
        grad_after_cross * decoder_flag,
        cross_kept,
        cross_weights,
        own_lengths,
        memory_lengths,
        jnp.asarray(False),
    )
    back_b, gain_b = normalize_back(cross_query, unit_b, scaled_b, gain_rows[1])
    grad_after_self = grad_after_cross + back_b
    self_query, self_key, self_grads = attend_back(
        grad_after_self, self_kept, self_weights, own_lengths, own_lengths, is_decoder
    )
    back_a, gain_a = normalize_back(self_query + self_key, unit_a, scaled_a, gain_rows[0])
    grad_rows_in = grad_after_self + back_a
    grad_gains = jnp.stack([gain_a, gain_b + gain_final, gain_c])
    local_grads = (
        grad_gains,
        self_grads[0],
        self_grads[1],
        self_grads[2],
        self_grads[3],
        grad_w_in,
        grad_w_out,
        cross_grads[0],
        cross_grads[1],
        cross_grads[2],
        cross_grads[3],
    )
    return (grad_rows_in, cross_key, local_grads)


def reduce_grads(local_grads, decoder_share):
    (
        gains_g,
        router_g,
        query_g,
        keyval_g,
        output_g,
        inner_g,
        outer_g,
        router_c,
        query_c,
        keyval_c,
        output_c,
    ) = local_grads
    gains_g, router_g, keyval_g, router_c, keyval_c = lax.psum(
        (gains_g, router_g, keyval_g, router_c, keyval_c), "mp"
    )

    def placed(value):
        return jnp.stack([value * (1.0 - decoder_share), value * decoder_share])

    return (
        lax.psum_scatter(placed(gains_g), ("section", "dp"), scatter_dimension=2, tiled=True),
        lax.psum_scatter(placed(router_g), ("section", "dp"), scatter_dimension=1, tiled=True),
        lax.psum_scatter(placed(query_g), ("section", "dp"), scatter_dimension=2, tiled=True),
        lax.psum_scatter(placed(keyval_g), ("section", "dp"), scatter_dimension=1, tiled=True),
        lax.psum_scatter(placed(output_g), ("section", "dp"), scatter_dimension=3, tiled=True),
        lax.psum_scatter(placed(inner_g), ("section", "dp"), scatter_dimension=1, tiled=True),
        lax.psum_scatter(placed(outer_g), ("section", "dp"), scatter_dimension=2, tiled=True),
        lax.psum_scatter(router_c, ("section", "dp"), scatter_dimension=0, tiled=True),
        lax.psum_scatter(query_c, ("section", "dp"), scatter_dimension=1, tiled=True),
        lax.psum_scatter(keyval_c, ("section", "dp"), scatter_dimension=0, tiled=True),
        lax.psum_scatter(output_c, ("section", "dp"), scatter_dimension=2, tiled=True),
    )


def shard_zeros(local_grads, shard_parts):
    shaped = []
    for position, value in enumerate(local_grads):
        dims_list = list(value.shape)
        if position < 7:
            dims_list = [2] + dims_list
        dims_list[SHARD_DIMS[position]] = dims_list[SHARD_DIMS[position]] // shard_parts
        shaped.append(jnp.zeros(tuple(dims_list), jnp.float32))
    return tuple(shaped)


def per_device(
    inputs,
    lengths,
    routes_self,
    routes_cross,
    gains,
    router_self,
    query_self,
    keyval_self,
    output_self,
    ffn_in,
    ffn_out,
    router_cross,
    query_cross,
    keyval_cross,
    output_cross,
    cotangent,
):
    section_index = lax.axis_index("section")
    is_decoder = section_index == 1
    decoder_share = is_decoder.astype(jnp.float32)
    own_rows = inputs[0, :, 0]
    micro_count = own_rows.shape[0]
    own_lengths = lengths[0, :, 0]
    own_routes = routes_self[0, :, 0]
    other_routes = routes_cross[:, 0]
    upstream_all = cotangent[:, 0]
    gain_rows = gains[0].astype(jnp.float32)
    zero_args = tuple(
        (
            jnp.zeros(value.shape, jnp.float32)
            for value in (
                gain_rows,
                router_self[0],
                query_self[0],
                keyval_self[0],
                output_self[0],
                ffn_in[0],
                ffn_out[0],
                router_cross,
                query_cross,
                keyval_cross,
                output_cross,
            )
        )
    )
    self_weights = (router_self[0], query_self[0], keyval_self[0], output_self[0])
    cross_weights = (router_cross, query_cross, keyval_cross, output_cross)
    ffn_weights = (ffn_in[0], ffn_out[0])
    shard_parts = lax.axis_size("section") * lax.axis_size("dp")
    start_totals = shard_zeros(zero_args, shard_parts)
    blank_kept = layer_empty(own_rows.shape[1], self_weights, cross_weights, ffn_weights)
    start_state = (
        jnp.zeros(own_rows.shape[1:], jnp.bfloat16),
        jnp.zeros(own_lengths.shape[1:], jnp.int32),
        jnp.zeros(own_rows.shape[1:], jnp.bfloat16),
        blank_kept,
        blank_kept,
        jnp.zeros(own_rows.shape, jnp.bfloat16),
        jnp.zeros(own_rows.shape, jnp.float32),
        start_totals,
    )

    def pick_kept(fresh, older):
        return jnp.where(is_decoder, fresh, older)

    def step(state_carry, moment):
        (
            memory,
            memory_lengths,
            memory_grad,
            kept_recent,
            kept_older,
            outputs,
            input_grads,
            totals,
        ) = state_carry
        ahead_at = moment - section_index
        behind = moment - 2 + section_index
        ahead_ok = (ahead_at >= 0) & (ahead_at < micro_count)
        behind_ok = (behind >= 0) & (behind < micro_count)
        ahead_idx = jnp.clip(ahead_at, 0, micro_count - 1)
        behind_idx = jnp.clip(behind, 0, micro_count - 1)
        result, kept_now = layer_forward(
            own_rows[ahead_idx].astype(jnp.float32),
            gain_rows,
            self_weights,
            cross_weights,
            ffn_weights,
            own_routes[ahead_idx],
            other_routes[ahead_idx],
            own_lengths[ahead_idx],
            memory,
            memory_lengths,
            is_decoder,
        )
        result_rows = result.astype(jnp.bfloat16)
        earlier = lax.dynamic_index_in_dim(outputs, ahead_idx, 0, False)
        outputs = lax.dynamic_update_index_in_dim(
            outputs, jnp.where(ahead_ok, result_rows, earlier), ahead_idx, 0
        )
        sent_memory, sent_lengths = passed_along(
            (result_rows, own_lengths[ahead_idx]), "section", 1
        )
        residuals = jax.tree.map(pick_kept, kept_now, kept_older)
        start_grad = jnp.where(
            is_decoder,
            upstream_all[behind_idx].astype(jnp.float32),
            memory_grad.astype(jnp.float32),
        ) * behind_ok.astype(jnp.float32)
        grad_rows_in, grad_memory, local_grads = layer_backward(
            start_grad,
            residuals,
            gain_rows,
            self_weights,
            cross_weights,
            ffn_weights,
            own_lengths[behind_idx],
            memory_lengths,
            is_decoder,
        )
        earlier_grad = lax.dynamic_index_in_dim(input_grads, behind_idx, 0, False)
        input_grads = lax.dynamic_update_index_in_dim(
            input_grads, jnp.where(behind_ok, grad_rows_in, earlier_grad), behind_idx, 0
        )
        returned = passed_along(grad_memory.astype(jnp.bfloat16), "section", -1)
        totals = jax.tree.map(jnp.add, totals, reduce_grads(local_grads, decoder_share))
        return (
            (
                sent_memory,
                sent_lengths,
                returned,
                kept_now,
                kept_recent,
                outputs,
                input_grads,
                totals,
            ),
            None,
        )

    final_state, unused_steps = lax.scan(
        step, start_state, jnp.arange(micro_count + 2, dtype=jnp.int32)
    )
    outputs, input_grads, totals = (final_state[5], final_state[6], final_state[7])
    return (
        outputs[None, :, None],
        input_grads[None, :, None],
        totals[0],
        totals[1],
        totals[2],
        totals[3],
        totals[4],
        totals[5],
        totals[6],
        totals[7],
        totals[8],
        totals[9],
        totals[10],
    )


def solution(mesh):
    placed = (
        P("section", None, "dp", "mp", None),
        P("section", None, "dp", None),
        P("section", None, "dp", "mp", None),
        P(None, "dp", "mp", None),
        P("section", None, None),
        P("section", None, None),
        P("section", "mp", None, None),
        P("section", None, None),
        P("section", "mp", None, None),
        P("section", None, "mp"),
        P("section", "mp", None),
        P(),
        P("mp", None, None),
        P(),
        P("mp", None, None),
        P(None, "dp", "mp", None),
    )
    return jax.shard_map(
        per_device,
        mesh=mesh,
        in_specs=placed,
        out_specs=(
            P("section", None, "dp", "mp", None),
            P("section", None, "dp", "mp", None),
            P(None, None, ("section", "dp")),
            P(None, ("section", "dp"), None),
            P(None, "mp", ("section", "dp"), None),
            P(None, ("section", "dp"), None),
            P(None, "mp", None, ("section", "dp")),
            P(None, ("section", "dp"), "mp"),
            P(None, "mp", ("section", "dp")),
            P(("section", "dp"), None),
            P("mp", ("section", "dp"), None),
            P(("section", "dp"), None),
            P("mp", None, ("section", "dp")),
        ),
        check_vma=False,
    )
```

profile of v0, /device:TPU:0, one launch (start us, length us, event | category | flops | bytes accessed | tf_op | source)
XLA Modules:
  0.0 5446.9 jit_solution(12459549587152632320)
XLA Ops:
  56.8 5378.8 %while.208 = (s32[]{:T(128)}, bf16[256,512]{1,0:T(8,128)(2,1)S(1)}, s32[8]{0:T(128)}, bf16[256,512]{1,0:T(8,128)(2,1)}, f32[256,512]{1,0:T(8,128)S(1)}, /*index=...) while((s32[]{:T(128)}, bf16[256,512]{1,0:T(8,128)(2,1)S(1)}, ...), condition=%wide.region_81.82_spmd.clone, body=%wide.region_0.81_spmd.clone.sunk | while | flops 6324016128 | bytes 601041856 | solution.py:667
  323.9 33.6 reduce-scatter.39.cloned.1.call-done
  620.1 32.5 reduce-scatter.63.cloned.1.call-done
  919.8 32.4 reduce-scatter.57.cloned.1.call-done
  1219.9 33.6 reduce-scatter.39.cloned.1.call-done
  1516.2 32.1 reduce-scatter.63.cloned.1.call-done
  1783.6 31.6 reduce-scatter.53.cloned.1.call-done
  1816.1 32.3 reduce-scatter.57.cloned.1.call-done
  2116.1 33.6 reduce-scatter.39.cloned.1.call-done
  2412.3 32.3 reduce-scatter.63.cloned.1.call-done
  2614.3 31.5 reduce-scatter.55.cloned.1.call-done
  2711.8 32.5 reduce-scatter.57.cloned.1.call-done
  3012.1 33.6 reduce-scatter.39.cloned.1.call-done
  3308.3 32.2 reduce-scatter.63.cloned.1.call-done
  3510.6 31.6 reduce-scatter.55.cloned.1.call-done
  3575.6 31.6 reduce-scatter.53.cloned.1.call-done
  3608.1 32.4 reduce-scatter.57.cloned.1.call-done
  3908.2 33.6 reduce-scatter.39.cloned.1.call-done
  4204.6 32.4 reduce-scatter.63.cloned.1.call-done
  4471.9 31.6 reduce-scatter.53.cloned.1.call-done
  4504.4 32.5 reduce-scatter.57.cloned.1.call-done
  4804.6 33.6 reduce-scatter.39.cloned.1.call-done
  5100.7 32.2 reduce-scatter.63.cloned.1.call-done
  5400.4 32.5 reduce-scatter.57.cloned.1.call-done
  (4772 shorter events, 4654.9 us)
Async XLA Ops:
  400.1 197.4 %all-reduce.11.cloned.1.call-start = ((), (), s32[]{:S(2)}) async-start(), calls=%async_computation.43 | async-start | bytes 4194304 | tf_op jit(solution)/shard_map/while
  420.7 186.6 %reduce-scatter.61.cloned.1.call-start = ((), (), s32[]{:S(2)}) async-start(), calls=%async_computation.42 | async-start | bytes 2359296 | tf_op jit(solution)/shard_map/while/body/eval_jaxpr/reduce_scatter | solution.py:506
  541.9 203.0 %reduce-scatter.59.cloned.1.call-start = ((), (), s32[]{:S(2)}) async-start(), calls=%async_computation.41 | async-start | bytes 589824 | tf_op jit(solution)/shard_map/while
  685.2 268.5 %collective-permute-start.2 = (bf16[256,512]{1,0:T(8,128)(2,1)}, bf16[256,512]{1,0:T(8,128)(2,1)}, u32[]{:S(2)}, u32[]{:S(2)}) collective-permute-start(bf16[256,512]{1,0:T(8,128)(2,1)} %convolution_convert_fusion.24), channel_id=1, source_target_pairs={{16,0},{17,1},{18,2},{19,3},{20,4},{21,5},{22,6},{23,7},{24,8},{25... | collective-permute-start | bytes 786440 | tf_op jit(solution)/shard_map/while/body/eval_jaxpr/ppermute | solution.py:17
  1296.1 197.6 %all-reduce.11.cloned.1.call-start = ((), (), s32[]{:S(2)}) async-start(), calls=%async_computation.43 | async-start | bytes 4194304 | tf_op jit(solution)/shard_map/while
  1318.0 185.4 %reduce-scatter.61.cloned.1.call-start = ((), (), s32[]{:S(2)}) async-start(), calls=%async_computation.42 | async-start | bytes 2359296 | tf_op jit(solution)/shard_map/while/body/eval_jaxpr/reduce_scatter | solution.py:506
  1438.0 202.8 %reduce-scatter.59.cloned.1.call-start = ((), (), s32[]{:S(2)}) async-start(), calls=%async_computation.41 | async-start | bytes 589824 | tf_op jit(solution)/shard_map/while
  1581.0 268.9 %collective-permute-start.2 = (bf16[256,512]{1,0:T(8,128)(2,1)}, bf16[256,512]{1,0:T(8,128)(2,1)}, u32[]{:S(2)}, u32[]{:S(2)}) collective-permute-start(bf16[256,512]{1,0:T(8,128)(2,1)} %convolution_convert_fusion.24), channel_id=1, source_target_pairs={{16,0},{17,1},{18,2},{19,3},{20,4},{21,5},{22,6},{23,7},{24,8},{25... | collective-permute-start | bytes 786440 | tf_op jit(solution)/shard_map/while/body/eval_jaxpr/ppermute | solution.py:17
  2192.3 197.3 %all-reduce.11.cloned.1.call-start = ((), (), s32[]{:S(2)}) async-start(), calls=%async_computation.43 | async-start | bytes 4194304 | tf_op jit(solution)/shard_map/while
  2214.2 185.1 %reduce-scatter.61.cloned.1.call-start = ((), (), s32[]{:S(2)}) async-start(), calls=%async_computation.42 | async-start | bytes 2359296 | tf_op jit(solution)/shard_map/while/body/eval_jaxpr/reduce_scatter | solution.py:506
  2334.0 203.0 %reduce-scatter.59.cloned.1.call-start = ((), (), s32[]{:S(2)}) async-start(), calls=%async_computation.41 | async-start | bytes 589824 | tf_op jit(solution)/shard_map/while
  2477.2 268.6 %collective-permute-start.2 = (bf16[256,512]{1,0:T(8,128)(2,1)}, bf16[256,512]{1,0:T(8,128)(2,1)}, u32[]{:S(2)}, u32[]{:S(2)}) collective-permute-start(bf16[256,512]{1,0:T(8,128)(2,1)} %convolution_convert_fusion.24), channel_id=1, source_target_pairs={{16,0},{17,1},{18,2},{19,3},{20,4},{21,5},{22,6},{23,7},{24,8},{25... | collective-permute-start | bytes 786440 | tf_op jit(solution)/shard_map/while/body/eval_jaxpr/ppermute | solution.py:17
  3088.3 197.4 %all-reduce.11.cloned.1.call-start = ((), (), s32[]{:S(2)}) async-start(), calls=%async_computation.43 | async-start | bytes 4194304 | tf_op jit(solution)/shard_map/while
  3110.3 185.1 %reduce-scatter.61.cloned.1.call-start = ((), (), s32[]{:S(2)}) async-start(), calls=%async_computation.42 | async-start | bytes 2359296 | tf_op jit(solution)/shard_map/while/body/eval_jaxpr/reduce_scatter | solution.py:506
  3230.0 202.9 %reduce-scatter.59.cloned.1.call-start = ((), (), s32[]{:S(2)}) async-start(), calls=%async_computation.41 | async-start | bytes 589824 | tf_op jit(solution)/shard_map/while
  3373.2 268.8 %collective-permute-start.2 = (bf16[256,512]{1,0:T(8,128)(2,1)}, bf16[256,512]{1,0:T(8,128)(2,1)}, u32[]{:S(2)}, u32[]{:S(2)}) collective-permute-start(bf16[256,512]{1,0:T(8,128)(2,1)} %convolution_convert_fusion.24), channel_id=1, source_target_pairs={{16,0},{17,1},{18,2},{19,3},{20,4},{21,5},{22,6},{23,7},{24,8},{25... | collective-permute-start | bytes 786440 | tf_op jit(solution)/shard_map/while/body/eval_jaxpr/ppermute | solution.py:17
  3984.5 197.5 %all-reduce.11.cloned.1.call-start = ((), (), s32[]{:S(2)}) async-start(), calls=%async_computation.43 | async-start | bytes 4194304 | tf_op jit(solution)/shard_map/while
  4006.4 185.3 %reduce-scatter.61.cloned.1.call-start = ((), (), s32[]{:S(2)}) async-start(), calls=%async_computation.42 | async-start | bytes 2359296 | tf_op jit(solution)/shard_map/while/body/eval_jaxpr/reduce_scatter | solution.py:506
  4126.4 203.1 %reduce-scatter.59.cloned.1.call-start = ((), (), s32[]{:S(2)}) async-start(), calls=%async_computation.41 | async-start | bytes 589824 | tf_op jit(solution)/shard_map/while
  4269.7 268.8 %collective-permute-start.2 = (bf16[256,512]{1,0:T(8,128)(2,1)}, bf16[256,512]{1,0:T(8,128)(2,1)}, u32[]{:S(2)}, u32[]{:S(2)}) collective-permute-start(bf16[256,512]{1,0:T(8,128)(2,1)} %convolution_convert_fusion.24), channel_id=1, source_target_pairs={{16,0},{17,1},{18,2},{19,3},{20,4},{21,5},{22,6},{23,7},{24,8},{25... | collective-permute-start | bytes 786440 | tf_op jit(solution)/shard_map/while/body/eval_jaxpr/ppermute | solution.py:17
  4880.8 197.4 %all-reduce.11.cloned.1.call-start = ((), (), s32[]{:S(2)}) async-start(), calls=%async_computation.43 | async-start | bytes 4194304 | tf_op jit(solution)/shard_map/while
  4902.8 185.2 %reduce-scatter.61.cloned.1.call-start = ((), (), s32[]{:S(2)}) async-start(), calls=%async_computation.42 | async-start | bytes 2359296 | tf_op jit(solution)/shard_map/while/body/eval_jaxpr/reduce_scatter | solution.py:506
  5022.6 203.0 %reduce-scatter.59.cloned.1.call-start = ((), (), s32[]{:S(2)}) async-start(), calls=%async_computation.41 | async-start | bytes 589824 | tf_op jit(solution)/shard_map/while
  5165.6 268.7 %collective-permute-start.2 = (bf16[256,512]{1,0:T(8,128)(2,1)}, bf16[256,512]{1,0:T(8,128)(2,1)}, u32[]{:S(2)}, u32[]{:S(2)}) collective-permute-start(bf16[256,512]{1,0:T(8,128)(2,1)} %convolution_convert_fusion.24), channel_id=1, source_target_pairs={{16,0},{17,1},{18,2},{19,3},{20,4},{21,5},{22,6},{23,7},{24,8},{25... | collective-permute-start | bytes 786440 | tf_op jit(solution)/shard_map/while/body/eval_jaxpr/ppermute | solution.py:17
  (1218 other events, 30534.0 us)
Sparse Core Ops, SparseCore 0:
  322.3 35.1 reduce-scatter.38
  437.7 65.1 all-reduce.10
  505.0 48.6 reduce-scatter.60
  777.2 42.1 all-reduce.8
  1218.3 35.1 reduce-scatter.38
  1333.8 65.1 all-reduce.10
  1401.1 48.6 reduce-scatter.60
  1673.2 42.0 all-reduce.8
  2114.5 35.1 reduce-scatter.38
  2230.0 65.0 all-reduce.10
  2297.5 48.5 reduce-scatter.60
  2569.1 42.0 all-reduce.8
  3010.5 35.1 reduce-scatter.38
  3125.9 65.0 all-reduce.10
  3193.3 48.5 reduce-scatter.60
  3465.4 41.9 all-reduce.8
  3906.6 35.1 reduce-scatter.38
  4022.2 65.0 all-reduce.10
  4089.6 48.5 reduce-scatter.60
  4361.7 42.0 all-reduce.8
  4803.0 35.1 reduce-scatter.38
  4918.5 65.0 all-reduce.10
  4986.0 48.5 reduce-scatter.60
  5257.7 42.0 all-reduce.8
  (84 shorter events, 2494.0 us)
where the time goes:
time: 5480 us; the launch traced here: 5450 us
  waiting for transfers between devices  2400 us (44%)
  local copies, waits for them, and re-layouts  1280 us (23%)
  other arithmetic  654 us (12%)
  matrix products  497 us (9%)
  starting transfers between devices  365 us (7%)
  blocking collectives  215 us (4%)
    while x2580, local copies, waits for them, and re-layouts  588 us
    while x150, waiting for transfers between devices  537 us
    all_gather x12, waiting for transfers between devices, hidden_rows(): return lax.all_gather(values, 'mp', axis=0, tiled=True)  312 us
    reduce_scatter x12, waiting for transfers between devices, hidden_sums(): return lax.psum_scatter(values, 'mp', scatter_dimension=0, tiled=True)  248 us
    reduce_scatter x12, waiting for transfers between devices, attend_back(): lax.psum_scatter(jnp.concatenate([grad_keys, grad_values], 1), 'mp', scat...  220 us
    reduce_scatter x6, waiting for transfers between devices, reduce_grads(): lax.psum_scatter(placed(keyval_g), ('section', 'dp'), scatter_dimension=1...  195 us
    reduce_scatter x6, waiting for transfers between devices, reduce_grads(): lax.psum_scatter(query_c, ('section', 'dp'), scatter_dimension=1, tiled=T...  194 us
    reduce_scatter x6, waiting for transfers between devices, reduce_grads(): lax.psum_scatter(keyval_c, ('section', 'dp'), scatter_dimension=0, tiled=...  154 us

commit v1 on v0

v1 whole, which is shorter than its diff:
```python
import functools

import jax
import jax.numpy as jnp
from jax import lax
from jax.experimental import pallas as pl
from jax.experimental.pallas import tpu as pltpu
from jax.sharding import PartitionSpec as P

EPS = 1e-05
MASK_VALUE = -1000000000.0
BF = jnp.bfloat16
F32 = jnp.float32
EX_AT = 160
CODE_ROW = 3
LEN_ROW = 4
ROUTER_AT = 8
GAIN_LANE = 64
ROUTER_LANES = (8, 24, 40)
VMEM_LIMIT = 56 * 1024 * 1024


def nn(left, right):
    return lax.dot_general(left, right, (((1,), (0,)), ((), ())), preferred_element_type=F32)


def nt(left, right):
    return lax.dot_general(left, right, (((1,), (1,)), ((), ())), preferred_element_type=F32)


def tn(left, right):
    return lax.dot_general(left, right, (((0,), (0,)), ((), ())), preferred_element_type=F32)


def norm_of(values, gain_row):
    center = values - jnp.mean(values, 1, keepdims=True)
    scaled = lax.rsqrt(jnp.mean(center * center, 1, keepdims=True) + EPS)
    unit_rows = center * scaled
    return unit_rows * gain_row, unit_rows, scaled


def norm_back(upstream, unit_rows, scaled, gain_row):
    inner = upstream * gain_row
    result = scaled * (
        inner
        - jnp.mean(inner, 1, keepdims=True)
        - unit_rows * jnp.mean(inner * unit_rows, 1, keepdims=True)
    )
    return result, jnp.sum(upstream * unit_rows, 0, keepdims=True)


def eye_of(size):
    return lax.broadcasted_iota(jnp.int32, (size, size), 0) == lax.broadcasted_iota(
        jnp.int32, (size, size), 1
    )


def row_to_col(row):
    return jnp.sum(jnp.where(eye_of(row.shape[1]), row, 0.0), 1, keepdims=True)


def col_to_row(col):
    return jnp.sum(jnp.where(eye_of(col.shape[0]), col, 0.0), 0, keepdims=True)


def ends_of(extra):
    lengths = extra[LEN_ROW : LEN_ROW + 1, 0:8] * 32.0 + extra[LEN_ROW : LEN_ROW + 1, 128:136]
    ends = [lengths[:, 0:1]]
    for k in range(1, 8):
        ends.append(ends[-1] + lengths[:, k : k + 1])
    return ends


def segments(places, ends):
    total = jnp.where(places >= ends[0], 1.0, 0.0)
    for end in ends[1:]:
        total = total + jnp.where(places >= end, 1.0, 0.0)
    return total


def extra_of(recv_ref, layer, quarter):
    return recv_ref[4 * layer + quarter, EX_AT : EX_AT + 16, :]


def gain_of(recv_ref, layer, which):
    return extra_of(recv_ref, layer, 0).astype(F32)[which : which + 1, :]


def rows_of(recv_ref, layer, quarter):
    return recv_ref[4 * layer + quarter, 0:128, :].astype(F32)


def other_kv(recv_ref, layer, quarter):
    packed = recv_ref[4 * layer + quarter, 128:160, :]
    return jnp.concatenate([packed[:, 128 * c : 128 * c + 128] for c in range(4)], 0)


def routing(query_rows, router_block, code_row):
    code = row_to_col(code_row)
    second = jnp.floor(code * 0.125)
    first = code - 8.0 * second
    e0, e1 = first.astype(jnp.int32), second.astype(jnp.int32)
    logits = nt(query_rows, router_block)
    lanes = lax.broadcasted_iota(jnp.int32, logits.shape, 1)
    l0 = jnp.sum(jnp.where(lanes == e0 + ROUTER_AT, logits, 0.0), 1, keepdims=True)
    l1 = jnp.sum(jnp.where(lanes == e1 + ROUTER_AT, logits, 0.0), 1, keepdims=True)
    top = jnp.maximum(l0, l1)
    x0, x1 = jnp.exp(l0 - top), jnp.exp(l1 - top)
    total = x0 + x1
    owners = lax.broadcasted_iota(jnp.int32, (code.shape[0], 512), 1) >> 6
    return e0, e1, x0 / total, x1 / total, owners == e0, owners == e1


def fold(wide, mask):
    kept = jnp.where(mask, wide, 0.0)
    return kept[:, 0:128] + kept[:, 128:256] + kept[:, 256:384] + kept[:, 384:512]


def spread(a0, a1, m0, m1):
    parts = []
    for c in range(4):
        cut = slice(128 * c, 128 * c + 128)
        parts.append(jnp.where(m0[:, cut], a0, jnp.where(m1[:, cut], a1, 0.0)))
    return jnp.concatenate(parts, 1).astype(BF)


def rounded(value):
    return value.astype(BF).astype(F32)


def start_pick(cond, yes, no, sem):
    src_yes, dst = yes
    src_no, unused_dst = no

    @pl.when(cond)
    def _():
        pltpu.make_async_copy(src_yes, dst, sem).start()

    @pl.when(jnp.logical_not(cond))
    def _():
        pltpu.make_async_copy(src_no, dst, sem).start()


def load_columns(cond, own, oth, lane, dst, sems, base):
    for m in range(4):
        cut = (m, slice(None), pl.ds(lane, 128))
        to = dst.at[:, pl.ds(128 * m, 128)]
        start_pick(cond, (own.at[cut], to), (oth.at[cut], to), sems.at[base + m])


def wait_columns(own, lane, dst, sems, base):
    for m in range(4):
        pltpu.make_async_copy(
            own.at[m, :, pl.ds(lane, 128)], dst.at[:, pl.ds(128 * m, 128)], sems.at[base + m]
        ).wait()


def load_whole(cond, own, oth, dst, sem):
    start_pick(cond, (own, dst), (oth, dst), sem)


def wait_whole(own, dst, sem):
    pltpu.make_async_copy(own, dst, sem).wait()


def widen_kv(kv_ref, k2_ref, v2_ref):
    for j in range(4):
        kv = kv_ref[j].reshape(256, 128).astype(F32)
        turned = pltpu.roll(kv, 64, 1)
        low = lax.broadcasted_iota(jnp.int32, kv.shape, 1) < 64
        k2_ref[256 * j : 256 * j + 256, :] = jnp.where(low, kv, turned).astype(BF)
        v2_ref[256 * j : 256 * j + 256, :] = jnp.where(low, turned, kv).astype(BF)


def attend_tile(query_rows, route, w_q, w_ot, k2, v2, allowed):
    e0, e1, g0, g1, m0, m1 = route
    q_all = nn(query_rows, w_q) * 0.125
    queries = jnp.concatenate([fold(q_all, m0), fold(q_all, m1)], 0).astype(BF)
    scores = nt(queries, k2)
    scores = jnp.concatenate(
        [
            jnp.where(allowed, scores[0:128], MASK_VALUE),
            jnp.where(allowed, scores[128:256], MASK_VALUE),
        ],
        0,
    )
    top = jnp.max(scores, 1, keepdims=True)
    weights = jnp.exp(scores - top)
    total = jnp.sum(weights, 1, keepdims=True)
    mixed = nn(weights.astype(BF), v2) / total
    log_total = top + jnp.log(total)
    gated = spread(rounded(g0) * mixed[0:128], rounded(g1) * mixed[128:256], m0, m1)
    out = nt(gated, w_ot)
    rows = jnp.concatenate([col_to_row(log_total[0:128]), col_to_row(log_total[128:256])], 0)
    return out, mixed, rows


def attend_back_tile(
    j, upstream, query_rows, route, mixed, log_rows, w_q, w_ot, router_block, router_lane, k2, v2,
    allowed_t, grad_k, grad_v, gated_ref, dz_ref, dq_ref, dlog_ref,
):
    e0, e1, g0, g1, m0, m1 = route
    q_all = nn(query_rows, w_q) * 0.125
    queries = jnp.concatenate([fold(q_all, m0), fold(q_all, m1)], 0).astype(BF)
    dz = upstream.astype(BF)
    dg_all = nn(dz, w_ot)
    dgated0, dgated1 = fold(dg_all, m0), fold(dg_all, m1)
    r0, r1 = rounded(g0), rounded(g1)
    mixed0, mixed1 = mixed[0:128], mixed[128:256]
    gated_ref[j] = spread(r0 * mixed0, r1 * mixed1, m0, m1)
    dz_ref[j] = dz
    dgate0 = rounded(jnp.sum(mixed0 * dgated0, 1, keepdims=True))
    dgate1 = rounded(jnp.sum(mixed1 * dgated1, 1, keepdims=True))
    do0, do1 = (r0 * dgated0).astype(BF), (r1 * dgated1).astype(BF)
    grad_mixed = jnp.concatenate([do0, do1], 0)
    inner_row = jnp.concatenate(
        [
            col_to_row(jnp.sum(do0.astype(F32) * mixed0, 1, keepdims=True)),
            col_to_row(jnp.sum(do1.astype(F32) * mixed1, 1, keepdims=True)),
        ],
        1,
    )
    log_row = jnp.concatenate([log_rows[0:1], log_rows[1:2]], 1)
    scores = nt(k2, queries)
    scores = jnp.concatenate(
        [
            jnp.where(allowed_t, scores[:, 0:128], MASK_VALUE),
            jnp.where(allowed_t, scores[:, 128:256], MASK_VALUE),
        ],
        1,
    )
    probs = jnp.exp(scores - log_row)
    grad_probs = nt(v2, grad_mixed)
    grad_scores = (probs * (grad_probs - inner_row)).astype(BF)
    grad_v[...] += nn(probs.astype(BF), grad_mixed)
    grad_k[...] += nn(grad_scores, queries)
    grad_q = rounded(tn(grad_scores, k2) * 0.125)
    dq_all = spread(grad_q[0:128], grad_q[128:256], m0, m1)
    dq_ref[j] = dq_all
    grad_rows = nt(dq_all, w_q)
    mean_grad = g0 * dgate0 + g1 * dgate1
    dc0, dc1 = g0 * (dgate0 - mean_grad), g1 * (dgate1 - mean_grad)
    lanes = lax.broadcasted_iota(jnp.int32, (128, 16), 1)
    dlog = jnp.where(lanes == e0 + ROUTER_AT, dc0, 0.0) + jnp.where(
        lanes == e1 + ROUTER_AT, dc1, 0.0
    )
    wide = lax.broadcasted_iota(jnp.int32, (128, 128), 1)
    dlog_ref[j] = (
        jnp.where(wide == e0 + router_lane, dc0, 0.0)
        + jnp.where(wide == e1 + router_lane, dc1, 0.0)
    ).astype(BF)
    return grad_rows + nn(dlog.astype(BF), router_block)


def allowed_rows(j, sec, ends_q, ends_k, causal):
    places = (256 * j + 128 * sec).astype(F32)
    query_at = places + lax.broadcasted_iota(jnp.int32, (128, 1), 0).astype(F32)
    key_at = lax.broadcasted_iota(jnp.int32, (1, 1024), 1).astype(F32)
    allowed = segments(query_at, ends_q) == segments(key_at, ends_k)
    if causal:
        allowed = allowed & (key_at <= query_at)
    return allowed


def key_segments_t(ends_k, segk_ref):
    for j in range(8):
        at = lax.broadcasted_iota(jnp.int32, (128, 128), 0).astype(F32) + 128.0 * j
        segk_ref[128 * j : 128 * j + 128, :] = segments(at, ends_k)


def allowed_cols(j, sec, ends_q, segk_ref, causal):
    places = (256 * j + 128 * sec).astype(F32)
    query_at = places + lax.broadcasted_iota(jnp.int32, (1, 128), 1).astype(F32)
    allowed = segk_ref[...] == segments(query_at, ends_q)
    if causal:
        key_at = lax.broadcasted_iota(jnp.int32, (1024, 128), 0).astype(F32)
        allowed = allowed & (key_at <= query_at)
    return allowed


def fold_kv(grad_k, grad_v, sec, own_ref, send_ref):
    for j in range(4):
        k = grad_k[256 * j : 256 * j + 256, :]
        v = grad_v[256 * j : 256 * j + 256, :]
        k = k + pltpu.roll(k, 64, 1)
        v = v + pltpu.roll(v, 64, 1)
        low = lax.broadcasted_iota(jnp.int32, k.shape, 1) < 64
        both = jnp.where(low, k, v)
        first, second = both[0:128], both[128:256]
        own_ref[j] = jnp.where(sec == 0, first, second)
        send_ref[j] = jnp.where(sec == 0, second, first).astype(send_ref.dtype)


def split_halves(value, sec, keep_ref, send_ref, m, lane):
    upper, lower = value[0:256], value[256:512]
    cut = slice(lane, lane + value.shape[1])
    keep_ref[m, :, cut] = jnp.where(sec == 0, upper, lower).astype(BF)
    send_ref[m, :, cut] = jnp.where(sec == 0, lower, upper).astype(BF)


def turned_rows(value):
    return value.astype(F32).T.astype(BF)


def attention_weight_grads(first_t, gated_ref, dz_ref, dq_ref, sec, keep_ref, send_ref):
    dz_t = turned_rows(dz_ref[...].reshape(512, 512))
    grad_q = nn(first_t, dq_ref[...].reshape(512, 512))
    grad_o = nn(dz_t, gated_ref[...].reshape(512, 512))
    for m in range(4):
        cut = slice(128 * m, 128 * m + 128)
        split_halves(grad_q[:, cut], sec, keep_ref, send_ref, m, 0)
        split_halves(grad_o[:, cut], sec, keep_ref, send_ref, m, 128)


def gelu_parts(pre):
    cdf = 0.5 * (1.0 + lax.erf(pre * 0.7071067811865476))
    slope = cdf + pre * (jnp.exp(-0.5 * pre * pre) * 0.3989422804014327)
    return pre * cdf, slope


def own_self_kv(recv_ref, layer, sec, gain, w_kv, kv_ref):
    for j in range(4):
        first = norm_of(rows_of(recv_ref, layer, j), gain)[0].astype(BF)
        kv_ref[j, sec] = nn(first, w_kv).astype(BF)
        kv_ref[j, 1 - sec] = other_kv(recv_ref, layer, j)


def pack_kernel(x_ref, gain_ref, w_kv_ref, extra_ref, send_ref):
    gain = gain_ref[0:1, :].astype(F32)
    w_kv = w_kv_ref[...]
    for m in range(4):
        first = norm_of(x_ref[m].astype(F32), gain)[0].astype(BF)
        kv = nn(first, w_kv).astype(BF)
        for h in range(2):
            to = 4 * h + m
            send_ref[to, 0:128, :] = x_ref[m, 128 * h : 128 * h + 128, :]
            far = kv[128 * (1 - h) : 128 * (1 - h) + 128]
            send_ref[to, 128:160, :] = jnp.concatenate(
                [far[32 * c : 32 * c + 32] for c in range(4)], 1
            )
            send_ref[to, EX_AT : EX_AT + 16, :] = extra_ref[to]


def enc_fwd_kernel(
    sec_ref, recv_ref, kvc_ref, wa_own, wa_oth, kvw_own, kvw_oth, f_own, f_oth,
    h1_ref, h2_ref, mixed_ref, log_ref, mem_ref, kvm_ref,
    wq, wot, wkv, w_in, w_out, kv_s, k2, v2, third_s, acc, sems,
):
    sec = sec_ref[0]
    mine = sec == 0
    load_whole(mine, kvw_own, kvw_oth, wkv, sems.at[0])
    load_columns(mine, wa_own, wa_oth, 0, wq, sems, 1)
    load_columns(mine, wa_own, wa_oth, 128, wot, sems, 5)
    load_whole(mine, f_own, f_oth, w_in, sems.at[9])
    load_whole(mine, f_oth, f_own, w_out, sems.at[10])
    wait_whole(kvw_own, wkv, sems.at[0])
    own_self_kv(recv_ref, 0, sec, gain_of(recv_ref, 0, 0), wkv[...], kv_s)
    widen_kv(kv_s, k2, v2)
    wait_columns(wa_own, 0, wq, sems, 1)
    wait_columns(wa_own, 128, wot, sems, 5)
    ends = ends_of(extra_of(recv_ref, 0, 0).astype(F32))
    router_block = extra_of(recv_ref, 0, 0)

    def tile(j, carry):
        rows = rows_of(recv_ref, 0, j)
        first = norm_of(rows, gain_of(recv_ref, 0, 0))[0].astype(BF)
        code_row = extra_of(recv_ref, 0, j).astype(F32)[CODE_ROW : CODE_ROW + 1, 0:128]
        route = routing(first, router_block, code_row)
        allowed = allowed_rows(j, sec, ends, ends, False)
        out, mixed, rows_log = attend_tile(
            first, route, wq[...], wot[...], k2[...], v2[...], allowed
        )
        after = rows + out
        h1_ref[j] = after
        mixed_ref[j] = mixed
        log_ref[j] = rows_log
        third_s[j] = norm_of(after, gain_of(recv_ref, 0, 2))[0].astype(BF)
        acc[j] = after
        return carry

    lax.fori_loop(0, 4, tile, 0)
    wait_whole(f_own, w_in, sems.at[9])
    wait_whole(f_own, w_out, sems.at[10])

    def chunk(c, carry):
        third = third_s[...].reshape(512, 512)
        pre = nn(third, w_in[c])
        hidden = (0.5 * pre * (1.0 + lax.erf(pre * 0.7071067811865476))).astype(BF)
        acc[...] += nn(hidden, w_out[c]).reshape(4, 128, 512)
        return carry

    lax.fori_loop(0, 4, chunk, 0)
    for j in range(4):
        h2 = acc[j]
        h2_ref[j] = h2
        memory = norm_of(h2, gain_of(recv_ref, 0, 1))[0].astype(BF)
        mem_ref[j] = memory
        kvm_ref[j] = nn(memory, kvc_ref[...]).astype(BF)


def dec_self_kernel(
    sec_ref, recv_ref, wa_own, wa_oth, kvw_own, kvw_oth,
    g1_ref, mixed_ref, log_ref,
    wq, wot, wkv, kv_s, k2, v2, sems,
):
    sec = sec_ref[0]
    mine = sec == 1
    load_whole(mine, kvw_own, kvw_oth, wkv, sems.at[0])
    load_columns(mine, wa_own, wa_oth, 0, wq, sems, 1)
    load_columns(mine, wa_own, wa_oth, 128, wot, sems, 5)
    wait_whole(kvw_own, wkv, sems.at[0])
    own_self_kv(recv_ref, 1, sec, gain_of(recv_ref, 1, 0), wkv[...], kv_s)
    widen_kv(kv_s, k2, v2)
    wait_columns(wa_own, 0, wq, sems, 1)
    wait_columns(wa_own, 128, wot, sems, 5)
    ends = ends_of(extra_of(recv_ref, 1, 0).astype(F32))
    router_block = extra_of(recv_ref, 1, 0)

    def tile(j, carry):
        rows = rows_of(recv_ref, 1, j)
        first = norm_of(rows, gain_of(recv_ref, 1, 0))[0].astype(BF)
        code_row = extra_of(recv_ref, 1, j).astype(F32)[CODE_ROW : CODE_ROW + 1, 0:128]
        route = routing(first, router_block, code_row)
        allowed = allowed_rows(j, sec, ends, ends, True)
        out, mixed, rows_log = attend_tile(
            first, route, wq[...], wot[...], k2[...], v2[...], allowed
        )
        g1_ref[j] = rows + out
        mixed_ref[j] = mixed
        log_ref[j] = rows_log
        return carry

    lax.fori_loop(0, 4, tile, 0)


def cross_kv(kvm_ref, kvo_ref, sec, kv_s):
    for j in range(4):
        kv_s[j, sec] = kvm_ref[j]
        kv_s[j, 1 - sec] = kvo_ref[j]


def dec_cross_kernel(
    sec_ref, recv_ref, g1_ref, kvm_ref, kvo_ref, rc_ref, cot_ref, wa_own, wa_oth, f_own, f_oth,
    g3_ref, dg2_ref, mixed_ref, log_ref, gain_ref, keep_ref, send_ref,
    wq, wot, w_in, w_out, kv_s, k2, v2, third_s, third_t, cot_t, acc, dthird, sems,
):
    sec = sec_ref[0]
    low = sec == 0
    load_columns(low, wa_own, wa_oth, 256, wq, sems, 0)
    load_columns(low, wa_oth, wa_own, 256, wot, sems, 4)
    load_whole(low, f_own, f_oth, w_in, sems.at[8])
    load_whole(low, f_oth, f_own, w_out, sems.at[9])
    cross_kv(kvm_ref, kvo_ref, sec, kv_s)
    widen_kv(kv_s, k2, v2)
    wait_columns(wa_own, 256, wq, sems, 0)
    wait_columns(wa_own, 256, wot, sems, 4)
    ends_k = ends_of(extra_of(recv_ref, 0, 0).astype(F32))
    ends_q = ends_of(extra_of(recv_ref, 1, 0).astype(F32))

    def tile(j, carry):
        before = g1_ref[j]
        second = norm_of(before, gain_of(recv_ref, 1, 1))[0].astype(BF)
        code_row = extra_of(recv_ref, 1, j).astype(F32)[CODE_ROW : CODE_ROW + 1, 128:256]
        route = routing(second, rc_ref[...], code_row)
        allowed = allowed_rows(j, sec, ends_q, ends_k, False)
        out, mixed, rows_log = attend_tile(
            second, route, wq[...], wot[...], k2[...], v2[...], allowed
        )
        after = before + out
        mixed_ref[j] = mixed
        log_ref[j] = rows_log
        third_s[j] = norm_of(after, gain_of(recv_ref, 1, 2))[0].astype(BF)
        acc[j] = after
        return carry

    lax.fori_loop(0, 4, tile, 0)
    for j in range(4):
        dg2_ref[j] = acc[j]
    third_t[...] = turned_rows(third_s[...].reshape(512, 512))
    cot_t[...] = turned_rows(cot_ref[...].reshape(512, 512))
    dthird[...] = jnp.zeros_like(dthird)
    wait_whole(f_own, w_in, sems.at[8])
    wait_whole(f_own, w_out, sems.at[9])

    def chunk(c, carry):
        third = third_s[...].reshape(512, 512)
        cot = cot_ref[...].reshape(512, 512)
        pre = nn(third, w_in[c])
        hidden, slope = gelu_parts(pre)
        hidden = hidden.astype(BF)
        acc[...] += nn(hidden, w_out[c]).reshape(4, 128, 512)
        dpre = (nt(cot, w_out[c]) * slope).astype(BF)
        dthird[...] += nt(dpre, w_in[c])
        split_halves(nn(third_t[...], dpre), sec, keep_ref, send_ref, c, 0)
        split_halves(nn(cot_t[...], hidden), sec, keep_ref, send_ref, c, 512)
        return carry

    lax.fori_loop(0, 4, chunk, 0)
    total = jnp.zeros((1, 512), F32)
    for j in range(4):
        g3_ref[j] = acc[j].astype(BF)
        gain = gain_of(recv_ref, 1, 2)
        unused_out, unit, scaled = norm_of(dg2_ref[j], gain)
        back, gain_grad = norm_back(dthird[128 * j : 128 * j + 128, :], unit, scaled, gain)
        dg2_ref[j] = cot_ref[j].astype(F32) + back
        total = total + gain_grad
    gain_ref[...] = total


def cross_back_kernel(
    sec_ref, recv_ref, g1_ref, dg2_ref, mixed_ref, log_ref, kvm_ref, kvo_ref, rc_ref, wa_own, wa_oth,
    dg1_ref, gain_ref, own_ref, send_ref, router_ref, keepw_ref, sendw_ref,
    wq, wot, kv_s, k2, v2, segk, grad_k, grad_v, second_s, gated_s, dz_s, dq_s, dlog_s, sems,
):
    sec = sec_ref[0]
    low = sec == 0
    load_columns(low, wa_own, wa_oth, 256, wq, sems, 0)
    load_columns(low, wa_oth, wa_own, 256, wot, sems, 4)
    cross_kv(kvm_ref, kvo_ref, sec, kv_s)
    widen_kv(kv_s, k2, v2)
    ends_k = ends_of(extra_of(recv_ref, 0, 0).astype(F32))
    ends_q = ends_of(extra_of(recv_ref, 1, 0).astype(F32))
    key_segments_t(ends_k, segk)
    grad_k[...] = jnp.zeros_like(grad_k)
    grad_v[...] = jnp.zeros_like(grad_v)
    wait_columns(wa_own, 256, wq, sems, 0)
    wait_columns(wa_own, 256, wot, sems, 4)

    def tile(j, total):
        gain = gain_of(recv_ref, 1, 1)
        second, unit, scaled = norm_of(g1_ref[j], gain)
        second = second.astype(BF)
        second_s[j] = second
        code_row = extra_of(recv_ref, 1, j).astype(F32)[CODE_ROW : CODE_ROW + 1, 128:256]
        route = routing(second, rc_ref[...], code_row)
        allowed = allowed_cols(j, sec, ends_q, segk, False)
        grad_rows = attend_back_tile(
            j, dg2_ref[j], second, route, mixed_ref[j], log_ref[j], wq[...], wot[...], rc_ref[...],
            ROUTER_LANES[2], k2[...], v2[...], allowed, grad_k, grad_v, gated_s, dz_s, dq_s, dlog_s,
        )
        back, gain_grad = norm_back(grad_rows, unit, scaled, gain)
        dg1_ref[j] = dg2_ref[j] + back
        return total + gain_grad

    gain_ref[...] = lax.fori_loop(0, 4, tile, jnp.zeros((1, 512), F32))
    fold_kv(grad_k, grad_v, sec, own_ref, send_ref)
    second_t = turned_rows(second_s[...].reshape(512, 512))
    router_ref[...] = nn(second_t, dlog_s[...].reshape(512, 128))
    attention_weight_grads(second_t, gated_s, dz_s, dq_s, sec, keepw_ref, sendw_ref)


def self_back_kernel(
    layer, sec_ref, recv_ref, up_ref, mixed_ref, log_ref, wa_own, wa_oth, kvw_own, kvw_oth,
    dfirst_ref, own_ref, send_ref, router_ref, keepw_ref, sendw_ref,
    wq, wot, wkv, kv_s, k2, v2, segk, grad_k, grad_v, first_s, gated_s, dz_s, dq_s, dlog_s, sems,
):
    sec = sec_ref[0]
    mine = sec == layer
    load_whole(mine, kvw_own, kvw_oth, wkv, sems.at[0])
    load_columns(mine, wa_own, wa_oth, 0, wq, sems, 1)
    load_columns(mine, wa_own, wa_oth, 128, wot, sems, 5)
    ends = ends_of(extra_of(recv_ref, layer, 0).astype(F32))
    key_segments_t(ends, segk)
    grad_k[...] = jnp.zeros_like(grad_k)
    grad_v[...] = jnp.zeros_like(grad_v)
    wait_whole(kvw_own, wkv, sems.at[0])
    own_self_kv(recv_ref, layer, sec, gain_of(recv_ref, layer, 0), wkv[...], kv_s)
    widen_kv(kv_s, k2, v2)
    wait_columns(wa_own, 0, wq, sems, 1)
    wait_columns(wa_own, 128, wot, sems, 5)
    router_block = extra_of(recv_ref, layer, 0)

    def tile(j, carry):
        first = norm_of(rows_of(recv_ref, layer, j), gain_of(recv_ref, layer, 0))[0].astype(BF)
        first_s[j] = first
        code_row = extra_of(recv_ref, layer, j).astype(F32)[CODE_ROW : CODE_ROW + 1, 0:128]
        route = routing(first, router_block, code_row)
        allowed = allowed_cols(j, sec, ends, segk, layer == 1)
        dfirst_ref[j] = attend_back_tile(
            j, up_ref[j], first, route, mixed_ref[j], log_ref[j], wq[...], wot[...], router_block,
            ROUTER_LANES[layer], k2[...], v2[...], allowed, grad_k, grad_v, gated_s, dz_s, dq_s,
            dlog_s,
        )
        return carry

    lax.fori_loop(0, 4, tile, 0)
    fold_kv(grad_k, grad_v, sec, own_ref, send_ref)
    first_t = turned_rows(first_s[...].reshape(512, 512))
    router_ref[...] = nn(first_t, dlog_s[...].reshape(512, 128))
    attention_weight_grads(first_t, gated_s, dz_s, dq_s, sec, keepw_ref, sendw_ref)


def enc_ffn_back_kernel(
    sec_ref, recv_ref, h1_ref, h2_ref, mem_ref, own_ref, come_ref, kvc_ref, f_own, f_oth,
    dh1_ref, gain_ref, gain2_ref, wkv_ref, keep_ref, send_ref,
    w_in, w_out, third_s, third_t, dy_s, dy_t, dthird, sems,
):
    sec = sec_ref[0]
    low = sec == 0
    load_whole(low, f_own, f_oth, w_in, sems.at[0])
    load_whole(low, f_oth, f_own, w_out, sems.at[1])
    dkv = (own_ref[...] + come_ref[...].astype(F32)).astype(BF)
    wkv_ref[...] = nn(turned_rows(mem_ref[...].reshape(512, 512)), dkv.reshape(512, 128))

    def tile(j, total):
        gain = gain_of(recv_ref, 0, 1)
        dkv_j = (own_ref[j] + come_ref[j].astype(F32)).astype(BF)
        dmem = rounded(nt(dkv_j, kvc_ref[...]))
        unused_out, unit, scaled = norm_of(h2_ref[j], gain)
        back, gain_grad = norm_back(dmem, unit, scaled, gain)
        dh1_ref[j] = back
        dy_s[j] = back.astype(BF)
        third_s[j] = norm_of(h1_ref[j], gain_of(recv_ref, 0, 2))[0].astype(BF)
        return total + gain_grad

    gain_ref[...] = lax.fori_loop(0, 4, tile, jnp.zeros((1, 512), F32))
    third_t[...] = turned_rows(third_s[...].reshape(512, 512))
    dy_t[...] = turned_rows(dy_s[...].reshape(512, 512))
    dthird[...] = jnp.zeros_like(dthird)
    wait_whole(f_own, w_in, sems.at[0])
    wait_whole(f_own, w_out, sems.at[1])

    def chunk(c, carry):
        pre = nn(third_s[...].reshape(512, 512), w_in[c])
        hidden, slope = gelu_parts(pre)
        hidden = hidden.astype(BF)
        dpre = (nt(dy_s[...].reshape(512, 512), w_out[c]) * slope).astype(BF)
        dthird[...] += nt(dpre, w_in[c])
        split_halves(nn(third_t[...], dpre), sec, keep_ref, send_ref, c, 0)
        split_halves(nn(dy_t[...], hidden), sec, keep_ref, send_ref, c, 512)
        return carry

    lax.fori_loop(0, 4, chunk, 0)
    total = jnp.zeros((1, 512), F32)
    for j in range(4):
        gain = gain_of(recv_ref, 0, 2)
        unused_out, unit, scaled = norm_of(h1_ref[j], gain)
        back, gain_grad = norm_back(dthird[128 * j : 128 * j + 128, :], unit, scaled, gain)
        dh1_ref[j] += back
        total = total + gain_grad
    gain2_ref[...] = total


def finish_kernel(
    sec_ref, recv_ref, up0, up1, df0, df1, own0, own1, come0, come1, kvw_own, kvw_oth,
    wkvc_ref, r0, r1, rc, gain_b, gain_e1, gain_e2, gain_d2,
    dx_ref, keep_ref, send_ref,
    wkv0, wkv1, first_s, sems,
):
    sec = sec_ref[0]
    load_whole(sec == 0, kvw_own, kvw_oth, wkv0, sems.at[0])
    load_whole(sec == 1, kvw_own, kvw_oth, wkv1, sems.at[1])
    wait_whole(kvw_own, wkv0, sems.at[0])
    wait_whole(kvw_own, wkv1, sems.at[1])
    first_gains = []
    kv_grads = []
    for layer in range(2):
        up, df, own, come, wkv = (
            (up0, df0, own0, come0, wkv0),
            (up1, df1, own1, come1, wkv1),
        )[layer]

        def tile(j, total, layer=layer, up=up, df=df, own=own, come=come, wkv=wkv):
            gain = gain_of(recv_ref, layer, 0)
            first, unit, scaled = norm_of(rows_of(recv_ref, layer, j), gain)
            first_s[j] = first.astype(BF)
            dkv = (own[j] + come[j].astype(F32)).astype(BF)
            dfirst = df[j] + nt(dkv, wkv[...])
            back, gain_grad = norm_back(dfirst, unit, scaled, gain)
            dx_ref[layer, j] = (up[j] + back).astype(BF)
            return total + gain_grad

        first_gains.append(lax.fori_loop(0, 4, tile, jnp.zeros((1, 512), F32)))
        dkv = (own[...] + come[...].astype(F32)).astype(BF).reshape(512, 128)
        kv_grads.append(nn(turned_rows(first_s[...].reshape(512, 512)), dkv))
    kv_grads.append(wkvc_ref[...])
    for i, grad in enumerate(kv_grads):
        cut = slice(128 * i, 128 * i + 128)
        keep_ref[:, cut] = jnp.where(sec == 0, grad[0:256], grad[256:512]).astype(BF)
        send_ref[:, cut] = jnp.where(sec == 0, grad[256:512], grad[0:256]).astype(BF)
    gains = (first_gains[0], gain_e1[...], gain_e2[...], first_gains[1], gain_b[...], gain_d2[...])
    lanes = lax.broadcasted_iota(jnp.int32, (128, 128), 1)
    blocks = []
    for b in range(4):
        cut = slice(128 * b, 128 * b + 128)
        misc = r0[cut, :] + r1[cut, :] + rc[cut, :]
        for i, row in enumerate(gains):
            misc = misc + jnp.where(lanes == GAIN_LANE + i, row_to_col(row[:, cut]), 0.0)
        blocks.append(misc)
    for b in range(2):
        cut = slice(128 * b, 128 * b + 128)
        keep_ref[cut, 384:512] = jnp.where(sec == 0, blocks[b], blocks[b + 2]).astype(BF)
        send_ref[cut, 384:512] = jnp.where(sec == 0, blocks[b + 2], blocks[b]).astype(BF)


def shaped(dims, kind):
    return jax.ShapeDtypeStruct(dims, kind)


def run(kernel, args, places, outs, scratch, flops):
    space = {
        "s": pl.BlockSpec(memory_space=pltpu.SMEM),
        "v": pl.BlockSpec(memory_space=pltpu.VMEM),
        "a": pl.BlockSpec(memory_space=pl.ANY),
    }
    return pl.pallas_call(
        kernel,
        out_shape=outs,
        in_specs=[space[p] for p in places],
        out_specs=jax.tree.map(lambda _: space["v"], outs),
        scratch_shapes=scratch,
        compiler_params=pltpu.CompilerParams(vmem_limit_bytes=VMEM_LIMIT),
        cost_estimate=pl.CostEstimate(flops=flops, bytes_accessed=8 << 20, transcendentals=0),
    )(*args)


def vm(*dims, kind=BF):
    return pltpu.VMEM(dims, kind)


def swapped(value):
    return lax.ppermute(value, "section", [(0, 1), (1, 0)])


def to_all(value, axes):
    return lax.all_to_all(value, axes, split_axis=0, concat_axis=0, tiled=True)


def from_all(value):
    return to_all(jnp.broadcast_to(value[None], (4,) + value.shape), "mp")


def scattered(kept, come):
    summed = (kept.astype(F32) + come.astype(F32)).astype(BF)
    return last_stages(summed)


def last_stages(summed):
    parts = to_all(summed, "mp")
    quarter = jnp.sum(parts.astype(F32), 0).astype(BF)
    rows, width = quarter.shape
    dp = lax.axis_size("dp")
    pieces = to_all(quarter.reshape(dp, rows // dp, width), "dp")
    return jnp.sum(pieces.astype(F32), 0)


def per_device(
    inputs,
    lengths,
    routes_self,
    routes_cross,
    gains,
    router_self,
    query_self,
    keyval_self,
    output_self,
    ffn_in,
    ffn_out,
    router_cross,
    query_cross,
    keyval_cross,
    output_cross,
    cotangent,
):
    sec = lax.axis_index("section")
    low = sec == 0
    sec_arr = sec.astype(jnp.int32).reshape(1)
    rows = inputs[0, :, 0]

    code_self = routes_self[0, :, 0, :, 0] + 8 * routes_self[0, :, 0, :, 1]
    code_cross = routes_cross[:, 0, :, 0] + 8 * routes_cross[:, 0, :, 1]
    codes = jnp.concatenate(
        [
            code_self.reshape(4, 2, 128).transpose(1, 0, 2).reshape(8, 128),
            code_cross.reshape(4, 2, 128).transpose(1, 0, 2).reshape(8, 128),
        ],
        1,
    ).astype(BF)
    lens = lengths[0, :, 0]
    lens = jnp.concatenate([lens, lens], 0)
    len_row = jnp.zeros((8, 512), BF)
    len_row = len_row.at[:, 0:8].set((lens // 32).astype(BF))
    len_row = len_row.at[:, 128:136].set((lens % 32).astype(BF))
    extra = jnp.concatenate(
        [
            jnp.broadcast_to(gains[0][None], (8, 3, 512)),
            jnp.pad(codes, ((0, 0), (0, 256)))[:, None],
            len_row[:, None],
            jnp.zeros((8, 3, 512), BF),
            jnp.broadcast_to(router_self[0].T[None], (8, 8, 512)),
        ],
        1,
    )
    router_c = jnp.concatenate([jnp.zeros((8, 512), BF), router_cross.T], 0)

    packed = run(
        pack_kernel,
        (rows, gains[0], keyval_self[0], extra),
        "vvvv",
        shaped((8, 176, 512), BF),
        [],
        10**9,
    )
    recv = to_all(packed, ("section", "mp"))

    q_cols = query_self[0].transpose(1, 0, 2).reshape(512, 128)
    o_cols = output_self[0].reshape(128, 512).T
    c_cols = jnp.where(
        low,
        query_cross.transpose(1, 0, 2).reshape(512, 128),
        output_cross.reshape(128, 512).T,
    )
    wa_own = from_all(jnp.concatenate([q_cols, o_cols, c_cols], 1))
    wa_oth = swapped(wa_own)
    kvw_own = keyval_self[0]
    kvw_oth = swapped(kvw_own)

    w_in, w_out = ffn_in[0], ffn_out[0]
    half_come = swapped(jnp.where(low, w_out, w_in))
    enc_own = from_all(jnp.where(low, w_in, half_come))
    enc_oth = swapped(enc_own)
    dec_own = from_all(jnp.where(low, half_come, w_out))
    dec_oth = swapped(dec_own)

    cot_cut = lax.dynamic_index_in_dim(cotangent[:, 0].reshape(4, 2, 128, 512), sec, 1, False)
    cot = to_all(cot_cut, "mp")

    act = shaped((4, 128, 512), F32)
    actb = shaped((4, 128, 512), BF)
    mixed_s = shaped((4, 256, 128), F32)
    log_s = shaped((4, 2, 128), F32)
    kv_b = shaped((4, 128, 128), BF)
    kv_f = shaped((4, 128, 128), F32)
    row_s = shaped((1, 512), F32)
    ffn_g = shaped((4, 256, 1024), BF)
    att_g = shaped((4, 256, 256), BF)
    lane_s = shaped((512, 128), F32)
    attn_scratch = [vm(512, 512), vm(512, 512)]
    kv_scratch = [vm(4, 2, 128, 128), vm(1024, 128), vm(1024, 128)]
    back_scratch = [
        vm(1024, 128, kind=F32), vm(1024, 128, kind=F32), vm(1024, 128, kind=F32),
        vm(4, 128, 512), vm(4, 128, 512), vm(4, 128, 512), vm(4, 128, 512), vm(4, 128, 128),
    ]
    ffn_scratch = [vm(4, 512, 512), vm(4, 512, 512)]

    h1, h2, mixed_e, log_e, memory, kvm = run(
        enc_fwd_kernel,
        (sec_arr, recv, keyval_cross, wa_own, wa_oth, kvw_own, kvw_oth, enc_own, enc_oth),
        "svvaaaaaa",
        (act, act, mixed_s, log_s, actb, kv_b),
        attn_scratch + [vm(512, 128)] + ffn_scratch + kv_scratch
        + [vm(4, 128, 512), vm(4, 128, 512, kind=F32), pltpu.SemaphoreType.DMA((11,))],
        4 * 10**9,
    )
    kvm_oth = swapped(kvm)
    g1, mixed_d, log_d = run(
        dec_self_kernel,
        (sec_arr, recv, wa_own, wa_oth, kvw_own, kvw_oth),
        "svaaaa",
        (act, mixed_s, log_s),
        attn_scratch + [vm(512, 128)] + kv_scratch + [pltpu.SemaphoreType.DMA((9,))],
        2 * 10**9,
    )
    g3, dg2, mixed_c, log_c, gain_d2, keep_d, send_d = run(
        dec_cross_kernel,
        (sec_arr, recv, g1, kvm, kvm_oth, router_c, cot, wa_own, wa_oth, dec_own, dec_oth),
        "svvvvvvaaaa",
        (actb, act, mixed_s, log_s, row_s, ffn_g, ffn_g),
        attn_scratch + ffn_scratch + kv_scratch
        + [vm(4, 128, 512), vm(512, 512), vm(512, 512), vm(4, 128, 512, kind=F32)]
        + [vm(512, 512, kind=F32), pltpu.SemaphoreType.DMA((10,))],
        8 * 10**9,
    )
    come_d = swapped(send_d)
    outs_recv = to_all(jnp.concatenate([memory, g3], 0), ("section", "mp"))
    dg1, gain_b, own_c, sendkv_c, router_cg, keep_wc, send_wc = run(
        cross_back_kernel,
        (sec_arr, recv, g1, dg2, mixed_c, log_c, kvm, kvm_oth, router_c, wa_own, wa_oth),
        "svvvvvvvvaa",
        (act, row_s, kv_f, kv_b, lane_s, att_g, att_g),
        attn_scratch + kv_scratch + back_scratch + [pltpu.SemaphoreType.DMA((8,))],
        4 * 10**9,
    )
    comekv_c = swapped(sendkv_c)
    ffn_dec = scattered(keep_d, come_d)
    self_scratch = (
        attn_scratch + [vm(512, 128)] + kv_scratch + back_scratch + [pltpu.SemaphoreType.DMA((9,))]
    )
    self_outs = (act, kv_f, kv_b, lane_s, att_g, att_g)
    df1, own_1, sendkv_1, router_1g, keep_w1, send_w1 = run(
        functools.partial(self_back_kernel, 1),
        (sec_arr, recv, dg1, mixed_d, log_d, wa_own, wa_oth, kvw_own, kvw_oth),
        "svvvvaaaa",
        self_outs,
        self_scratch,
        4 * 10**9,
    )
    comekv_1 = swapped(sendkv_1)
    dh1, gain_e1, gain_e2, wkvc, keep_e, send_e = run(
        enc_ffn_back_kernel,
        (sec_arr, recv, h1, h2, memory, own_c, comekv_c, keyval_cross, enc_own, enc_oth),
        "svvvvvvvaa",
        (act, row_s, row_s, lane_s, ffn_g, ffn_g),
        ffn_scratch
        + [vm(4, 128, 512), vm(512, 512), vm(4, 128, 512), vm(512, 512)]
        + [vm(512, 512, kind=F32), pltpu.SemaphoreType.DMA((2,))],
        8 * 10**9,
    )
    come_e = swapped(send_e)
    df0, own_0, sendkv_0, router_0g, keep_w0, send_w0 = run(
        functools.partial(self_back_kernel, 0),
        (sec_arr, recv, dh1, mixed_e, log_e, wa_own, wa_oth, kvw_own, kvw_oth),
        "svvvvaaaa",
        self_outs,
        self_scratch,
        4 * 10**9,
    )
    comekv_0 = swapped(sendkv_0)
    ffn_enc = scattered(keep_e, come_e)
    dx, keep_s, send_s = run(
        finish_kernel,
        (
            sec_arr, recv, dh1, dg1, df0, df1, own_0, own_1, comekv_0, comekv_1, kvw_own, kvw_oth,
            wkvc, router_0g, router_1g, router_cg, gain_b, gain_e1, gain_e2, gain_d2,
        ),
        "svvvvvvvvvaavvvvvvvv",
        (shaped((2, 4, 128, 512), BF), shaped((256, 512), BF), shaped((256, 512), BF)),
        [vm(512, 128), vm(512, 128), vm(4, 128, 512), pltpu.SemaphoreType.DMA((2,))],
        10**9,
    )
    dx_recv = to_all(dx.reshape(8, 128, 512), ("section", "mp"))
    send_small = jnp.concatenate(
        [send_w0, send_w1, send_wc, send_s.reshape(256, 4, 128).transpose(1, 0, 2)], 2
    )
    come_small = swapped(send_small)
    keep_small = jnp.concatenate(
        [keep_w0, keep_w1, keep_wc, keep_s.reshape(256, 4, 128).transpose(1, 0, 2)], 2
    )
    summed = (keep_small.astype(F32) + come_small.astype(F32)).astype(BF)
    shared = summed[:, :, 768:].transpose(1, 0, 2).reshape(1, 256, 512)
    small = last_stages(
        jnp.concatenate([summed[:, :, :768], jnp.broadcast_to(shared, (4, 256, 512))], 2)
    )

    def placed(value):
        whole = value.reshape(2, 4, 128, 512).transpose(1, 0, 2, 3)
        return whole.reshape(1, 4, 1, 256, 512)

    share = small.shape[0]

    def query_of(at):
        return small[:, at : at + 128].reshape(share, 2, 64).transpose(1, 0, 2)

    def output_of(at):
        return small[:, at : at + 128].T.reshape(2, 64, share)

    misc = small[:, 1152:1280]

    def router_of(layer):
        return misc[:, ROUTER_LANES[layer] : ROUTER_LANES[layer] + 8]

    return (
        placed(outs_recv),
        placed(dx_recv).astype(F32),
        misc[:, GAIN_LANE : GAIN_LANE + 6].T.reshape(2, 3, share),
        jnp.stack([router_of(0), router_of(1)]),
        jnp.stack([query_of(0), query_of(256)]),
        jnp.stack([small[:, 768:896], small[:, 896:1024]]),
        jnp.stack([output_of(128), output_of(384)]),
        jnp.stack([ffn_enc[:, :512], ffn_dec[:, :512]]),
        jnp.stack([ffn_enc[:, 512:].T, ffn_dec[:, 512:].T]),
        router_of(2),
        query_of(512),
        small[:, 1024:1152],
        output_of(640),
    )


def solution(mesh):
    placed = (
        P("section", None, "dp", "mp", None),
        P("section", None, "dp", None),
        P("section", None, "dp", "mp", None),
        P(None, "dp", "mp", None),
        P("section", None, None),
        P("section", None, None),
        P("section", "mp", None, None),
        P("section", None, None),
        P("section", "mp", None, None),
        P("section", None, "mp"),
        P("section", "mp", None),
        P(),
        P("mp", None, None),
        P(),
        P("mp", None, None),
        P(None, "dp", "mp", None),
    )
    return jax.shard_map(
        per_device,
        mesh=mesh,
        in_specs=placed,
        out_specs=(
            P("section", None, "dp", "mp", None),
            P("section", None, "dp", "mp", None),
            P(None, None, ("section", "dp")),
            P(None, ("section", "dp"), None),
            P(None, "mp", ("section", "dp"), None),
            P(None, ("section", "dp"), None),
            P(None, "mp", None, ("section", "dp")),
            P(None, ("section", "dp"), "mp"),
            P(None, "mp", ("section", "dp")),
            P(("section", "dp"), None),
            P("mp", ("section", "dp"), None),
            P(("section", "dp"), None),
            P("mp", None, ("section", "dp")),
        ),
        check_vma=False,
    )
```

time: 5480 us -> 416 us (0.08)
  waiting for transfers between devices: 2400 us -> 167 us
  local copies, waits for them, and re-layouts: 1280 us -> 25.9 us
  other arithmetic: 654 us -> 30.5 us
  matrix products: 497 us -> 0 us
  starting transfers between devices: 365 us -> 53.3 us
  blocking collectives: 215 us -> 28.3 us
  Pallas kernels: 0 us -> 108 us
    reduce_scatter x48 -> x0, waiting for transfers between devices: 1010 us -> none  [the longest x12 248 us: hidden_sums(): return lax.psum_scatter(values, 'mp', scatter_dimension=0, tiled=True)]
    while x2580 -> x0, local copies, waits for them, and re-layouts: 588 us -> none
    while x150 -> x0, waiting for transfers between devices: 537 us -> none
    dot_general x258 -> x0, matrix products: 484 us -> none  [the longest x6 44.5 us: layer_forward(): hidden_pre = jnp.dot(gathered, w_in, preferred_element_type=jnp.float32)]
    gather x84 -> x0, local copies, waits for them, and re-layouts: 373 us -> none  [the longest x12 81.9 us: attend(): places[token_of]]
    all_gather x12 -> x0, waiting for transfers between devices: 312 us -> none  [hidden_rows(): return lax.all_gather(values, 'mp', axis=0, tiled=True)]
    all_to_all x84 -> x12, starting transfers between devices: 314 us -> 49.4 us  [to_all(): return lax.all_to_all(value, axes, split_axis=0, concat_axis=0, tiled=True)]
    all_to_all x84 -> x12, waiting for transfers between devices: 390 us -> 164 us  [to_all(): return lax.all_to_all(value, axes, split_axis=0, concat_axis=0, tiled=True)]
where the time goes in v1:
time: 416 us; the launch traced here: 415 us
  waiting for transfers between devices  167 us (40%)
  Pallas kernels  108 us (26%)
  starting transfers between devices  53.3 us (13%)
  other arithmetic  30.5 us (7%)
  blocking collectives  28.3 us (7%)
  local copies, waits for them, and re-layouts  25.9 us (6%)
    all_to_all x12, waiting for transfers between devices, to_all(): return lax.all_to_all(value, axes, split_axis=0, concat_axis=0, tiled=True)  164 us
    pallas_call x9, Pallas kernels, run(): pl.pallas_call(kernel, out_shape=outs, in_specs=[space[p] for p in places...  108 us
    all_to_all x12, starting transfers between devices, to_all(): return lax.all_to_all(value, axes, split_axis=0, concat_axis=0, tiled=True)  49.4 us
    all_to_all x1, blocking collectives, to_all(): return lax.all_to_all(value, axes, split_axis=0, concat_axis=0, tiled=True)  28.3 us
  transfers between devices with their start and end apart: 24, of which 12 were waited for; matrix products, arithmetic and copies ran while one was open for 9% of the time, Pallas kernels for 18%

profile of v1, /device:TPU:0, one launch (start us, length us, event | category | flops | bytes accessed | tf_op | source)
XLA Modules:
  0.0 414.7 jit_solution(5029132458323864579)
XLA Ops:
  6.3 5.2 %all-to-all-start.1 = ((bf16[4,512,384]{2,1,0:T(8,128)(2,1)}), bf16[4,512,384]{2,1,0:T(8,128)(2,1)}, u32[]{:S(2)}, u32[]{:S(2)}) async-start(bf16[4,512,384]{2,1,0:T(8,128)(2,1)} %broadcast_in_dim.53), calls=%async_computation.1 | async-start | bytes 3145728 | tf_op jit(solution)/shard_map/all_to_all | solution.py:726
  13.6 17.9 %all-to-all-done.1.wa_own = bf16[4,512,384]{2,1,0:T(8,128)(2,1)} async-done(((bf16[4,512,384]{2,1,0:T(8,128)(2,1)}), bf16[4,512,384]{2,1,0:T(8,128)(2,1)}, u32[]{:S(2)}, u32[]{:S(2)}) %all-to-all-start.1) | async-done | bytes 1572896 | tf_op jit(solution)/shard_map/all_to_all | solution.py:726
  31.6 28.3 %all_to_all.65.f_own = bf16[4,512,512]{2,1,0:T(8,128)(2,1)} all-to-all(bf16[4,512,512]{2,1,0:T(8,128)(2,1)S(1)} %broadcast_in_dim.54), channel_id=1, replica_groups=mesh['section'=2,'dp'=4,'mp'=4] {'mp'}, dimensions={0} | all-to-all | bytes 4194304 | tf_op jit(solution)/shard_map/all_to_all | solution.py:726
  61.5 4.6 %all-to-all-start.4 = ((bf16[4,512,512]{2,1,0:T(8,128)(2,1)}), bf16[4,512,512]{2,1,0:T(8,128)(2,1)}, u32[]{:S(2)}, u32[]{:S(2)}) async-start(bf16[4,512,512]{2,1,0:T(8,128)(2,1)} %broadcast_in_dim.55), calls=%async_computation.4 | async-start | bytes 4194304 | tf_op jit(solution)/shard_map/all_to_all | solution.py:726
  68.1 21.1 %all-to-all-done.4.f_own = bf16[4,512,512]{2,1,0:T(8,128)(2,1)} async-done(((bf16[4,512,512]{2,1,0:T(8,128)(2,1)}), bf16[4,512,512]{2,1,0:T(8,128)(2,1)}, u32[]{:S(2)}, u32[]{:S(2)}) %all-to-all-start.4) | async-done | bytes 2097184 | tf_op jit(solution)/shard_map/all_to_all | solution.py:726
  101.3 17.0 %all-to-all-done.recv_ref = bf16[8,176,512]{2,1,0:T(8,128)(2,1)S(1)} async-done(((bf16[8,176,512]{2,1,0:T(8,128)(2,1)}), bf16[8,176,512]{2,1,0:T(8,128)(2,1)S(1)}, u32[]{:S(2)}, u32[]{:S(2)}) %all-to-all-start) | async-done | bytes 1441824 | tf_op jit(solution)/shard_map/all_to_all | solution.py:726
  122.6 13.5 %shard_map.256 = (f32[4,128,512]{2,1,0:T(8,128)}, f32[4,128,512]{2,1,0:T(8,128)}, f32[4,256,128]{2,1,0:T(8,128)}, f32[4,2,128]{2,1,0:T(2,128)}, bf16[4,128,512]{...) custom-call(s32[1]{0:T(128)} %bitcast.sec_ref, bf16[8,176,512]{2,1,0:T(8,128)(2,1)} %copy-done.4, bf16[512,128]{1,0:T(8,128)(2,1)} %kvc_ref.3, ...), custom_call_target="tpu_custom_call" | custom-call | flops 4000000000 | bytes 8388608 | tf_op jit(solution)/shard_map/pallas_call | solution.py:706
  136.4 9.3 %shard_map.257 = (f32[4,128,512]{2,1,0:T(8,128)}, f32[4,256,128]{2,1,0:T(8,128)}, f32[4,2,128]{2,1,0:T(2,128)}) custom-call(s32[1]{0:T(128)} %bitcast.sec_ref, bf16[8,176,512]{2,1,0:T(8,128)(2,1)} %copy-done.4, bf16[4,512,384]{2,1,0:T(8,128)(2,1)} %all-to-all-done.1.wa_own, bf16[4,512,384]{2,1,0:T(8,128)(2,1)} %collective-permute-done.wa_oth, ...), custom_call_target="tpu_custom_call" | custom-call | flops 2000000000 | bytes 8388608 | tf_op jit(solution)/shard_map/pallas_call | solution.py:706
  146.6 19.6 %shard_map.258 = (bf16[4,128,512]{2,1,0:T(8,128)(2,1)}, f32[4,128,512]{2,1,0:T(8,128)}, f32[4,256,128]{2,1,0:T(8,128)}, f32[4,2,128]{2,1,0:T(2,128)}, f32[1,512]...) custom-call(s32[1]{0:T(128)} %bitcast.sec_ref, bf16[8,176,512]{2,1,0:T(8,128)(2,1)} %copy-done.4, ...), custom_call_target="tpu_custom_call" | custom-call | flops 8000000000 | bytes 8388608 | tf_op jit(solution)/shard_map/pallas_call | solution.py:706
  166.3 14.3 %shard_map.259 = (f32[4,128,512]{2,1,0:T(8,128)}, f32[1,512]{1,0:T(1,128)}, f32[4,128,128]{2,1,0:T(8,128)}, bf16[4,128,128]{2,1,0:T(8,128)(2,1)}, f32[512,128]{1...) custom-call(s32[1]{0:T(128)} %bitcast.sec_ref, bf16[8,176,512]{2,1,0:T(8,128)(2,1)} %copy-done.4, ...), custom_call_target="tpu_custom_call" | custom-call | flops 4000000000 | bytes 8388608 | tf_op jit(solution)/shard_map/pallas_call | solution.py:706
  181.2 13.1 %shard_map.262 = (f32[4,128,512]{2,1,0:T(8,128)}, f32[4,128,128]{2,1,0:T(8,128)}, bf16[4,128,128]{2,1,0:T(8,128)(2,1)}, f32[512,128]{1,0:T(8,128)}, bf16[4,256,2...) custom-call(s32[1]{0:T(128)} %bitcast.sec_ref, bf16[8,176,512]{2,1,0:T(8,128)(2,1)} %copy-done.4, ...), custom_call_target="tpu_custom_call" | custom-call | flops 4000000000 | bytes 8388608 | tf_op jit(solution)/shard_map/pallas_call | solution.py:706
  200.4 13.5 %shard_map.260 = (f32[4,128,512]{2,1,0:T(8,128)}, f32[1,512]{1,0:T(1,128)}, f32[1,512]{1,0:T(1,128)}, f32[512,128]{1,0:T(8,128)}, bf16[4,256,1024]{2,1,0:T(8,128)(2,1)}, /*index=5*/bf16[4,256,1024]{2,1,0:T(8,128)(2,1)}) custom-call(s32[1]{0:T(128)} %bitcast.sec_ref, bf16[8,176,512]{2,1,0:T(8,128)(2,1)} %copy-done.4, ...), custom_call_target="tpu_custom_call" | custom-call | flops 8000000000 | bytes 8388608 | tf_op jit(solution)/shard_map/pallas_call | solution.py:706
  213.9 12.9 %shard_map.261 = (f32[4,128,512]{2,1,0:T(8,128)}, f32[4,128,128]{2,1,0:T(8,128)}, bf16[4,128,128]{2,1,0:T(8,128)(2,1)}, f32[512,128]{1,0:T(8,128)}, bf16[4,256,2...) custom-call(s32[1]{0:T(128)} %bitcast.sec_ref, bf16[8,176,512]{2,1,0:T(8,128)(2,1)} %copy-done.4, ...), custom_call_target="tpu_custom_call" | custom-call | flops 4000000000 | bytes 8388608 | tf_op jit(solution)/shard_map/pallas_call | solution.py:706
  229.3 8.8 %shard_map.263 = (bf16[2,4,128,512]{3,2,1,0:T(8,128)(2,1)}, bf16[256,512]{1,0:T(8,128)(2,1)}, bf16[256,512]{1,0:T(8,128)(2,1)}) custom-call(s32[1]{0:T(128)} %bitcast.sec_ref, bf16[8,176,512]{2,1,0:T(8,128)(2,1)} %copy-done.4, f32[4,128,512]{2,1,0:T(8,128)} %get-tuple-element.92.up_ref.up0, f32[4,128,512]{2,1,0:T(8,128)} %get-tuple-element.93.up_ref.up1, ...), custom_call_target="tpu_custom_call" | custom-call | flops 1000000000 | bytes 8388608 | tf_op jit(solution)/shard_map/pallas_call | solution.py:706
  247.5 10.5 %all-to-all-done.6 = bf16[8,128,512]{2,1,0:T(8,128)(2,1)S(1)} async-done(((bf16[8,128,512]{2,1,0:T(8,128)(2,1)}), bf16[8,128,512]{2,1,0:T(8,128)(2,1)S(1)}, u32[]{:S(2)}, u32[]{:S(2)}) %all-to-all-start.6) | async-done | bytes 1048608 | tf_op jit(solution)/shard_map/all_to_all | solution.py:726
  269.5 18.7 %all-to-all-done.11 = bf16[4,256,1024]{2,1,0:T(8,128)(2,1)S(1)} async-done(((bf16[4,256,1024]{2,1,0:T(8,128)(2,1)}), bf16[4,256,1024]{2,1,0:T(8,128)(2,1)S(1)}, u32[]{:S(2)}, u32[]{:S(2)}) %all-to-all-start.11) | async-done | bytes 2097184 | tf_op jit(solution)/shard_map/all_to_all | solution.py:726
  288.2 4.7 %all-to-all-start.9 = ((bf16[4,256,1024]{2,1,0:T(8,128)(2,1)}), bf16[4,256,1024]{2,1,0:T(8,128)(2,1)}, u32[]{:S(2)}, u32[]{:S(2)}) async-start(bf16[4,256,1024]{2,1,0:T(8,128)(2,1)} %add_convert_fusion.1), calls=%async_computation.9 | async-start | bytes 4194304 | tf_op jit(solution)/shard_map/all_to_all | solution.py:726
  299.4 18.1 %all-to-all-done.9 = bf16[4,256,1024]{2,1,0:T(8,128)(2,1)} async-done(((bf16[4,256,1024]{2,1,0:T(8,128)(2,1)}), bf16[4,256,1024]{2,1,0:T(8,128)(2,1)}, u32[]{:S(2)}, u32[]{:S(2)}) %all-to-all-start.9) | async-done | bytes 2097184 | tf_op jit(solution)/shard_map/all_to_all | solution.py:726
  324.1 27.0 %all-to-all-done.7 = bf16[4,256,1280]{2,1,0:T(8,128)(2,1)S(1)} async-done(((bf16[4,256,1280]{2,1,0:T(8,128)(2,1)}), bf16[4,256,1280]{2,1,0:T(8,128)(2,1)S(1)}, u32[]{:S(2)}, u32[]{:S(2)}) %all-to-all-start.7) | async-done | bytes 2621472 | tf_op jit(solution)/shard_map/all_to_all | solution.py:726
  351.1 4.6 %all-to-all-start.12 = ((bf16[4,64,1024]{2,1,0:T(8,128)(2,1)}), bf16[4,64,1024]{2,1,0:T(8,128)(2,1)S(1)}, u32[]{:S(2)}, u32[]{:S(2)}) async-start(bf16[4,64,1024]{2,1,0:T(8,128)(2,1)} %bitcast.127), calls=%async_computation.12 | async-start | bytes 1048576 | tf_op jit(solution)/shard_map/all_to_all | solution.py:726
  358.7 10.7 %all-to-all-done.12 = bf16[4,64,1024]{2,1,0:T(8,128)(2,1)S(1)} async-done(((bf16[4,64,1024]{2,1,0:T(8,128)(2,1)}), bf16[4,64,1024]{2,1,0:T(8,128)(2,1)S(1)}, u32[]{:S(2)}, u32[]{:S(2)}) %all-to-all-start.12) | async-done | bytes 524320 | tf_op jit(solution)/shard_map/all_to_all | solution.py:726
  369.4 4.1 all-to-all-start.10
  375.0 12.6 %all-to-all-done.10 = bf16[4,64,1024]{2,1,0:T(8,128)(2,1)} async-done(((bf16[4,64,1024]{2,1,0:T(8,128)(2,1)}), bf16[4,64,1024]{2,1,0:T(8,128)(2,1)}, u32[]{:S(2)}, u32[]{:S(2)}) %all-to-all-start.10) | async-done | bytes 524320 | tf_op jit(solution)/shard_map/all_to_all | solution.py:726
  397.7 10.2 %all-to-all-done.8 = bf16[4,64,1280]{2,1,0:T(8,128)(2,1)S(1)} async-done(((bf16[4,64,1280]{2,1,0:T(8,128)(2,1)}), bf16[4,64,1280]{2,1,0:T(8,128)(2,1)S(1)}, u32[]{:S(2)}, u32[]{:S(2)}) %all-to-all-start.8) | async-done | bytes 655392 | tf_op jit(solution)/shard_map/all_to_all | solution.py:726
  (177 shorter events, 92.9 us)
Async XLA Ops:
  6.3 25.2 %all-to-all-start.1 = ((bf16[4,512,384]{2,1,0:T(8,128)(2,1)}), bf16[4,512,384]{2,1,0:T(8,128)(2,1)}, u32[]{:S(2)}, u32[]{:S(2)}) async-start(bf16[4,512,384]{2,1,0:T(8,128)(2,1)} %broadcast_in_dim.53), calls=%async_computation.1 | async-start | bytes 3145728 | tf_op jit(solution)/shard_map/all_to_all | solution.py:726
  11.5 2.0 collective-permute-start.2
  61.5 27.8 %all-to-all-start.4 = ((bf16[4,512,512]{2,1,0:T(8,128)(2,1)}), bf16[4,512,512]{2,1,0:T(8,128)(2,1)}, u32[]{:S(2)}, u32[]{:S(2)}) async-start(bf16[4,512,512]{2,1,0:T(8,128)(2,1)} %broadcast_in_dim.55), calls=%async_computation.4 | async-start | bytes 4194304 | tf_op jit(solution)/shard_map/all_to_all | solution.py:726
  67.4 54.6 %collective-permute-start.3 = (bf16[4,512,512]{2,1,0:T(8,128)(2,1)}, bf16[4,512,512]{2,1,0:T(8,128)(2,1)}, u32[]{:S(2)}, u32[]{:S(2)}) collective-permute-start(bf16[4,512,512]{2,1,0:T(8,128)(2,1)} %all_to_all.65.f_own), channel_id=1, source_target_pairs={{0,16},{16,0},{1,17},{17,1},{2,18},{18,2},{3,19},{19,3},{4,20},{20... | collective-permute-start | bytes 6291464 | tf_op jit(solution)/shard_map/ppermute | solution.py:722
  67.6 54.4 %collective-permute-start = (bf16[4,512,384]{2,1,0:T(8,128)(2,1)}, bf16[4,512,384]{2,1,0:T(8,128)(2,1)}, u32[]{:S(2)}, u32[]{:S(2)}) collective-permute-start(bf16[4,512,384]{2,1,0:T(8,128)(2,1)} %all-to-all-done.1.wa_own), channel_id=1, source_target_pairs={{0,16},{16,0},{1,17},{17,1},{2,18},{18,2},{3,19},{19,3},{4,20},{20... | collective-permute-start | bytes 4718600 | tf_op jit(solution)/shard_map/ppermute | solution.py:722
  89.2 56.6 %collective-permute-start.5 = (bf16[4,512,512]{2,1,0:T(8,128)(2,1)}, bf16[4,512,512]{2,1,0:T(8,128)(2,1)}, u32[]{:S(2)}, u32[]{:S(2)}) collective-permute-start(bf16[4,512,512]{2,1,0:T(8,128)(2,1)} %all-to-all-done.4.f_own), channel_id=1, source_target_pairs={{0,16},{16,0},{1,17},{17,1},{2,18},{18,2},{3,19},{19,3},{4,20},{20... | collective-permute-start | bytes 6291464 | tf_op jit(solution)/shard_map/ppermute | solution.py:722
  95.5 22.7 %all-to-all-start = ((bf16[8,176,512]{2,1,0:T(8,128)(2,1)}), bf16[8,176,512]{2,1,0:T(8,128)(2,1)S(1)}, u32[]{:S(2)}, u32[]{:S(2)}) async-start(bf16[8,176,512]{2,1,0:T(8,128)(2,1)} %shard_map.255), calls=%async_computation | async-start | bytes 2883584 | tf_op jit(solution)/shard_map/all_to_all | solution.py:726
  99.3 22.7 %collective-permute-start.1 = (bf16[512,128]{1,0:T(8,128)(2,1)S(1)}, bf16[512,128]{1,0:T(8,128)(2,1)S(1)}, u32[]{:S(2)}, u32[]{:S(2)}) collective-permute-start(bf16[512,128]{1,0:T(8,128)(2,1)S(1)} %bitcast.140), channel_id=1, source_target_pairs={{0,16},{16,0},{1,17},{17,1},{2,18},{18,2},{3,19},{19,3},{4,20},{20... | collective-permute-start | bytes 393224 | tf_op jit(solution)/shard_map/ppermute | solution.py:722
  118.3 27.5 %all-to-all-start.3 = ((bf16[4,128,512]{2,1,0:T(8,128)(2,1)}), bf16[4,128,512]{2,1,0:T(8,128)(2,1)S(1)}, u32[]{:S(2)}, u32[]{:S(2)}) async-start(bf16[4,128,512]{2,1,0:T(8,128)(2,1)} %dynamic-slice_bitcast_fusion), calls=%async_computation.3 | async-start | bytes 1048576 | tf_op jit(solution)/shard_map/all_to_all | solution.py:726
  136.1 9.7 %collective-permute-start.4 = (bf16[4,128,128]{2,1,0:T(8,128)(2,1)}, bf16[4,128,128]{2,1,0:T(8,128)(2,1)S(1)}, u32[]{:S(2)}, u32[]{:S(2)}) collective-permute-start(bf16[4,128,128]{2,1,0:T(8,128)(2,1)} %get-tuple-element.83.kvm_ref), channel_id=1, source_target_pairs={{0,16},{16,0},{1,17},{17,1},{2,18},{18,2},{3,19},{19,3},{4,20},{20... | collective-permute-start | bytes 393224 | tf_op jit(solution)/shard_map/ppermute | solution.py:722
  180.6 19.2 %collective-permute-start.6 = (bf16[4,128,128]{2,1,0:T(8,128)(2,1)}, bf16[4,128,128]{2,1,0:T(8,128)(2,1)S(1)}, u32[]{:S(2)}, u32[]{:S(2)}) collective-permute-start(bf16[4,128,128]{2,1,0:T(8,128)(2,1)} %get-tuple-element.91), channel_id=1, source_target_pairs={{0,16},{16,0},{1,17},{17,1},{2,18},{18,2},{3,19},{19,3},{4,20},{20... | collective-permute-start | bytes 393224 | tf_op jit(solution)/shard_map/ppermute | solution.py:722
  181.0 62.7 %collective-permute-start.11 = (bf16[4,256,1024]{2,1,0:T(8,128)(2,1)}, bf16[4,256,1024]{2,1,0:T(8,128)(2,1)}, u32[]{:S(2)}, u32[]{:S(2)}) collective-permute-start(bf16[4,256,1024]{2,1,0:T(8,128)(2,1)} %get-tuple-element.124), channel_id=1, source_target_pairs={{0,16},{16,0},{1,17},{17,1},{2,18},{18,2},{3,19},{19,3},{4,20},{20... | collective-permute-start | bytes 6291464 | tf_op jit(solution)/shard_map/ppermute | solution.py:722
  194.3 33.1 %collective-permute-start.8 = (bf16[4,128,128]{2,1,0:T(8,128)(2,1)}, bf16[4,128,128]{2,1,0:T(8,128)(2,1)S(1)}, u32[]{:S(2)}, u32[]{:S(2)}) collective-permute-start(bf16[4,128,128]{2,1,0:T(8,128)(2,1)} %get-tuple-element.103), channel_id=1, source_target_pairs={{0,16},{16,0},{1,17},{17,1},{2,18},{18,2},{3,19},{19,3},{4,20},{20... | collective-permute-start | bytes 393224 | tf_op jit(solution)/shard_map/ppermute | solution.py:722
  195.8 42.3 %all-to-all-start.5 = ((bf16[8,128,512]{2,1,0:T(8,128)(2,1)}), bf16[8,128,512]{2,1,0:T(8,128)(2,1)S(1)}, u32[]{:S(2)}, u32[]{:S(2)}) async-start(bf16[8,128,512]{2,1,0:T(8,128)(2,1)} %pad_maximum_fusion.2), calls=%async_computation.5 | async-start | bytes 2097152 | tf_op jit(solution)/shard_map/all_to_all | solution.py:726
  226.8 1.8 collective-permute-start.7
  239.1 18.9 %all-to-all-start.6 = ((bf16[8,128,512]{2,1,0:T(8,128)(2,1)}), bf16[8,128,512]{2,1,0:T(8,128)(2,1)S(1)}, u32[]{:S(2)}, u32[]{:S(2)}) async-start(bf16[8,128,512]{2,1,0:T(8,128)(2,1)} %bitcast.129), calls=%async_computation.6 | async-start | bytes 2097152 | tf_op jit(solution)/shard_map/all_to_all | solution.py:726
  243.2 22.4 %collective-permute-start.10 = (bf16[4,256,1024]{2,1,0:T(8,128)(2,1)}, bf16[4,256,1024]{2,1,0:T(8,128)(2,1)}, u32[]{:S(2)}, u32[]{:S(2)}) collective-permute-start(bf16[4,256,1024]{2,1,0:T(8,128)(2,1)} %get-tuple-element.122), channel_id=1, source_target_pairs={{0,16},{16,0},{1,17},{17,1},{2,18},{18,2},{3,19},{19,3},{4,20},{20... | collective-permute-start | bytes 6291464 | tf_op jit(solution)/shard_map/ppermute | solution.py:722
  259.0 29.2 %all-to-all-start.11 = ((bf16[4,256,1024]{2,1,0:T(8,128)(2,1)}), bf16[4,256,1024]{2,1,0:T(8,128)(2,1)S(1)}, u32[]{:S(2)}, u32[]{:S(2)}) async-start(bf16[4,256,1024]{2,1,0:T(8,128)(2,1)} %add_convert_fusion), calls=%async_computation.11 | async-start | bytes 4194304 | tf_op jit(solution)/shard_map/all_to_all | solution.py:726
  265.3 27.7 %collective-permute-start.9 = (bf16[4,256,896]{2,1,0:T(8,128)(2,1)}, bf16[4,256,896]{2,1,0:T(8,128)(2,1)}, u32[]{:S(2)}, u32[]{:S(2)}) collective-permute-start(bf16[4,256,896]{2,1,0:T(8,128)(2,1)} %pad_maximum_fusion.1), channel_id=1, source_target_pairs={{0,16},{16,0},{1,17},{17,1},{2,18},{18,2},{3,19},{19,3},{4,20},{20... | collective-permute-start | bytes 5505032 | tf_op jit(solution)/shard_map/ppermute | solution.py:722
  288.2 29.3 %all-to-all-start.9 = ((bf16[4,256,1024]{2,1,0:T(8,128)(2,1)}), bf16[4,256,1024]{2,1,0:T(8,128)(2,1)}, u32[]{:S(2)}, u32[]{:S(2)}) async-start(bf16[4,256,1024]{2,1,0:T(8,128)(2,1)} %add_convert_fusion.1), calls=%async_computation.9 | async-start | bytes 4194304 | tf_op jit(solution)/shard_map/all_to_all | solution.py:726
  317.5 33.6 %all-to-all-start.7 = ((bf16[4,256,1280]{2,1,0:T(8,128)(2,1)}), bf16[4,256,1280]{2,1,0:T(8,128)(2,1)S(1)}, u32[]{:S(2)}, u32[]{:S(2)}) async-start(bf16[4,256,1280]{2,1,0:T(8,128)(2,1)} %pad_maximum_fusion), calls=%async_computation.7 | async-start | bytes 5242880 | tf_op jit(solution)/shard_map/all_to_all | solution.py:726
  351.1 18.3 %all-to-all-start.12 = ((bf16[4,64,1024]{2,1,0:T(8,128)(2,1)}), bf16[4,64,1024]{2,1,0:T(8,128)(2,1)S(1)}, u32[]{:S(2)}, u32[]{:S(2)}) async-start(bf16[4,64,1024]{2,1,0:T(8,128)(2,1)} %bitcast.127), calls=%async_computation.12 | async-start | bytes 1048576 | tf_op jit(solution)/shard_map/all_to_all | solution.py:726
  369.4 18.2 %all-to-all-start.10 = ((bf16[4,64,1024]{2,1,0:T(8,128)(2,1)}), bf16[4,64,1024]{2,1,0:T(8,128)(2,1)}, u32[]{:S(2)}, u32[]{:S(2)}) async-start(bf16[4,64,1024]{2,1,0:T(8,128)(2,1)} %bitcast.126), calls=%async_computation.10 | async-start | bytes 1048576 | tf_op jit(solution)/shard_map/all_to_all | solution.py:726
  387.6 20.2 %all-to-all-start.8 = ((bf16[4,64,1280]{2,1,0:T(8,128)(2,1)}), bf16[4,64,1280]{2,1,0:T(8,128)(2,1)S(1)}, u32[]{:S(2)}, u32[]{:S(2)}) async-start(bf16[4,64,1280]{2,1,0:T(8,128)(2,1)} %bitcast.42), calls=%async_computation.8 | async-start | bytes 1310720 | tf_op jit(solution)/shard_map/all_to_all | solution.py:726
  (34 other events, 404.5 us)

commit v2 on v1

v2 whole, which is shorter than its diff:
```python
import functools

import jax
import jax.numpy as jnp
from jax import lax
from jax.experimental import pallas as pl
from jax.experimental.pallas import tpu as pltpu
from jax.sharding import PartitionSpec as P

EPS = 1e-05
MASK_VALUE = -1000000000.0
BF = jnp.bfloat16
F32 = jnp.float32
TILE = 256
EX_AT = 160
CODE_ROW = 3
LEN_ROW = 4
ROUTER_AT = 8
GAIN_LANE = 64
ROUTER_LANES = (8, 24, 40)
VMEM_LIMIT = 56 * 1024 * 1024


def nn(left, right):
    return lax.dot_general(left, right, (((1,), (0,)), ((), ())), preferred_element_type=F32)


def nt(left, right):
    return lax.dot_general(left, right, (((1,), (1,)), ((), ())), preferred_element_type=F32)


def tn(left, right):
    return lax.dot_general(left, right, (((0,), (0,)), ((), ())), preferred_element_type=F32)


def norm_of(values, gain_row):
    center = values - jnp.mean(values, 1, keepdims=True)
    scaled = lax.rsqrt(jnp.mean(center * center, 1, keepdims=True) + EPS)
    unit_rows = center * scaled
    return unit_rows * gain_row, unit_rows, scaled


def norm_back(upstream, unit_rows, scaled, gain_row):
    inner = upstream * gain_row
    result = scaled * (
        inner
        - jnp.mean(inner, 1, keepdims=True)
        - unit_rows * jnp.mean(inner * unit_rows, 1, keepdims=True)
    )
    return result, jnp.sum(upstream * unit_rows, 0, keepdims=True)


def eye_of(size):
    return lax.broadcasted_iota(jnp.int32, (size, size), 0) == lax.broadcasted_iota(
        jnp.int32, (size, size), 1
    )


def row_to_col(row):
    return jnp.sum(jnp.where(eye_of(128), row, 0.0), 1, keepdims=True)


def col_to_row(col):
    parts = []
    for at in range(0, col.shape[0], 128):
        part = jnp.where(eye_of(128), col[at : at + 128], 0.0)
        parts.append(jnp.sum(part, 0, keepdims=True))
    return jnp.concatenate(parts, 1)


def ends_of(extra):
    lengths = extra[LEN_ROW : LEN_ROW + 1, 0:8] * 32.0 + extra[LEN_ROW : LEN_ROW + 1, 128:136]
    ends = [lengths[:, 0:1]]
    for k in range(1, 8):
        ends.append(ends[-1] + lengths[:, k : k + 1])
    return ends


def segments(places, ends):
    total = jnp.where(places >= ends[0], 1.0, 0.0)
    for end in ends[1:]:
        total = total + jnp.where(places >= end, 1.0, 0.0)
    return total


def extra_of(recv_ref, layer, quarter):
    return recv_ref[4 * layer + quarter, EX_AT : EX_AT + 16, :]


def gain_of(recv_ref, layer, which):
    return extra_of(recv_ref, layer, 0).astype(F32)[which : which + 1, :]


def rows_of(recv_ref, layer, t):
    return recv_ref[pl.ds(4 * layer + 2 * t, 2), 0:128, :].reshape(TILE, 512).astype(F32)


def codes_of(recv_ref, layer, t, lane):
    cols = []
    for i in range(2):
        extra = extra_of(recv_ref, layer, 2 * t + i).astype(F32)
        cols.append(row_to_col(extra[CODE_ROW : CODE_ROW + 1, lane : lane + 128]))
    return jnp.concatenate(cols, 0)


def other_kv(recv_ref, layer, quarter):
    packed = recv_ref[4 * layer + quarter, 128:160, :]
    return jnp.concatenate([packed[:, 128 * c : 128 * c + 128] for c in range(4)], 0)


def routing(query_rows, router_block, code, m):
    second = jnp.floor(code * 0.125)
    first = code - 8.0 * second
    e0, e1 = first.astype(jnp.int32), second.astype(jnp.int32)
    logits = nt(query_rows, router_block)
    lanes = lax.broadcasted_iota(jnp.int32, logits.shape, 1)
    l0 = jnp.sum(jnp.where(lanes == e0 + ROUTER_AT, logits, 0.0), 1, keepdims=True)
    l1 = jnp.sum(jnp.where(lanes == e1 + ROUTER_AT, logits, 0.0), 1, keepdims=True)
    top = jnp.maximum(l0, l1)
    x0, x1 = jnp.exp(l0 - top), jnp.exp(l1 - top)
    total = x0 + x1
    owners = lax.broadcasted_iota(jnp.int32, (code.shape[0], 512), 1) >> 6
    mask0 = owners == (e0 ^ (2 * m))
    mask1 = owners == (e1 ^ (2 * m))
    return e0, e1, x0 / total, x1 / total, mask0, mask1


def fold(wide, mask):
    kept = jnp.where(mask, wide, 0.0)
    return kept[:, 0:128] + kept[:, 128:256] + kept[:, 256:384] + kept[:, 384:512]


def spread(a0, a1, m0, m1):
    parts = []
    for c in range(4):
        cut = slice(128 * c, 128 * c + 128)
        parts.append(jnp.where(m0[:, cut], a0, jnp.where(m1[:, cut], a1, 0.0)))
    return jnp.concatenate(parts, 1).astype(BF)


def rounded(value):
    return value.astype(BF).astype(F32)


def start_pick(cond, yes, no, dst, sem):
    @pl.when(cond)
    def _():
        pltpu.make_async_copy(yes, dst, sem).start()

    @pl.when(jnp.logical_not(cond))
    def _():
        pltpu.make_async_copy(no, dst, sem).start()


class Loads:
    def __init__(self, sems):
        self.sems, self.used = sems, 0

    def start(self, cond, yes, no, dst):
        sem = self.sems.at[self.used]
        self.used += 1
        start_pick(cond, yes, no, dst, sem)
        return functools.partial(lambda a, b, c: pltpu.make_async_copy(a, b, c).wait(), yes, dst, sem)

    def plain(self, src, dst):
        sem = self.sems.at[self.used]
        self.used += 1
        copy = pltpu.make_async_copy(src, dst, sem)
        copy.start()
        return copy.wait

    def rows(self, cond, yes, no, at, dst):
        cut = pl.ds(at, 128)
        return [
            self.start(cond, yes[b].at[cut], no[b].at[cut], dst.at[pl.ds(128 * b, 128)])
            for b in range(4)
        ]

    def blocks(self, cond, yes, no, dst):
        return [self.start(cond, yes[b], no[b], dst.at[b]) for b in range(4)]


def wait_all(waits):
    for wait in waits:
        wait()


def widen_kv(kv_ref, k2_ref, v2_ref):
    for j in range(4):
        kv = kv_ref[j].reshape(256, 128).astype(F32)
        turned = pltpu.roll(kv, 64, 1)
        low = lax.broadcasted_iota(jnp.int32, kv.shape, 1) < 64
        k2_ref[256 * j : 256 * j + 256, :] = jnp.where(low, kv, turned).astype(BF)
        v2_ref[256 * j : 256 * j + 256, :] = jnp.where(low, turned, kv).astype(BF)


def attend_tile(query_rows, route, w_qt, w_o, k2, v2, allowed):
    e0, e1, g0, g1, m0, m1 = route
    q_all = nt(query_rows, w_qt) * 0.125
    queries = jnp.concatenate([fold(q_all, m0), fold(q_all, m1)], 0).astype(BF)
    scores = nt(queries, k2)
    scores = jnp.concatenate(
        [
            jnp.where(allowed, scores[0:TILE], MASK_VALUE),
            jnp.where(allowed, scores[TILE:], MASK_VALUE),
        ],
        0,
    )
    top = jnp.max(scores, 1, keepdims=True)
    weights = jnp.exp(scores - top)
    total = jnp.sum(weights, 1, keepdims=True)
    mixed = nn(weights.astype(BF), v2) / total
    log_total = top + jnp.log(total)
    gated = spread(rounded(g0) * mixed[0:TILE], rounded(g1) * mixed[TILE:], m0, m1)
    return nn(gated, w_o), mixed, col_to_row(log_total)


def attend_back_tile(
    t, upstream, query_rows, route, mixed, log_row, w_qt, w_o, router_block, router_lane, k2, v2,
    allowed_t, grad_k, grad_v, gated_ref, dz_ref, dq_ref, dlog_ref,
):
    e0, e1, g0, g1, m0, m1 = route
    q_all = nt(query_rows, w_qt) * 0.125
    queries = jnp.concatenate([fold(q_all, m0), fold(q_all, m1)], 0).astype(BF)
    dz = upstream.astype(BF)
    dg_all = nt(dz, w_o)
    dgated0, dgated1 = fold(dg_all, m0), fold(dg_all, m1)
    r0, r1 = rounded(g0), rounded(g1)
    mixed0, mixed1 = mixed[0:TILE], mixed[TILE:]
    gated_ref[t] = spread(r0 * mixed0, r1 * mixed1, m0, m1)
    dz_ref[t] = dz
    dgate0 = rounded(jnp.sum(mixed0 * dgated0, 1, keepdims=True))
    dgate1 = rounded(jnp.sum(mixed1 * dgated1, 1, keepdims=True))
    do0, do1 = (r0 * dgated0).astype(BF), (r1 * dgated1).astype(BF)
    grad_mixed = jnp.concatenate([do0, do1], 0)
    inner_row = jnp.concatenate(
        [
            col_to_row(jnp.sum(do0.astype(F32) * mixed0, 1, keepdims=True)),
            col_to_row(jnp.sum(do1.astype(F32) * mixed1, 1, keepdims=True)),
        ],
        1,
    )
    scores = nt(k2, queries)
    scores = jnp.concatenate(
        [
            jnp.where(allowed_t, scores[:, 0:TILE], MASK_VALUE),
            jnp.where(allowed_t, scores[:, TILE:], MASK_VALUE),
        ],
        1,
    )
    probs = jnp.exp(scores - log_row)
    grad_probs = nt(v2, grad_mixed)
    grad_scores = (probs * (grad_probs - inner_row)).astype(BF)
    grad_v[...] += nn(probs.astype(BF), grad_mixed)
    grad_k[...] += nn(grad_scores, queries)
    grad_q = rounded(tn(grad_scores, k2) * 0.125)
    dq_all = spread(grad_q[0:TILE], grad_q[TILE:], m0, m1)
    dq_ref[t] = dq_all
    grad_rows = nn(dq_all, w_qt)
    mean_grad = g0 * dgate0 + g1 * dgate1
    dc0, dc1 = g0 * (dgate0 - mean_grad), g1 * (dgate1 - mean_grad)
    lanes = lax.broadcasted_iota(jnp.int32, (TILE, 16), 1)
    dlog = jnp.where(lanes == e0 + ROUTER_AT, dc0, 0.0) + jnp.where(
        lanes == e1 + ROUTER_AT, dc1, 0.0
    )
    wide = lax.broadcasted_iota(jnp.int32, (TILE, 128), 1)
    dlog_ref[t] = (
        jnp.where(wide == e0 + router_lane, dc0, 0.0)
        + jnp.where(wide == e1 + router_lane, dc1, 0.0)
    ).astype(BF)
    return grad_rows + nn(dlog.astype(BF), router_block)


def query_places(t, sec, dims, along):
    local = lax.broadcasted_iota(jnp.int32, dims, along)
    return (512 * t + 128 * sec + local + (local & ~127)).astype(F32)


def allowed_rows(t, sec, ends_q, ends_k, causal):
    query_at = query_places(t, sec, (TILE, 1), 0)
    key_at = lax.broadcasted_iota(jnp.int32, (1, 1024), 1).astype(F32)
    allowed = segments(query_at, ends_q) == segments(key_at, ends_k)
    if causal:
        allowed = allowed & (key_at <= query_at)
    return allowed


def key_segments_t(ends_k, segk_ref):
    for j in range(8):
        at = lax.broadcasted_iota(jnp.int32, (128, TILE), 0).astype(F32) + 128.0 * j
        segk_ref[128 * j : 128 * j + 128, :] = segments(at, ends_k)


def allowed_cols(t, sec, ends_q, segk_ref, causal):
    query_at = query_places(t, sec, (1, TILE), 1)
    allowed = segk_ref[...] == segments(query_at, ends_q)
    if causal:
        key_at = lax.broadcasted_iota(jnp.int32, (1024, TILE), 0).astype(F32)
        allowed = allowed & (key_at <= query_at)
    return allowed


def fold_kv(grad_k, grad_v, sec, own_ref, send_ref):
    for j in range(4):
        k = grad_k[256 * j : 256 * j + 256, :]
        v = grad_v[256 * j : 256 * j + 256, :]
        k = k + pltpu.roll(k, 64, 1)
        v = v + pltpu.roll(v, 64, 1)
        low = lax.broadcasted_iota(jnp.int32, k.shape, 1) < 64
        both = jnp.where(low, k, v)
        first, second = both[0:128], both[128:256]
        own_ref[j] = jnp.where(sec == 0, first, second)
        send_ref[j] = jnp.where(sec == 0, second, first).astype(send_ref.dtype)


def split_halves(value, sec, keep_ref, send_ref, m, lane):
    upper, lower = value[0:256], value[256:512]
    cut = slice(lane, lane + value.shape[1])
    keep_ref[m, :, cut] = jnp.where(sec == 0, upper, lower).astype(BF)
    send_ref[m, :, cut] = jnp.where(sec == 0, lower, upper).astype(BF)


def split_flat(value, sec, keep_ref, send_ref, lane):
    upper, lower = value[0:256], value[256:512]
    cut = slice(lane, lane + value.shape[1])
    keep_ref[:, cut] = jnp.where(sec == 0, upper, lower).astype(BF)
    send_ref[:, cut] = jnp.where(sec == 0, lower, upper).astype(BF)


def turned_rows(value):
    return value.astype(F32).T.astype(BF)


def flat(ref):
    return ref[...].reshape(512, ref.shape[-1])


def attention_weight_grads(first_t, gated_ref, dz_ref, dq_ref, sec, keep_ref, send_ref):
    grad_q = nn(first_t, flat(dq_ref))
    grad_o = nn(turned_rows(flat(dz_ref)), flat(gated_ref))
    for b in range(4):
        cut = slice(128 * b, 128 * b + 128)
        split_halves(grad_q[:, cut], sec, keep_ref, send_ref, b, 0)
        split_halves(grad_o[:, cut], sec, keep_ref, send_ref, b, 128)


def gelu_parts(pre):
    cdf = 0.5 * (1.0 + lax.erf(pre * 0.7071067811865476))
    slope = cdf + pre * (jnp.exp(-0.5 * pre * pre) * 0.3989422804014327)
    return pre * cdf, slope


def own_self_kv(recv_ref, layer, sec, w_kv, kv_ref):
    gain = gain_of(recv_ref, layer, 0)
    for t in range(2):
        first = norm_of(rows_of(recv_ref, layer, t), gain)[0].astype(BF)
        kv = nn(first, w_kv).astype(BF)
        for i in range(2):
            j = 2 * t + i
            kv_ref[j, sec] = kv[128 * i : 128 * i + 128]
            kv_ref[j, 1 - sec] = other_kv(recv_ref, layer, j)


def cross_kv(kvm_ref, kvo_ref, sec, kv_s):
    for j in range(4):
        kv_s[j, sec] = kvm_ref[j]
        kv_s[j, 1 - sec] = kvo_ref[j]


def pack_kernel(ids_ref, len_ref, x_ref, gain_ref, w_kv_ref, own_ref, cross_ref, router_ref, *rest):
    sends, kv_s, extra_s = rest[:8], rest[8], rest[9]
    sec, m = ids_ref[0], ids_ref[1]
    gain = gain_ref[0:1, :].astype(F32)
    w_kv = w_kv_ref[...]
    for i in range(4):
        first = norm_of(x_ref[i].astype(F32), gain)[0].astype(BF)
        kv_s[i] = nn(first, w_kv).astype(BF).reshape(2, 128, 128)
    extra_s[...] = jnp.zeros_like(extra_s)
    extra_s[0:3, :] = gain_ref[...].astype(F32)
    extra_s[ROUTER_AT : ROUTER_AT + 8, :] = router_ref[...].astype(F32)
    lanes = lax.broadcasted_iota(jnp.int32, (1, 512), 1)
    for b in range(4):
        to = m ^ b
        row = jnp.zeros((1, 512), jnp.int32)
        for k in range(8):
            length = len_ref[to, k]
            row = jnp.where(lanes == k, length >> 5, row)
            row = jnp.where(lanes == 128 + k, length & 31, row)
        extra_s[LEN_ROW : LEN_ROW + 1, :] = row.astype(F32)
        own, cross = own_ref[to], cross_ref[to]
        own_code = (own[0:1] + 8 * own[1:2]).astype(F32)
        cross_code = (cross[0:1] + 8 * cross[1:2]).astype(F32)
        for a in range(2):
            half = sec ^ a
            ref = sends[4 * a + b]
            ref[0:128, :] = x_ref[to, pl.ds(pl.multiple_of(128 * half, 128), 128), :]
            far = kv_s[to, 1 - half]
            ref[128:160, :] = jnp.concatenate([far[32 * c : 32 * c + 32] for c in range(4)], 1)
            extra_s[CODE_ROW : CODE_ROW + 1, 0:128] = jnp.where(
                half == 0, own_code[:, 0:128], own_code[:, 128:256]
            )
            extra_s[CODE_ROW : CODE_ROW + 1, 128:256] = jnp.where(
                half == 0, cross_code[:, 0:128], cross_code[:, 128:256]
            )
            ref[EX_AT : EX_AT + 16, :] = extra_s[...].astype(BF)


def self_fwd_kernel(ids_ref, *refs):
    pieces, wa_own, wa_oth, kvw_own, kvw_oth = refs[:8], refs[8:12], refs[12:16], refs[16], refs[17]
    recv_ref, h1_ref, g1_ref, mixed_e, mixed_d, log_e, log_d = refs[18:25]
    wq, wo, wkv, kv_s, k2, v2, sems = refs[25:]
    sec, m = ids_ref[0], ids_ref[1]
    loads = Loads(sems)
    come = []
    for a in range(2):
        for b in range(4):
            at = 4 * (sec ^ a) + (m ^ b)
            come.append(loads.plain(pieces[4 * a + b], recv_ref.at[at]))
    kv_waits = [loads.start(sec == i, kvw_own, kvw_oth, wkv.at[i]) for i in range(2)]
    waits = []
    for layer in range(2):
        waits += loads.rows(sec == layer, wa_own, wa_oth, 0, wq.at[layer])
        waits += loads.rows(sec == layer, wa_own, wa_oth, 128, wo.at[layer])
    wait_all(come)
    wait_all(kv_waits)
    for layer in range(2):
        own_self_kv(recv_ref, layer, sec, wkv[layer], kv_s)
        widen_kv(kv_s, k2.at[layer], v2.at[layer])
    wait_all(waits)
    ends = [ends_of(extra_of(recv_ref, layer, 0).astype(F32)) for layer in range(2)]

    def tile(t, carry):
        for layer, after_ref, mixed_ref, log_ref in (
            (0, h1_ref, mixed_e, log_e),
            (1, g1_ref, mixed_d, log_d),
        ):
            rows = rows_of(recv_ref, layer, t)
            first = norm_of(rows, gain_of(recv_ref, layer, 0))[0].astype(BF)
            route = routing(
                first, extra_of(recv_ref, layer, 0), codes_of(recv_ref, layer, t, 0), m
            )
            allowed = allowed_rows(t, sec, ends[layer], ends[layer], layer == 1)
            out, mixed, row_log = attend_tile(
                first, route, wq[layer], wo[layer], k2[layer], v2[layer], allowed
            )
            after_ref[t] = rows + out
            mixed_ref[t] = mixed
            log_ref[t] = row_log
        return carry

    lax.fori_loop(0, 2, tile, 0)


def enc_ffn_kernel(recv_ref, h1_ref, kvc_ref, *refs):
    ids_ref, f_own, f_oth = refs[0], refs[1:5], refs[5:9]
    h2_ref, mem_ref, kvm_ref, w_in, w_out, third_s, sems = refs[9:]
    low = ids_ref[0] == 0
    loads = Loads(sems)
    waits = [
        (
            loads.start(low, f_own[b], f_oth[b], w_in.at[b]),
            loads.start(low, f_oth[b], f_own[b], w_out.at[b]),
        )
        for b in range(4)
    ]
    for t in range(2):
        h2_ref[t] = h1_ref[t]
        third_s[t] = norm_of(h1_ref[t], gain_of(recv_ref, 0, 2))[0].astype(BF)
    for pair in waits:
        wait_all(pair)

    def chunk(c, carry):
        pre = nn(flat(third_s), w_in[c])
        hidden = (0.5 * pre * (1.0 + lax.erf(pre * 0.7071067811865476))).astype(BF)
        h2_ref[...] += nn(hidden, w_out[c]).reshape(2, TILE, 512)
        return carry

    lax.fori_loop(0, 4, chunk, 0)
    for t in range(2):
        memory = norm_of(h2_ref[t], gain_of(recv_ref, 0, 1))[0].astype(BF)
        mem_ref[t] = memory
        kv = nn(memory, kvc_ref[...]).astype(BF)
        kvm_ref[2 * t] = kv[0:128]
        kvm_ref[2 * t + 1] = kv[128:256]


def cross_fwd_kernel(ids_ref, recv_ref, g1_ref, kvm_ref, kvo_ref, rc_ref, *refs):
    wa_own, wa_oth = refs[:4], refs[4:8]
    g2_ref, mixed_ref, log_ref, wq, wo, kv_s, k2, v2, sems = refs[8:]
    sec, m = ids_ref[0], ids_ref[1]
    loads = Loads(sems)
    waits = loads.rows(sec == 0, wa_own, wa_oth, 256, wq)
    waits += loads.rows(sec == 0, wa_oth, wa_own, 256, wo)
    cross_kv(kvm_ref, kvo_ref, sec, kv_s)
    widen_kv(kv_s, k2, v2)
    wait_all(waits)
    ends_k = ends_of(extra_of(recv_ref, 0, 0).astype(F32))
    ends_q = ends_of(extra_of(recv_ref, 1, 0).astype(F32))

    def tile(t, carry):
        before = g1_ref[t]
        second = norm_of(before, gain_of(recv_ref, 1, 1))[0].astype(BF)
        route = routing(second, rc_ref[...], codes_of(recv_ref, 1, t, 128), m)
        allowed = allowed_rows(t, sec, ends_q, ends_k, False)
        out, mixed, row_log = attend_tile(second, route, wq[...], wo[...], k2[...], v2[...], allowed)
        g2_ref[t] = before + out
        mixed_ref[t] = mixed
        log_ref[t] = row_log
        return carry

    lax.fori_loop(0, 2, tile, 0)


def ffn_both(c, third_s, third_t, dy_s, dy_t, w_in, w_out, dthird, sec, keep_ref, send_ref):
    pre = nn(flat(third_s), w_in[c])
    hidden, slope = gelu_parts(pre)
    hidden = hidden.astype(BF)
    dpre = (nt(flat(dy_s), w_out[c]) * slope).astype(BF)
    dthird[...] += nt(dpre, w_in[c])
    split_halves(nn(third_t[...], dpre), sec, keep_ref, send_ref, c, 0)
    split_halves(nn(dy_t[...], hidden), sec, keep_ref, send_ref, c, 512)
    return hidden


def dec_ffn_kernel(ids_ref, recv_ref, g2_ref, mem_ref, *refs):
    cots, f_own, f_oth = refs[:4], refs[4:8], refs[8:12]
    outs, dg2_ref, gain_ref, keep_ref, send_ref = refs[12:20], refs[20], refs[21], refs[22], refs[23]
    w_in, w_out, cot_s, third_s, third_t, cot_t, acc, dthird, sems = refs[24:]
    sec, m = ids_ref[0], ids_ref[1]
    low = sec == 0
    loads = Loads(sems)
    cot_waits = [loads.plain(cots[b], cot_s.at[m ^ b]) for b in range(4)]
    waits = loads.blocks(low, f_own, f_oth, w_in) + loads.blocks(low, f_oth, f_own, w_out)
    for t in range(2):
        acc[t] = g2_ref[t]
        third_s[t] = norm_of(g2_ref[t], gain_of(recv_ref, 1, 2))[0].astype(BF)
    third_t[...] = turned_rows(flat(third_s))
    wait_all(cot_waits)
    cot_t[...] = turned_rows(flat(cot_s))
    dthird[...] = jnp.zeros_like(dthird)
    wait_all(waits)

    def chunk(c, carry):
        hidden = ffn_both(
            c, third_s, third_t, cot_s, cot_t, w_in, w_out, dthird, sec, keep_ref, send_ref
        )
        acc[...] += nn(hidden, w_out[c]).reshape(2, TILE, 512)
        return carry

    lax.fori_loop(0, 4, chunk, 0)
    total = jnp.zeros((1, 512), F32)
    gain = gain_of(recv_ref, 1, 2)
    for t in range(2):
        unused_out, unit, scaled = norm_of(g2_ref[t], gain)
        back, gain_grad = norm_back(dthird[TILE * t : TILE * t + TILE, :], unit, scaled, gain)
        dg2_ref[t] = cot_s[2 * t : 2 * t + 2].reshape(TILE, 512).astype(F32) + back
        total = total + gain_grad
    gain_ref[...] = total
    for a in range(2):
        for b in range(4):
            t, i = (m ^ b) >> 1, (m ^ b) & 1
            cut = pl.ds(pl.multiple_of(128 * i, 128), 128)
            outs[4 * a + b][...] = jnp.where(
                (sec ^ a) == 0, mem_ref[t, cut, :].astype(F32), acc[t, cut, :]
            ).astype(BF)


def cross_back_kernel(
    ids_ref, recv_ref, g1_ref, dg2_ref, mixed_ref, log_ref, kvm_ref, kvo_ref, rc_ref, *refs
):
    wa_own, wa_oth = refs[:4], refs[4:8]
    dg1_ref, gain_ref, own_ref, send_ref, router_ref, keepw_ref, sendw_ref = refs[8:15]
    wq, wo, kv_s, k2, v2, segk, grad_k, grad_v, second_s, gated_s, dz_s, dq_s, dlog_s, sems = refs[15:]
    sec, m = ids_ref[0], ids_ref[1]
    loads = Loads(sems)
    waits = loads.rows(sec == 0, wa_own, wa_oth, 256, wq)
    waits += loads.rows(sec == 0, wa_oth, wa_own, 256, wo)
    cross_kv(kvm_ref, kvo_ref, sec, kv_s)
    widen_kv(kv_s, k2, v2)
    ends_k = ends_of(extra_of(recv_ref, 0, 0).astype(F32))
    ends_q = ends_of(extra_of(recv_ref, 1, 0).astype(F32))
    key_segments_t(ends_k, segk)
    grad_k[...] = jnp.zeros_like(grad_k)
    grad_v[...] = jnp.zeros_like(grad_v)
    wait_all(waits)

    def tile(t, total):
        gain = gain_of(recv_ref, 1, 1)
        second, unit, scaled = norm_of(g1_ref[t], gain)
        second = second.astype(BF)
        second_s[t] = second
        route = routing(second, rc_ref[...], codes_of(recv_ref, 1, t, 128), m)
        allowed = allowed_cols(t, sec, ends_q, segk, False)
        grad_rows = attend_back_tile(
            t, dg2_ref[t], second, route, mixed_ref[t], log_ref[t], wq[...], wo[...], rc_ref[...],
            ROUTER_LANES[2], k2[...], v2[...], allowed, grad_k, grad_v, gated_s, dz_s, dq_s, dlog_s,
        )
        back, gain_grad = norm_back(grad_rows, unit, scaled, gain)
        dg1_ref[t] = dg2_ref[t] + back
        return total + gain_grad

    gain_ref[...] = lax.fori_loop(0, 2, tile, jnp.zeros((1, 512), F32))
    fold_kv(grad_k, grad_v, sec, own_ref, send_ref)
    second_t = turned_rows(flat(second_s))
    router_ref[...] = nn(second_t, flat(dlog_s))
    attention_weight_grads(second_t, gated_s, dz_s, dq_s, sec, keepw_ref, sendw_ref)


def self_back_kernel(layer, ids_ref, recv_ref, up_ref, mixed_ref, log_ref, *refs):
    wa_own, wa_oth, kvw_own, kvw_oth = refs[:4], refs[4:8], refs[8], refs[9]
    dfirst_ref, own_ref, send_ref, router_ref, keepw_ref, sendw_ref = refs[10:16]
    wq, wo, wkv, kv_s, k2, v2, segk, grad_k, grad_v = refs[16:25]
    first_s, gated_s, dz_s, dq_s, dlog_s, sems = refs[25:]
    sec, m = ids_ref[0], ids_ref[1]
    mine = sec == layer
    loads = Loads(sems)
    kv_wait = loads.start(mine, kvw_own, kvw_oth, wkv)
    waits = loads.rows(mine, wa_own, wa_oth, 0, wq) + loads.rows(mine, wa_own, wa_oth, 128, wo)
    ends = ends_of(extra_of(recv_ref, layer, 0).astype(F32))
    key_segments_t(ends, segk)
    grad_k[...] = jnp.zeros_like(grad_k)
    grad_v[...] = jnp.zeros_like(grad_v)
    kv_wait()
    own_self_kv(recv_ref, layer, sec, wkv[...], kv_s)
    widen_kv(kv_s, k2, v2)
    wait_all(waits)
    router_block = extra_of(recv_ref, layer, 0)

    def tile(t, carry):
        first = norm_of(rows_of(recv_ref, layer, t), gain_of(recv_ref, layer, 0))[0].astype(BF)
        first_s[t] = first
        route = routing(first, router_block, codes_of(recv_ref, layer, t, 0), m)
        allowed = allowed_cols(t, sec, ends, segk, layer == 1)
        dfirst_ref[t] = attend_back_tile(
            t, up_ref[t], first, route, mixed_ref[t], log_ref[t], wq[...], wo[...], router_block,
            ROUTER_LANES[layer], k2[...], v2[...], allowed, grad_k, grad_v, gated_s, dz_s, dq_s,
            dlog_s,
        )
        return carry

    lax.fori_loop(0, 2, tile, 0)
    fold_kv(grad_k, grad_v, sec, own_ref, send_ref)
    first_t = turned_rows(flat(first_s))
    router_ref[...] = nn(first_t, flat(dlog_s))
    attention_weight_grads(first_t, gated_s, dz_s, dq_s, sec, keepw_ref, sendw_ref)


def enc_ffn_back_kernel(ids_ref, recv_ref, h1_ref, h2_ref, own_ref, come_ref, kvc_ref, *refs):
    f_own, f_oth = refs[:4], refs[4:8]
    dh1_ref, gain_ref, gain2_ref, keep_ref, send_ref = refs[8:13]
    w_in, w_out, third_s, third_t, dy_s, dy_t, dthird, sems = refs[13:]
    sec = ids_ref[0]
    low = sec == 0
    loads = Loads(sems)
    waits = loads.blocks(low, f_own, f_oth, w_in) + loads.blocks(low, f_oth, f_own, w_out)
    total = jnp.zeros((1, 512), F32)
    gain = gain_of(recv_ref, 0, 1)
    for t in range(2):
        dkv = (own_ref[2 * t : 2 * t + 2] + come_ref[2 * t : 2 * t + 2].astype(F32)).astype(BF)
        dmem = rounded(nt(dkv.reshape(TILE, 128), kvc_ref[...]))
        unused_out, unit, scaled = norm_of(h2_ref[t], gain)
        back, gain_grad = norm_back(dmem, unit, scaled, gain)
        dh1_ref[t] = back
        dy_s[t] = back.astype(BF)
        third_s[t] = norm_of(h1_ref[t], gain_of(recv_ref, 0, 2))[0].astype(BF)
        total = total + gain_grad
    gain_ref[...] = total
    third_t[...] = turned_rows(flat(third_s))
    dy_t[...] = turned_rows(flat(dy_s))
    dthird[...] = jnp.zeros_like(dthird)
    wait_all(waits)

    def chunk(c, carry):
        ffn_both(c, third_s, third_t, dy_s, dy_t, w_in, w_out, dthird, sec, keep_ref, send_ref)
        return carry

    lax.fori_loop(0, 4, chunk, 0)
    total = jnp.zeros((1, 512), F32)
    gain = gain_of(recv_ref, 0, 2)
    for t in range(2):
        unused_out, unit, scaled = norm_of(h1_ref[t], gain)
        back, gain_grad = norm_back(dthird[TILE * t : TILE * t + TILE, :], unit, scaled, gain)
        dh1_ref[t] += back
        total = total + gain_grad
    gain2_ref[...] = total


def finish_rows(layer, recv_ref, up_ref, df_ref, own_ref, come_ref, wkv, first_s, dx_s):
    total = jnp.zeros((1, 512), F32)
    gain = gain_of(recv_ref, layer, 0)
    dkvs = []
    for t in range(2):
        first, unit, scaled = norm_of(rows_of(recv_ref, layer, t), gain)
        first_s[t] = first.astype(BF)
        dkv = (own_ref[2 * t : 2 * t + 2] + come_ref[2 * t : 2 * t + 2].astype(F32)).astype(BF)
        dkv = dkv.reshape(TILE, 128)
        dkvs.append(dkv)
        back, gain_grad = norm_back(df_ref[t] + nt(dkv, wkv), unit, scaled, gain)
        dx_s[t] = (up_ref[t] + back).astype(BF)
        total = total + gain_grad
    grad = nn(turned_rows(flat(first_s)), jnp.concatenate(dkvs, 0))
    return total, grad


def dec_finish_kernel(
    ids_ref, recv_ref, up_ref, df_ref, own_ref, come_ref, own_c, come_c, mem_ref, kvw_own, kvw_oth,
    dx_ref, gain_ref, keep_ref, send_ref,
    wkv, first_s, sems,
):
    sec = ids_ref[0]
    wait = Loads(sems).start(sec == 1, kvw_own, kvw_oth, wkv)
    dkv_c = (own_c[...] + come_c[...].astype(F32)).astype(BF).reshape(512, 128)
    split_flat(nn(turned_rows(flat(mem_ref)), dkv_c), sec, keep_ref, send_ref, 128)
    wait()
    gain_ref[...], grad = finish_rows(
        1, recv_ref, up_ref, df_ref, own_ref, come_ref, wkv[...], first_s, dx_ref
    )
    split_flat(grad, sec, keep_ref, send_ref, 0)


def enc_finish_kernel(
    ids_ref, recv_ref, up_ref, df_ref, own_ref, come_ref, dx1_ref, r0, r1, rc,
    gain_e1, gain_e2, gain_d0, gain_d1, gain_d2, kvw_own, kvw_oth, *refs
):
    outs, keep_ref, send_ref, wkv, first_s, dx_s, sems = refs[:8], *refs[8:]
    sec, m = ids_ref[0], ids_ref[1]
    Loads(sems).start(sec == 0, kvw_own, kvw_oth, wkv)()
    gain_e0, grad = finish_rows(
        0, recv_ref, up_ref, df_ref, own_ref, come_ref, wkv[...], first_s, dx_s
    )
    split_flat(grad, sec, keep_ref, send_ref, 0)
    for a in range(2):
        for b in range(4):
            t, i = (m ^ b) >> 1, (m ^ b) & 1
            cut = pl.ds(pl.multiple_of(128 * i, 128), 128)
            outs[4 * a + b][...] = jnp.where(
                (sec ^ a) == 0, dx_s[t, cut, :].astype(F32), dx1_ref[t, cut, :].astype(F32)
            ).astype(BF)
    gains = (gain_e0, gain_e1[...], gain_e2[...], gain_d0[...], gain_d1[...], gain_d2[...])
    lanes = lax.broadcasted_iota(jnp.int32, (128, 128), 1)
    blocks = []
    for b in range(4):
        cut = slice(128 * b, 128 * b + 128)
        misc = r0[cut, :] + r1[cut, :] + rc[cut, :]
        for i, row in enumerate(gains):
            misc = misc + jnp.where(lanes == GAIN_LANE + i, row_to_col(row[:, cut]), 0.0)
        blocks.append(misc)
    for b in range(2):
        cut = slice(128 * b, 128 * b + 128)
        keep_ref[cut, 128:256] = jnp.where(sec == 0, blocks[b], blocks[b + 2]).astype(BF)
        send_ref[cut, 128:256] = jnp.where(sec == 0, blocks[b + 2], blocks[b]).astype(BF)


def add_kernel(counts, *refs):
    n = len(counts)
    keeps, comes, outs = refs[:n], refs[n : 2 * n], refs[2 * n :]
    for b in range(4):
        lane = 0
        for keep, come, (pieces, width) in zip(keeps, comes, counts):
            left = keep[b] if pieces == 4 else keep[...]
            right = come[b] if pieces == 4 else come[...]
            outs[b][:, lane : lane + width] = (left.astype(F32) + right.astype(F32)).astype(BF)
            lane += width


def sum_kernel(ids_ref, *refs):
    groups = (len(refs) - 4) // 4
    outs = refs[4 * groups :]
    rows = outs[0].shape[0]
    d = ids_ref[2]
    for k in range(4):
        cut = pl.ds(pl.multiple_of((d ^ k) * rows, rows), rows)
        lane = 0
        for g in range(groups):
            parts = refs[4 * g : 4 * g + 4]
            total = parts[0][cut, :].astype(F32)
            for part in parts[1:]:
                total = total + part[cut, :].astype(F32)
            width = parts[0].shape[1]
            outs[k][:, lane : lane + width] = total.astype(BF)
            lane += width


def place_kernel(ids_ref, *refs):
    pieces, out_ref, buf, sems = refs[:8], refs[8], refs[9], refs[10]
    sec, m = ids_ref[0], ids_ref[1]
    loads = Loads(sems)
    waits = [loads.plain(pieces[i], buf.at[i]) for i in range(8)]
    wait_all(waits)
    for a in range(2):
        for b in range(4):
            out_ref[m ^ b, sec ^ a] = buf[4 * a + b].astype(out_ref.dtype)


def shaped(dims, kind):
    return jax.ShapeDtypeStruct(dims, kind)


def run(kernel, args, places, outs, scratch, flops):
    space = {
        "s": pl.BlockSpec(memory_space=pltpu.SMEM),
        "v": pl.BlockSpec(memory_space=pltpu.VMEM),
        "a": pl.BlockSpec(memory_space=pl.ANY),
    }
    return pl.pallas_call(
        kernel,
        out_shape=outs,
        in_specs=[space[p] for p in places],
        out_specs=jax.tree.map(lambda _: space["v"], outs),
        scratch_shapes=scratch,
        compiler_params=pltpu.CompilerParams(vmem_limit_bytes=VMEM_LIMIT),
        cost_estimate=pl.CostEstimate(flops=flops, bytes_accessed=8 << 20, transcendentals=0),
    )(*args)


def vm(*dims, kind=BF):
    return pltpu.VMEM(dims, kind)


def dma(count):
    return pltpu.SemaphoreType.DMA((count,))


def across(value, axes, size, by):
    return lax.ppermute(value, axes, [(i, i ^ by) for i in range(size)])


def swapped(value):
    return across(value, "section", 2, 1)


def group_exchange(pieces):
    return [pieces[0]] + [across(pieces[i], ("section", "mp"), 8, i) for i in range(1, 8)]


def mp_exchange(pieces):
    return [pieces[0]] + [across(pieces[b], "mp", 4, b) for b in range(1, 4)]


def gathered(value):
    return mp_exchange([value] * 4)


def dp_sum(pieces):
    come = [pieces[0]] + [across(pieces[k], "dp", 4, k) for k in range(1, 4)]
    total = come[0].astype(F32)
    for piece in come[1:]:
        total = total + piece.astype(F32)
    return total


def add_shares(keeps, comes):
    counts = tuple((4 if k.ndim == 3 else 1, k.shape[-1]) for k in keeps)
    width = sum(c[1] for c in counts)
    return run(
        functools.partial(add_kernel, counts),
        (*keeps, *comes),
        "v" * (2 * len(keeps)),
        [shaped((256, width), BF)] * 4,
        [],
        10**8,
    )


def sum_over_rows(ids, groups):
    dp = lax.axis_size("dp")
    width = sum(g[0].shape[1] for g in groups)
    if dp == 4:
        args = [piece for g in groups for piece in g]
        pieces = run(
            sum_kernel,
            (ids, *args),
            "s" + "v" * len(args),
            [shaped((64, width), BF)] * 4,
            [],
            10**8,
        )
        return dp_sum(pieces)
    totals = []
    for group in groups:
        total = group[0].astype(F32)
        for piece in group[1:]:
            total = total + piece.astype(F32)
        totals.append(total)
    quarter = jnp.concatenate(totals, 1).astype(BF).reshape(dp, 256 // dp, width)
    come = lax.all_to_all(quarter, "dp", split_axis=0, concat_axis=0, tiled=True)
    return jnp.sum(come.astype(F32), 0)


def per_device(
    inputs,
    lengths,
    routes_self,
    routes_cross,
    gains,
    router_self,
    query_self,
    keyval_self,
    output_self,
    ffn_in,
    ffn_out,
    router_cross,
    query_cross,
    keyval_cross,
    output_cross,
    cotangent,
):
    sec, m, d = lax.axis_index("section"), lax.axis_index("mp"), lax.axis_index("dp")
    low = sec == 0
    ids = jnp.stack([sec, m, d]).astype(jnp.int32)
    sem = dma(40)

    q_rows = query_self[0].transpose(0, 2, 1).reshape(128, 512)
    o_rows = output_self[0].reshape(128, 512)
    c_rows = jnp.where(
        low, query_cross.transpose(0, 2, 1).reshape(128, 512), output_cross.reshape(128, 512)
    )
    wa_own = gathered(jnp.concatenate([q_rows, o_rows, c_rows], 0))
    kvw_own = keyval_self[0]
    kvw_oth = swapped(kvw_own)
    router_c = jnp.concatenate([jnp.zeros((8, 512), BF), router_cross.T], 0)

    packed = run(
        pack_kernel,
        (
            ids,
            lengths[0, :, 0],
            inputs[0, :, 0],
            gains[0],
            keyval_self[0],
            routes_self[0, :, 0].transpose(0, 2, 1),
            routes_cross[:, 0].transpose(0, 2, 1),
            router_self[0].T,
        ),
        "ssvvvvvv",
        [shaped((176, 512), BF)] * 8,
        [vm(4, 2, 128, 128), vm(16, 512, kind=F32)],
        10**9,
    )
    pieces = group_exchange(packed)
    wa_oth = [swapped(piece) for piece in wa_own]

    w_in, w_out = ffn_in[0], ffn_out[0]
    half_come = swapped(jnp.where(low, w_out, w_in))
    enc_own = gathered(jnp.where(low, w_in, half_come))
    enc_oth = [swapped(piece) for piece in enc_own]
    dec_own = gathered(jnp.where(low, half_come, w_out))
    dec_oth = [swapped(piece) for piece in dec_own]
    cot_cut = cotangent[:, 0].reshape(4, 2, 128, 512)
    cots = mp_exchange([cot_cut[m ^ b, sec] for b in range(4)])

    act = shaped((2, TILE, 512), F32)
    actb = shaped((2, TILE, 512), BF)
    mixed_s = shaped((2, 2 * TILE, 128), F32)
    log_s = shaped((2, 1, 2 * TILE), F32)
    kv_b = shaped((4, 128, 128), BF)
    kv_f = shaped((4, 128, 128), F32)
    row_s = shaped((1, 512), F32)
    ffn_g = shaped((4, 256, 1024), BF)
    att_g = shaped((4, 256, 256), BF)
    flat_g = shaped((256, 256), BF)
    lane_s = shaped((512, 128), F32)
    wide = [vm(512, 512), vm(512, 512)]
    kv_scratch = [vm(4, 2, 128, 128), vm(1024, 128), vm(1024, 128)]
    back_scratch = [
        vm(1024, TILE, kind=F32), vm(1024, 128, kind=F32), vm(1024, 128, kind=F32),
        vm(2, TILE, 512), vm(2, TILE, 512), vm(2, TILE, 512), vm(2, TILE, 512), vm(2, TILE, 128),
    ]
    ffn_w = [vm(4, 512, 512), vm(4, 512, 512)]

    recv, h1, g1, mixed_e, mixed_d, log_e, log_d = run(
        self_fwd_kernel,
        (ids, *pieces, *wa_own, *wa_oth, kvw_own, kvw_oth),
        "s" + "a" * 18,
        (shaped((8, 176, 512), BF), act, act, mixed_s, mixed_s, log_s, log_s),
        [vm(2, 512, 512), vm(2, 512, 512), vm(2, 512, 128), vm(4, 2, 128, 128)]
        + [vm(2, 1024, 128), vm(2, 1024, 128), sem],
        4 * 10**9,
    )
    h2, memory, kvm = run(
        enc_ffn_kernel,
        (recv, h1, keyval_cross, ids, *enc_own, *enc_oth),
        "vvvs" + "a" * 8,
        (act, actb, kv_b),
        ffn_w + [vm(2, TILE, 512), sem],
        4 * 10**9,
    )
    kvm_oth = swapped(kvm)
    g2, mixed_c, log_c = run(
        cross_fwd_kernel,
        (ids, recv, g1, kvm, kvm_oth, router_c, *wa_own, *wa_oth),
        "svvvvv" + "a" * 8,
        (act, mixed_s, log_s),
        wide + kv_scratch + [sem],
        2 * 10**9,
    )
    dec_ffn = run(
        dec_ffn_kernel,
        (ids, recv, g2, memory, *cots, *dec_own, *dec_oth),
        "svvv" + "a" * 12,
        [shaped((128, 512), BF)] * 8 + [act, row_s, ffn_g, ffn_g],
        ffn_w
        + [vm(4, 128, 512), vm(2, TILE, 512), vm(512, 512), vm(512, 512)]
        + [vm(2, TILE, 512, kind=F32), vm(512, 512, kind=F32), sem],
        12 * 10**9,
    )
    out_pieces, (dg2, gain_d2, keep_d, send_d) = dec_ffn[:8], dec_ffn[8:]
    come_d = swapped(send_d)
    outs_come = group_exchange(out_pieces)
    dg1, gain_d1, own_c, sendkv_c, router_cg, keep_wc, send_wc = run(
        cross_back_kernel,
        (ids, recv, g1, dg2, mixed_c, log_c, kvm, kvm_oth, router_c, *wa_own, *wa_oth),
        "svvvvvvvv" + "a" * 8,
        (act, row_s, kv_f, kv_b, lane_s, att_g, att_g),
        wide + kv_scratch + back_scratch + [sem],
        4 * 10**9,
    )
    comekv_c = swapped(sendkv_c)
    come_wc = swapped(send_wc)
    ffn_d_parts = mp_exchange(add_shares([keep_d], [come_d]))
    self_scratch = wide + [vm(512, 128)] + kv_scratch + back_scratch + [sem]
    self_outs = (act, kv_f, kv_b, lane_s, att_g, att_g)
    df1, own_1, sendkv_1, router_1g, keep_w1, send_w1 = run(
        functools.partial(self_back_kernel, 1),
        (ids, recv, dg1, mixed_d, log_d, *wa_own, *wa_oth, kvw_own, kvw_oth),
        "svvvv" + "a" * 10,
        self_outs,
        self_scratch,
        4 * 10**9,
    )
    comekv_1 = swapped(sendkv_1)
    come_w1 = swapped(send_w1)
    dh1, gain_e1, gain_e2, keep_e, send_e = run(
        enc_ffn_back_kernel,
        (ids, recv, h1, h2, own_c, comekv_c, keyval_cross, *enc_own, *enc_oth),
        "svvvvvv" + "a" * 8,
        (act, row_s, row_s, ffn_g, ffn_g),
        ffn_w
        + [vm(2, TILE, 512), vm(512, 512), vm(2, TILE, 512), vm(512, 512)]
        + [vm(512, 512, kind=F32), sem],
        12 * 10**9,
    )
    come_e = swapped(send_e)
    dx1, gain_d0, keep_s1, send_s1 = run(
        dec_finish_kernel,
        (ids, recv, dg1, df1, own_1, comekv_1, own_c, comekv_c, memory, kvw_own, kvw_oth),
        "svvvvvvvvaa",
        (actb, row_s, flat_g, flat_g),
        [vm(512, 128), vm(2, TILE, 512), sem],
        10**9,
    )
    come_s1 = swapped(send_s1)
    df0, own_0, sendkv_0, router_0g, keep_w0, send_w0 = run(
        functools.partial(self_back_kernel, 0),
        (ids, recv, dh1, mixed_e, log_e, *wa_own, *wa_oth, kvw_own, kvw_oth),
        "svvvv" + "a" * 10,
        self_outs,
        self_scratch,
        4 * 10**9,
    )
    comekv_0 = swapped(sendkv_0)
    come_w0 = swapped(send_w0)
    ffn_e_parts = mp_exchange(add_shares([keep_e], [come_e]))
    att_d_parts = mp_exchange(
        add_shares([keep_wc, keep_w1, keep_s1], [come_wc, come_w1, come_s1])
    )
    finish = run(
        enc_finish_kernel,
        (
            ids, recv, dh1, df0, own_0, comekv_0, dx1, router_0g, router_1g, router_cg,
            gain_e1, gain_e2, gain_d0, gain_d1, gain_d2, kvw_own, kvw_oth,
        ),
        "s" + "v" * 14 + "aa",
        [shaped((128, 512), BF)] * 8 + [flat_g, flat_g],
        [vm(512, 128), vm(2, TILE, 512), vm(2, TILE, 512), sem],
        10**9,
    )
    dx_pieces, (keep_s0, send_s0) = finish[:8], finish[8:]
    come_s0 = swapped(send_s0)
    dx_come = group_exchange(dx_pieces)
    att_e_parts = mp_exchange(add_shares([keep_w0, keep_s0], [come_w0, come_s0]))

    ffn_dec = sum_over_rows(ids, [ffn_d_parts])
    att_dec = sum_over_rows(ids, [att_d_parts])
    ffn_enc = sum_over_rows(ids, [ffn_e_parts])
    att_enc = sum_over_rows(ids, [att_e_parts])

    def placed(come, kind):
        whole = run(
            place_kernel,
            (ids, *come),
            "s" + "a" * 8,
            shaped((4, 2, 128, 512), kind),
            [vm(8, 128, 512), dma(8)],
            10**8,
        )
        return whole.reshape(1, 4, 1, 256, 512)

    share = att_enc.shape[0]

    def query_of(value, at):
        return value[:, at : at + 128].reshape(share, 2, 64).transpose(1, 0, 2)

    def output_of(value, at):
        return value[:, at : at + 128].T.reshape(2, 64, share)

    misc = att_enc[:, 384:512]

    def router_of(layer):
        return misc[:, ROUTER_LANES[layer] : ROUTER_LANES[layer] + 8]

    return (
        placed(outs_come, BF),
        placed(dx_come, F32),
        misc[:, GAIN_LANE : GAIN_LANE + 6].T.reshape(2, 3, share),
        jnp.stack([router_of(0), router_of(1)]),
        jnp.stack([query_of(att_enc, 0), query_of(att_dec, 256)]),
        jnp.stack([att_enc[:, 256:384], att_dec[:, 512:640]]),
        jnp.stack([output_of(att_enc, 128), output_of(att_dec, 384)]),
        jnp.stack([ffn_enc[:, :512], ffn_dec[:, :512]]),
        jnp.stack([ffn_enc[:, 512:].T, ffn_dec[:, 512:].T]),
        router_of(2),
        query_of(att_dec, 0),
        att_dec[:, 640:768],
        output_of(att_dec, 128),
    )


def solution(mesh):
    placed = (
        P("section", None, "dp", "mp", None),
        P("section", None, "dp", None),
        P("section", None, "dp", "mp", None),
        P(None, "dp", "mp", None),
        P("section", None, None),
        P("section", None, None),
        P("section", "mp", None, None),
        P("section", None, None),
        P("section", "mp", None, None),
        P("section", None, "mp"),
        P("section", "mp", None),
        P(),
        P("mp", None, None),
        P(),
        P("mp", None, None),
        P(None, "dp", "mp", None),
    )
    return jax.shard_map(
        per_device,
        mesh=mesh,
        in_specs=placed,
        out_specs=(
            P("section", None, "dp", "mp", None),
            P("section", None, "dp", "mp", None),
            P(None, None, ("section", "dp")),
            P(None, ("section", "dp"), None),
            P(None, "mp", ("section", "dp"), None),
            P(None, ("section", "dp"), None),
            P(None, "mp", None, ("section", "dp")),
            P(None, ("section", "dp"), "mp"),
            P(None, "mp", ("section", "dp")),
            P(("section", "dp"), None),
            P("mp", ("section", "dp"), None),
            P(("section", "dp"), None),
            P("mp", None, ("section", "dp")),
        ),
        check_vma=False,
    )
```

time: 416 us -> 379 us (0.911)
  waiting for transfers between devices: 167 us -> 132 us
  Pallas kernels: 108 us -> 142 us
  blocking collectives: 28.3 us -> 0 us
  starting transfers between devices: 53.3 us -> 77.6 us
  other arithmetic: 30.5 us -> 6.32 us
  local copies, waits for them, and re-layouts: 25.9 us -> 14 us
    all_to_all x12 -> x0, waiting for transfers between devices: 164 us -> none  [to_all(): return lax.all_to_all(value, axes, split_axis=0, concat_axis=0, tiled=True)]
    ppermute x12 -> x82, waiting for transfers between devices: 3.11 us -> 132 us  [across(): return lax.ppermute(value, axes, [(i, i ^ by) for i in range(size)])]
    ppermute x12 -> x82, starting transfers between devices: 3.95 us -> 77.6 us  [across(): return lax.ppermute(value, axes, [(i, i ^ by) for i in range(size)])]
    all_to_all x12 -> x0, starting transfers between devices: 49.4 us -> none  [to_all(): return lax.all_to_all(value, axes, split_axis=0, concat_axis=0, tiled=True)]
    pallas_call x9 -> x21, Pallas kernels: 108 us -> 142 us  [run(): pl.pallas_call(kernel, out_shape=outs, in_specs=[space[p] for p in places...]
    all_to_all x1 -> x0, blocking collectives: 28.3 us -> none  [to_all(): return lax.all_to_all(value, axes, split_axis=0, concat_axis=0, tiled=True)]
    convert_element_type x3 -> x0, other arithmetic: 9.83 us -> none  [the longest x2 7.8 us: scattered(): summed = (kept.astype(F32) + come.astype(F32)).astype(BF)]
    reduce_sum x6 -> x0, other arithmetic: 8.56 us -> none  [the longest x3 7.25 us: last_stages(): quarter = jnp.sum(parts.astype(F32), 0).astype(BF)]
  transfers between devices with their start and end apart: 24 -> 82, of which waited for: 12 -> 24; matrix products, arithmetic and copies ran while one was open for 9% -> 3% of each run, Pallas kernels for 18% -> 34%
where the time goes in v2:
time: 379 us; the launch traced here: 374 us
  Pallas kernels  142 us (37%)
  waiting for transfers between devices  132 us (35%)
  starting transfers between devices  77.6 us (20%)
  local copies, waits for them, and re-layouts  14 us (4%)
  other arithmetic  6.32 us (2%)
    pallas_call x21, Pallas kernels, run(): pl.pallas_call(kernel, out_shape=outs, in_specs=[space[p] for p in places...  142 us
    ppermute x82, waiting for transfers between devices, across(): return lax.ppermute(value, axes, [(i, i ^ by) for i in range(size)])  132 us
    ppermute x82, starting transfers between devices, across(): return lax.ppermute(value, axes, [(i, i ^ by) for i in range(size)])  77.6 us
    unnamed x177, local copies, waits for them, and re-layouts  9.44 us
  transfers between devices with their start and end apart: 82, of which 24 were waited for; matrix products, arithmetic and copies ran while one was open for 3% of the time, Pallas kernels for 34%

profile of v2, /device:TPU:0, one launch (start us, length us, event | category | flops | bytes accessed | tf_op | source)
XLA Modules:
  0.0 374.1 jit_solution(6217570171595532248)
XLA Ops:
  18.1 11.9 %collective-permute-done.1.refs_2_ = bf16[176,512]{1,0:T(8,128)(2,1)S(1)} collective-permute-done((bf16[176,512]{1,0:T(8,128)(2,1)}, bf16[176,512]{1,0:T(8,128)(2,1)S(1)}, u32[]{:S(2)}, u32[]{:S(2)}) %collective-permute-start.1) | collective-permute-done | bytes 180256 | tf_op jit(solution)/shard_map/ppermute | solution.py:825
  32.0 10.9 %collective-permute-done.4.refs_5_ = bf16[176,512]{1,0:T(8,128)(2,1)S(1)} collective-permute-done((bf16[176,512]{1,0:T(8,128)(2,1)S(1)}, bf16[176,512]{1,0:T(8,128)(2,1)S(1)}, u32[]{:S(2)}, u32[]{:S(2)}) %collective-permute-start.4) | collective-permute-done | bytes 180256 | tf_op jit(solution)/shard_map/ppermute | solution.py:825
  44.7 4.5 %collective-permute-done.5.refs_6_ = bf16[176,512]{1,0:T(8,128)(2,1)S(1)} collective-permute-done((bf16[176,512]{1,0:T(8,128)(2,1)S(1)}, bf16[176,512]{1,0:T(8,128)(2,1)S(1)}, u32[]{:S(2)}, u32[]{:S(2)}) %collective-permute-start.5) | collective-permute-done | bytes 180256 | tf_op jit(solution)/shard_map/ppermute | solution.py:825
  52.2 6.1 %collective-permute-done.6.refs_7_ = bf16[176,512]{1,0:T(8,128)(2,1)S(1)} collective-permute-done((bf16[176,512]{1,0:T(8,128)(2,1)S(1)}, bf16[176,512]{1,0:T(8,128)(2,1)S(1)}, u32[]{:S(2)}, u32[]{:S(2)}) %collective-permute-start.6) | collective-permute-done | bytes 180256 | tf_op jit(solution)/shard_map/ppermute | solution.py:825
  65.2 8.9 %collective-permute-done.29.refs_7_ = bf16[512,512]{1,0:T(8,128)(2,1)S(1)} collective-permute-done((bf16[512,512]{1,0:T(8,128)(2,1)S(1)}, bf16[512,512]{1,0:T(8,128)(2,1)S(1)}, u32[]{:S(2)}, u32[]{:S(2)}) %collective-permute-start.29) | collective-permute-done | bytes 524320 | tf_op jit(solution)/shard_map/ppermute | solution.py:825
  75.8 19.9 %collective-permute-done.28.refs_6_ = bf16[512,512]{1,0:T(8,128)(2,1)S(1)} collective-permute-done((bf16[512,512]{1,0:T(8,128)(2,1)S(1)}, bf16[512,512]{1,0:T(8,128)(2,1)S(1)}, u32[]{:S(2)}, u32[]{:S(2)}) %collective-permute-start.28) | collective-permute-done | bytes 524320 | tf_op jit(solution)/shard_map/ppermute | solution.py:825
  96.3 10.6 %collective-permute-done.17.refs_3_.refs_2_ = bf16[512,512]{1,0:T(8,128)(2,1)S(1)} collective-permute-done((bf16[512,512]{1,0:T(8,128)(2,1)S(1)}, bf16[512,512]{1,0:T(8,128)(2,1)S(1)}, u32[]{:S(2)}, u32[]{:S(2)}) %collective-permute-start.17) | collective-permute-done | bytes 524320 | tf_op jit(solution)/shard_map/ppermute | solution.py:825
  107.4 13.7 %shard_map.256 = (bf16[8,176,512]{2,1,0:T(8,128)(2,1)}, f32[2,256,512]{2,1,0:T(8,128)}, f32[2,256,512]{2,1,0:T(8,128)}, f32[2,512,128]{2,1,0:T(8,128)}, f32[2,51...) custom-call(s32[3]{0:T(128)} %pad_add_fusion.ids_ref.refs_0_, ...), custom_call_target="tpu_custom_call" | custom-call | flops 4000000000 | bytes 8388608 | tf_op jit(solution)/shard_map/pallas_call | solution.py:805
  124.5 8.5 %shard_map.257 = (f32[2,256,512]{2,1,0:T(8,128)}, bf16[2,256,512]{2,1,0:T(8,128)(2,1)}, bf16[4,128,128]{2,1,0:T(8,128)(2,1)}) custom-call(bf16[8,176,512]{2,1,0:T(8,128)(2,1)} %get-tuple-element.124.recv_ref, f32[2,256,512]{2,1,0:T(8,128)} %get-tuple-element.126.h1_ref, bf16[512,128]{1,0:T(8,128)(2,1)} %kvc_ref.3, s32[3]{0:T(128)} %pad_add_fusion.ids_ref.refs_0_, ...), custom_call_target="tpu_custom_call" | custom-call | flops 4000000000 | bytes 8388608 | tf_op jit(solution)/shard_map/pallas_call | solution.py:805
  135.3 9.2 %shard_map.258 = (f32[2,256,512]{2,1,0:T(8,128)}, f32[2,512,128]{2,1,0:T(8,128)}, f32[2,1,512]{2,1,0:T(1,128)}) custom-call(s32[3]{0:T(128)} %pad_add_fusion.ids_ref.refs_0_, bf16[8,176,512]{2,1,0:T(8,128)(2,1)} %get-tuple-element.124.recv_ref, f32[2,256,512]{2,1,0:T(8,128)} %get-tuple-element.125.g1_ref, bf16[4,128,128]{2,1,0:T(8,128)(2,1)} %get-tuple-element.127.kvm_ref, ...), custom_call_target="tpu_custom_call" | custom-call | flops 2000000000 | bytes 8388608 | tf_op jit(solution)/shard_map/pallas_call | solution.py:805
  145.9 15.8 %shard_map.259 = (bf16[128,512]{1,0:T(8,128)(2,1)}, bf16[128,512]{1,0:T(8,128)(2,1)}, bf16[128,512]{1,0:T(8,128)(2,1)}, bf16[128,512]{1,0:T(8,128)(2,1)}, bf16[1...) custom-call(s32[3]{0:T(128)} %pad_add_fusion.ids_ref.refs_0_, ...), custom_call_target="tpu_custom_call" | custom-call | flops 12000000000 | bytes 8388608 | tf_op jit(solution)/shard_map/pallas_call | solution.py:805
  165.2 13.0 %shard_map.261 = (f32[2,256,512]{2,1,0:T(8,128)}, f32[1,512]{1,0:T(1,128)}, f32[4,128,128]{2,1,0:T(8,128)}, bf16[4,128,128]{2,1,0:T(8,128)(2,1)}, f32[512,128]{1...) custom-call(s32[3]{0:T(128)} %pad_add_fusion.ids_ref.refs_0_, ...), custom_call_target="tpu_custom_call" | custom-call | flops 4000000000 | bytes 8388608 | tf_op jit(solution)/shard_map/pallas_call | solution.py:805
  178.9 12.5 %shard_map.264 = (f32[2,256,512]{2,1,0:T(8,128)}, f32[4,128,128]{2,1,0:T(8,128)}, bf16[4,128,128]{2,1,0:T(8,128)(2,1)}, f32[512,128]{1,0:T(8,128)}, bf16[4,256,2...) custom-call(s32[3]{0:T(128)} %pad_add_fusion.ids_ref.refs_0_, bf16[8,176,512]{2,1,0:T(8,128)(2,1)} %get-tuple-element.124.recv_ref, ...), custom_call_target="tpu_custom_call" | custom-call | flops 4000000000 | bytes 8388608 | tf_op jit(solution)/shard_map/pallas_call | solution.py:805
  192.1 13.6 %shard_map.262 = (f32[2,256,512]{2,1,0:T(8,128)}, f32[1,512]{1,0:T(1,128)}, f32[1,512]{1,0:T(1,128)}, bf16[4,256,1024]{2,1,0:T(8,128)(2,1)}, bf16[4,256,1024]{2,1,0:T(8,128)(2,1)}) custom-call(s32[3]{0:T(128)} %pad_add_fusion.ids_ref.refs_0_, bf16[8,176,512]{2,1,0:T(8,128)(2,1)} %get-tuple-element.124.recv_ref, f32[2,256,512]{2,1,0:T(8,128)} %get-tuple-element.126.h1_ref, ...), custom_call_target="tpu_custom_call" | custom-call | flops 12000000000 | bytes 8388608 | tf_op jit(solution)/shard_map/pallas_call | solution.py:805
  205.7 12.3 %shard_map.263 = (f32[2,256,512]{2,1,0:T(8,128)}, f32[4,128,128]{2,1,0:T(8,128)}, bf16[4,128,128]{2,1,0:T(8,128)(2,1)}, f32[512,128]{1,0:T(8,128)}, bf16[4,256,2...) custom-call(s32[3]{0:T(128)} %pad_add_fusion.ids_ref.refs_0_, bf16[8,176,512]{2,1,0:T(8,128)(2,1)} %get-tuple-element.124.recv_ref, ...), custom_call_target="tpu_custom_call" | custom-call | flops 4000000000 | bytes 8388608 | tf_op jit(solution)/shard_map/pallas_call | solution.py:805
  222.3 5.5 %shard_map.265 = (bf16[2,256,512]{2,1,0:T(8,128)(2,1)}, f32[1,512]{1,0:T(1,128)}, bf16[256,256]{1,0:T(8,128)(2,1)}, bf16[256,256]{1,0:T(8,128)(2,1)}) custom-call(s32[3]{0:T(128)} %pad_add_fusion.ids_ref.refs_0_, bf16[8,176,512]{2,1,0:T(8,128)(2,1)} %get-tuple-element.124.recv_ref, f32[2,256,512]{2,1,0:T(8,128)} %get-tuple-element.150.up_ref, ...), custom_call_target="tpu_custom_call" | custom-call | flops 1000000000 | bytes 8388608 | tf_op jit(solution)/shard_map/pallas_call | solution.py:805
  228.4 6.3 %shard_map.266 = (bf16[128,512]{1,0:T(8,128)(2,1)}, bf16[128,512]{1,0:T(8,128)(2,1)}, bf16[128,512]{1,0:T(8,128)(2,1)}, bf16[128,512]{1,0:T(8,128)(2,1)}, bf16[1...) custom-call(s32[3]{0:T(128)} %pad_add_fusion.ids_ref.refs_0_, ...), custom_call_target="tpu_custom_call" | custom-call | flops 1000000000 | bytes 8388608 | tf_op jit(solution)/shard_map/pallas_call | solution.py:805
  267.3 4.3 %collective-permute-done.54.refs_2_ = bf16[256,512]{1,0:T(8,128)(2,1)S(1)} collective-permute-done((bf16[256,512]{1,0:T(8,128)(2,1)}, bf16[256,512]{1,0:T(8,128)(2,1)S(1)}, u32[]{:S(2)}, u32[]{:S(2)}) %collective-permute-start.54) | collective-permute-done | bytes 262176 | tf_op jit(solution)/shard_map/ppermute | solution.py:825
  276.2 4.1 %collective-permute-done.62.refs_1_ = bf16[256,768]{1,0:T(8,128)(2,1)S(1)} collective-permute-done((bf16[256,768]{1,0:T(8,128)(2,1)}, bf16[256,768]{1,0:T(8,128)(2,1)S(1)}, u32[]{:S(2)}, u32[]{:S(2)}) %collective-permute-start.62) | collective-permute-done | bytes 393248 | tf_op jit(solution)/shard_map/ppermute | solution.py:825
  281.9 5.7 %collective-permute-done.63.refs_2_ = bf16[256,768]{1,0:T(8,128)(2,1)S(1)} collective-permute-done((bf16[256,768]{1,0:T(8,128)(2,1)}, bf16[256,768]{1,0:T(8,128)(2,1)S(1)}, u32[]{:S(2)}, u32[]{:S(2)}) %collective-permute-start.63) | collective-permute-done | bytes 393248 | tf_op jit(solution)/shard_map/ppermute | solution.py:825
  307.4 3.8 %shard_map.274 = (bf16[256,1024]{1,0:T(8,128)(2,1)}, bf16[256,1024]{1,0:T(8,128)(2,1)}, bf16[256,1024]{1,0:T(8,128)(2,1)}, bf16[256,1024]{1,0:T(8,128)(2,1)}) custom-call(bf16[4,256,1024]{2,1,0:T(8,128)(2,1)} %get-tuple-element.209.refs_0_, bf16[4,256,1024]{2,1,0:T(8,128)(2,1)} %copy-done), custom_call_target="tpu_custom_call" | custom-call | flops 100000000 | bytes 8388608 | tf_op jit(solution)/shard_map/pallas_call | solution.py:805
  329.8 8.8 %collective-permute-done.77.refs_2_ = bf16[256,1024]{1,0:T(8,128)(2,1)S(1)} collective-permute-done((bf16[256,1024]{1,0:T(8,128)(2,1)}, bf16[256,1024]{1,0:T(8,128)(2,1)S(1)}, u32[]{:S(2)}, u32[]{:S(2)}) %collective-permute-start.77) | collective-permute-done | bytes 524320 | tf_op jit(solution)/shard_map/ppermute | solution.py:825
  343.8 5.0 %collective-permute-done.69.refs_1_ = bf16[256,1024]{1,0:T(8,128)(2,1)S(1)} collective-permute-done((bf16[256,1024]{1,0:T(8,128)(2,1)}, bf16[256,1024]{1,0:T(8,128)(2,1)S(1)}, u32[]{:S(2)}, u32[]{:S(2)}) %collective-permute-start.69) | collective-permute-done | bytes 524320 | tf_op jit(solution)/shard_map/ppermute | solution.py:825
  353.5 4.7 %collective-permute-done.70.refs_2_ = bf16[256,1024]{1,0:T(8,128)(2,1)S(1)} collective-permute-done((bf16[256,1024]{1,0:T(8,128)(2,1)}, bf16[256,1024]{1,0:T(8,128)(2,1)S(1)}, u32[]{:S(2)}, u32[]{:S(2)}) %collective-permute-start.70) | collective-permute-done | bytes 524320 | tf_op jit(solution)/shard_map/ppermute | solution.py:825
  (372 shorter events, 152.9 us)
Async XLA Ops:
  14.2 36.6 %collective-permute-start.15 = (bf16[512,512]{1,0:T(8,128)(2,1)S(1)}, bf16[512,512]{1,0:T(8,128)(2,1)S(1)}, u32[]{:S(2)}, u32[]{:S(2)}) collective-permute-start(bf16[512,512]{1,0:T(8,128)(2,1)S(1)} %bitcast_select_fusion.1), channel_id=1, source_target_pairs={{0,16},{16,0},{1,17},{17,1},{2,18},{18,2},{3,19},{19,3},{4,20},{20... | collective-permute-start | bytes 1572872 | tf_op jit(solution)/shard_map/ppermute | solution.py:825
  18.1 31.8 %collective-permute-start.9 = (bf16[384,512]{1,0:T(8,128)(2,1)S(1)}, bf16[384,512]{1,0:T(8,128)(2,1)S(1)}, u32[]{:S(2)}, u32[]{:S(2)}) collective-permute-start(bf16[384,512]{1,0:T(8,128)(2,1)S(1)} %pad_maximum_fusion.refs_8_.refs_0_), channel_id=1, source_target_pairs={{0,3},{1,2},{2,1},{3,0},{4,7},{5,6},{6,5},{7,4},{8,11},{9,10},{10,... | collective-permute-start | bytes 1179656 | tf_op jit(solution)/shard_map/ppermute | solution.py:825
  59.9 35.8 %collective-permute-start.28 = (bf16[512,512]{1,0:T(8,128)(2,1)S(1)}, bf16[512,512]{1,0:T(8,128)(2,1)S(1)}, u32[]{:S(2)}, u32[]{:S(2)}) collective-permute-start(bf16[512,512]{1,0:T(8,128)(2,1)S(1)} %get-tuple-element.262.refs_4_), channel_id=1, source_target_pairs={{0,2},{1,3},{2,0},{3,1},{4,6},{5,7},{6,4},{7,5},{8,10},{9,11},{10,... | collective-permute-start | bytes 1572872 | tf_op jit(solution)/shard_map/ppermute | solution.py:825
  61.6 34.1 %collective-permute-start.18 = (bf16[512,512]{1,0:T(8,128)(2,1)S(1)}, bf16[512,512]{1,0:T(8,128)(2,1)S(1)}, u32[]{:S(2)}, u32[]{:S(2)}) collective-permute-start(bf16[512,512]{1,0:T(8,128)(2,1)S(1)} %get-tuple-element.263.refs_1_.refs_0_), channel_id=1, source_target_pairs={{0,3},{1,2},{2,1},{3,0},{4,7},{5,6},{6,5},{7,4},{8,11},{9,10},{10,... | collective-permute-start | bytes 1572872 | tf_op jit(solution)/shard_map/ppermute | solution.py:825
  62.9 44.0 %collective-permute-start.17 = (bf16[512,512]{1,0:T(8,128)(2,1)S(1)}, bf16[512,512]{1,0:T(8,128)(2,1)S(1)}, u32[]{:S(2)}, u32[]{:S(2)}) collective-permute-start(bf16[512,512]{1,0:T(8,128)(2,1)S(1)} %get-tuple-element.263.refs_1_.refs_0_), channel_id=1, source_target_pairs={{0,2},{1,3},{2,0},{3,1},{4,6},{5,7},{6,4},{7,5},{8,10},{9,11},{10,... | collective-permute-start | bytes 1572872 | tf_op jit(solution)/shard_map/ppermute | solution.py:825
  63.4 43.5 %collective-permute-start.16 = (bf16[512,512]{1,0:T(8,128)(2,1)S(1)}, bf16[512,512]{1,0:T(8,128)(2,1)S(1)}, u32[]{:S(2)}, u32[]{:S(2)}) collective-permute-start(bf16[512,512]{1,0:T(8,128)(2,1)S(1)} %get-tuple-element.263.refs_1_.refs_0_), channel_id=1, source_target_pairs={{0,1},{1,0},{2,3},{3,2},{4,5},{5,4},{6,7},{7,6},{8,9},{9,8},{10,11... | collective-permute-start | bytes 1572872 | tf_op jit(solution)/shard_map/ppermute | solution.py:825
  74.1 47.0 %collective-permute-start.27 = (bf16[512,512]{1,0:T(8,128)(2,1)S(1)}, bf16[512,512]{1,0:T(8,128)(2,1)S(1)}, u32[]{:S(2)}, u32[]{:S(2)}) collective-permute-start(bf16[512,512]{1,0:T(8,128)(2,1)S(1)} %get-tuple-element.262.refs_4_), channel_id=1, source_target_pairs={{0,1},{1,0},{2,3},{3,2},{4,5},{5,4},{6,7},{7,6},{8,9},{9,8},{10,11... | collective-permute-start | bytes 1572872 | tf_op jit(solution)/shard_map/ppermute | solution.py:825
  95.7 27.1 %collective-permute-start.19 = (bf16[512,512]{1,0:T(8,128)(2,1)S(1)}, bf16[512,512]{1,0:T(8,128)(2,1)S(1)}, u32[]{:S(2)}, u32[]{:S(2)}) collective-permute-start(bf16[512,512]{1,0:T(8,128)(2,1)S(1)} %get-tuple-element.263.refs_1_.refs_0_), channel_id=1, source_target_pairs={{0,16},{16,0},{1,17},{17,1},{2,18},{18,2},{3,19},{19,3},{4,20},{20... | collective-permute-start | bytes 1572872 | tf_op jit(solution)/shard_map/ppermute | solution.py:825
  95.8 27.1 %collective-permute-start.22 = (bf16[512,512]{1,0:T(8,128)(2,1)S(1)}, bf16[512,512]{1,0:T(8,128)(2,1)S(1)}, u32[]{:S(2)}, u32[]{:S(2)}) collective-permute-start(bf16[512,512]{1,0:T(8,128)(2,1)S(1)} %collective-permute-done.18.refs_4_.refs_3_), channel_id=1, source_target_pairs={{0,16},{16,0},{1,17},{17,1},{2,18},{18,2},{3,19},{19,3},{4,20},{20... | collective-permute-start | bytes 1572872 | tf_op jit(solution)/shard_map/ppermute | solution.py:825
  122.8 21.7 %collective-permute-start.30 = (bf16[512,512]{1,0:T(8,128)(2,1)S(1)}, bf16[512,512]{1,0:T(8,128)(2,1)S(1)}, u32[]{:S(2)}, u32[]{:S(2)}) collective-permute-start(bf16[512,512]{1,0:T(8,128)(2,1)S(1)} %get-tuple-element.262.refs_4_), channel_id=1, source_target_pairs={{0,16},{16,0},{1,17},{17,1},{2,18},{18,2},{3,19},{19,3},{4,20},{20... | collective-permute-start | bytes 1572872 | tf_op jit(solution)/shard_map/ppermute | solution.py:825
  122.9 21.6 %collective-permute-start.33 = (bf16[512,512]{1,0:T(8,128)(2,1)S(1)}, bf16[512,512]{1,0:T(8,128)(2,1)S(1)}, u32[]{:S(2)}, u32[]{:S(2)}) collective-permute-start(bf16[512,512]{1,0:T(8,128)(2,1)S(1)} %collective-permute-done.29.refs_7_), channel_id=1, source_target_pairs={{0,16},{16,0},{1,17},{17,1},{2,18},{18,2},{3,19},{19,3},{4,20},{20... | collective-permute-start | bytes 1572872 | tf_op jit(solution)/shard_map/ppermute | solution.py:825
  161.7 56.3 %collective-permute-start.34 = (bf16[128,512]{1,0:T(8,128)(2,1)}, bf16[128,512]{1,0:T(8,128)(2,1)S(1)}, u32[]{:S(2)}, u32[]{:S(2)}) collective-permute-start(bf16[128,512]{1,0:T(8,128)(2,1)} %get-tuple-element.131), channel_id=1, source_target_pairs={{0,1},{1,0},{2,3},{3,2},{16,17},{17,16},{18,19},{19,18},{4,5},{5,4... | collective-permute-start | bytes 393224 | tf_op jit(solution)/shard_map/ppermute | solution.py:825
  163.1 55.0 %collective-permute-start.35 = (bf16[128,512]{1,0:T(8,128)(2,1)}, bf16[128,512]{1,0:T(8,128)(2,1)S(1)}, u32[]{:S(2)}, u32[]{:S(2)}) collective-permute-start(bf16[128,512]{1,0:T(8,128)(2,1)} %get-tuple-element.132), channel_id=1, source_target_pairs={{0,2},{1,3},{2,0},{3,1},{16,18},{17,19},{18,16},{19,17},{4,6},{5,7... | collective-permute-start | bytes 393224 | tf_op jit(solution)/shard_map/ppermute | solution.py:825
  163.9 55.7 %collective-permute-start.36 = (bf16[128,512]{1,0:T(8,128)(2,1)}, bf16[128,512]{1,0:T(8,128)(2,1)S(1)}, u32[]{:S(2)}, u32[]{:S(2)}) collective-permute-start(bf16[128,512]{1,0:T(8,128)(2,1)} %get-tuple-element.133), channel_id=1, source_target_pairs={{0,3},{1,2},{2,1},{3,0},{16,19},{17,18},{18,17},{19,16},{4,7},{5,6... | collective-permute-start | bytes 393224 | tf_op jit(solution)/shard_map/ppermute | solution.py:825
  165.2 55.0 %collective-permute-start.37 = (bf16[128,512]{1,0:T(8,128)(2,1)}, bf16[128,512]{1,0:T(8,128)(2,1)S(1)}, u32[]{:S(2)}, u32[]{:S(2)}) collective-permute-start(bf16[128,512]{1,0:T(8,128)(2,1)} %get-tuple-element.134), channel_id=1, source_target_pairs={{0,16},{1,17},{2,18},{3,19},{16,0},{17,1},{18,2},{19,3},{4,20},{5,... | collective-permute-start | bytes 393224 | tf_op jit(solution)/shard_map/ppermute | solution.py:825
  191.5 30.1 %collective-permute-start.43 = (bf16[4,128,128]{2,1,0:T(8,128)(2,1)}, bf16[4,128,128]{2,1,0:T(8,128)(2,1)S(1)}, u32[]{:S(2)}, u32[]{:S(2)}) collective-permute-start(bf16[4,128,128]{2,1,0:T(8,128)(2,1)} %get-tuple-element.155), channel_id=1, source_target_pairs={{0,16},{16,0},{1,17},{17,1},{2,18},{18,2},{3,19},{19,3},{4,20},{20... | collective-permute-start | bytes 393224 | tf_op jit(solution)/shard_map/ppermute | solution.py:825
  221.6 84.4 %collective-permute-start.75 = (bf16[4,256,1024]{2,1,0:T(8,128)(2,1)}, bf16[4,256,1024]{2,1,0:T(8,128)(2,1)S(1)}, u32[]{:S(2)}, u32[]{:S(2)}) collective-permute-start(bf16[4,256,1024]{2,1,0:T(8,128)(2,1)} %get-tuple-element.210), channel_id=1, source_target_pairs={{0,16},{16,0},{1,17},{17,1},{2,18},{18,2},{3,19},{19,3},{4,20},{20... | collective-permute-start | bytes 6291464 | tf_op jit(solution)/shard_map/ppermute | solution.py:825
  250.4 62.3 %collective-permute-start.68 = (bf16[4,256,1024]{2,1,0:T(8,128)(2,1)}, bf16[4,256,1024]{2,1,0:T(8,128)(2,1)S(1)}, u32[]{:S(2)}, u32[]{:S(2)}) collective-permute-start(bf16[4,256,1024]{2,1,0:T(8,128)(2,1)} %get-tuple-element.200), channel_id=1, source_target_pairs={{0,16},{16,0},{1,17},{17,1},{2,18},{18,2},{3,19},{19,3},{4,20},{20... | collective-permute-start | bytes 6291464 | tf_op jit(solution)/shard_map/ppermute | solution.py:825
  280.3 21.3 %collective-permute-start.56 = (bf16[64,512]{1,0:T(8,128)(2,1)}, bf16[64,512]{1,0:T(8,128)(2,1)S(1)}, u32[]{:S(2)}, u32[]{:S(2)}) collective-permute-start(bf16[64,512]{1,0:T(8,128)(2,1)} %get-tuple-element.182), channel_id=1, source_target_pairs={{0,4},{4,0},{8,12},{12,8},{1,5},{5,1},{9,13},{13,9},{2,6},{6,2},{1... | collective-permute-start | bytes 196616 | tf_op jit(solution)/shard_map/ppermute | solution.py:825
  312.7 25.9 %collective-permute-start.77 = (bf16[256,1024]{1,0:T(8,128)(2,1)}, bf16[256,1024]{1,0:T(8,128)(2,1)S(1)}, u32[]{:S(2)}, u32[]{:S(2)}) collective-permute-start(bf16[256,1024]{1,0:T(8,128)(2,1)} %get-tuple-element.213), channel_id=1, source_target_pairs={{0,2},{1,3},{2,0},{3,1},{4,6},{5,7},{6,4},{7,5},{8,10},{9,11},{10,... | collective-permute-start | bytes 1572872 | tf_op jit(solution)/shard_map/ppermute | solution.py:825
  319.4 29.4 %collective-permute-start.69 = (bf16[256,1024]{1,0:T(8,128)(2,1)}, bf16[256,1024]{1,0:T(8,128)(2,1)S(1)}, u32[]{:S(2)}, u32[]{:S(2)}) collective-permute-start(bf16[256,1024]{1,0:T(8,128)(2,1)} %get-tuple-element.202), channel_id=1, source_target_pairs={{0,1},{1,0},{2,3},{3,2},{4,5},{5,4},{6,7},{7,6},{8,9},{9,8},{10,11... | collective-permute-start | bytes 1572872 | tf_op jit(solution)/shard_map/ppermute | solution.py:825
  322.8 35.5 %collective-permute-start.70 = (bf16[256,1024]{1,0:T(8,128)(2,1)}, bf16[256,1024]{1,0:T(8,128)(2,1)S(1)}, u32[]{:S(2)}, u32[]{:S(2)}) collective-permute-start(bf16[256,1024]{1,0:T(8,128)(2,1)} %get-tuple-element.203), channel_id=1, source_target_pairs={{0,2},{1,3},{2,0},{3,1},{4,6},{5,7},{6,4},{7,5},{8,10},{9,11},{10,... | collective-permute-start | bytes 1572872 | tf_op jit(solution)/shard_map/ppermute | solution.py:825
  326.2 32.0 %collective-permute-start.71 = (bf16[256,1024]{1,0:T(8,128)(2,1)}, bf16[256,1024]{1,0:T(8,128)(2,1)S(1)}, u32[]{:S(2)}, u32[]{:S(2)}) collective-permute-start(bf16[256,1024]{1,0:T(8,128)(2,1)} %get-tuple-element.204), channel_id=1, source_target_pairs={{0,3},{1,2},{2,1},{3,0},{4,7},{5,6},{6,5},{7,4},{8,11},{9,10},{10,... | collective-permute-start | bytes 1572872 | tf_op jit(solution)/shard_map/ppermute | solution.py:825
  342.1 24.0 %collective-permute-start.80 = (bf16[64,1024]{1,0:T(8,128)(2,1)}, bf16[64,1024]{1,0:T(8,128)(2,1)S(1)}, u32[]{:S(2)}, u32[]{:S(2)}) collective-permute-start(bf16[64,1024]{1,0:T(8,128)(2,1)} %get-tuple-element.217), channel_id=1, source_target_pairs={{0,8},{4,12},{8,0},{12,4},{1,9},{5,13},{9,1},{13,5},{2,10},{6,14},... | collective-permute-start | bytes 393224 | tf_op jit(solution)/shard_map/ppermute | solution.py:825
  (145 other events, 2489.7 us)

commit v3 on v2

--- a/solution.py
+++ b/solution.py
@@ -16,8 +16,8 @@
 CODE_ROW = 3
 LEN_ROW = 4
 ROUTER_AT = 8
-GAIN_LANE = 64
-ROUTER_LANES = (8, 24, 40)
+GAIN_ROW = 24
+ROUTER_LANES = (0, 8, 16)
 VMEM_LIMIT = 56 * 1024 * 1024
 
 
@@ -108,7 +108,7 @@
     return jnp.concatenate([packed[:, 128 * c : 128 * c + 128] for c in range(4)], 0)
 
 
-def routing(query_rows, router_block, code, m):
+def routing(query_rows, router_block, code):
     second = jnp.floor(code * 0.125)
     first = code - 8.0 * second
     e0, e1 = first.astype(jnp.int32), second.astype(jnp.int32)
@@ -120,9 +120,7 @@
     x0, x1 = jnp.exp(l0 - top), jnp.exp(l1 - top)
     total = x0 + x1
     owners = lax.broadcasted_iota(jnp.int32, (code.shape[0], 512), 1) >> 6
-    mask0 = owners == (e0 ^ (2 * m))
-    mask1 = owners == (e1 ^ (2 * m))
-    return e0, e1, x0 / total, x1 / total, mask0, mask1
+    return e0, e1, x0 / total, x1 / total, owners == e0, owners == e1
 
 
 def fold(wide, mask):
@@ -169,15 +167,22 @@
         copy.start()
         return copy.wait
 
-    def rows(self, cond, yes, no, at, dst):
+    def rows(self, cond, yes, no, at, dst, m):
         cut = pl.ds(at, 128)
         return [
-            self.start(cond, yes[b].at[cut], no[b].at[cut], dst.at[pl.ds(128 * b, 128)])
+            self.start(cond, yes[b].at[cut], no[b].at[cut], dst.at[pl.ds(128 * (m ^ b), 128)])
             for b in range(4)
         ]
 
-    def blocks(self, cond, yes, no, dst):
-        return [self.start(cond, yes[b], no[b], dst.at[b]) for b in range(4)]
+    def stacked(self, cond, yes, no, at, dst):
+        cut = pl.ds(at, 128)
+        return [
+            self.start(cond, yes.at[i, cut], no.at[i, cut], dst.at[pl.ds(128 * i, 128)])
+            for i in range(4)
+        ]
+
+    def pieces(self, cond, yes, no, dst, m):
+        return [self.start(cond, yes[b], no[b], dst.at[m ^ b]) for b in range(4)]
 
 
 def wait_all(waits):
@@ -335,13 +340,18 @@
     return ref[...].reshape(512, ref.shape[-1])
 
 
-def attention_weight_grads(first_t, gated_ref, dz_ref, dq_ref, sec, keep_ref, send_ref):
+def attention_weight_grads(first_t, gated_ref, dz_ref, dq_ref, sec, keep_ref, send_ref, lane):
     grad_q = nn(first_t, flat(dq_ref))
     grad_o = nn(turned_rows(flat(dz_ref)), flat(gated_ref))
     for b in range(4):
         cut = slice(128 * b, 128 * b + 128)
-        split_halves(grad_q[:, cut], sec, keep_ref, send_ref, b, 0)
-        split_halves(grad_o[:, cut], sec, keep_ref, send_ref, b, 128)
+        split_halves(grad_q[:, cut], sec, keep_ref, send_ref, b, lane)
+        split_halves(grad_o[:, cut], sec, keep_ref, send_ref, b, lane + 128)
+
+
+def router_grads(dlog_ref, rows_ref):
+    turned = flat(dlog_ref).astype(F32).T.astype(BF)
+    return nn(turned, flat(rows_ref))[0:32]
 
 
 def gelu_parts(pre):
@@ -367,61 +377,51 @@
         kv_s[j, 1 - sec] = kvo_ref[j]
 
 
-def pack_kernel(ids_ref, len_ref, x_ref, gain_ref, w_kv_ref, own_ref, cross_ref, router_ref, *rest):
-    sends, kv_s, extra_s = rest[:8], rest[8], rest[9]
-    sec, m = ids_ref[0], ids_ref[1]
+def pack_kernel(
+    len_ref, x_ref, gain_ref, w_kv_ref, own_ref, cross_ref, router_ref, send_ref, extra_s
+):
     gain = gain_ref[0:1, :].astype(F32)
     w_kv = w_kv_ref[...]
-    for i in range(4):
-        first = norm_of(x_ref[i].astype(F32), gain)[0].astype(BF)
-        kv_s[i] = nn(first, w_kv).astype(BF).reshape(2, 128, 128)
     extra_s[...] = jnp.zeros_like(extra_s)
     extra_s[0:3, :] = gain_ref[...].astype(F32)
     extra_s[ROUTER_AT : ROUTER_AT + 8, :] = router_ref[...].astype(F32)
     lanes = lax.broadcasted_iota(jnp.int32, (1, 512), 1)
-    for b in range(4):
-        to = m ^ b
+    for i in range(4):
+        first = norm_of(x_ref[i].astype(F32), gain)[0].astype(BF)
+        kv = nn(first, w_kv).astype(BF)
         row = jnp.zeros((1, 512), jnp.int32)
         for k in range(8):
-            length = len_ref[to, k]
+            length = len_ref[i, k]
             row = jnp.where(lanes == k, length >> 5, row)
             row = jnp.where(lanes == 128 + k, length & 31, row)
         extra_s[LEN_ROW : LEN_ROW + 1, :] = row.astype(F32)
-        own, cross = own_ref[to], cross_ref[to]
+        own, cross = own_ref[i], cross_ref[i]
         own_code = (own[0:1] + 8 * own[1:2]).astype(F32)
         cross_code = (cross[0:1] + 8 * cross[1:2]).astype(F32)
-        for a in range(2):
-            half = sec ^ a
-            ref = sends[4 * a + b]
-            ref[0:128, :] = x_ref[to, pl.ds(pl.multiple_of(128 * half, 128), 128), :]
-            far = kv_s[to, 1 - half]
-            ref[128:160, :] = jnp.concatenate([far[32 * c : 32 * c + 32] for c in range(4)], 1)
-            extra_s[CODE_ROW : CODE_ROW + 1, 0:128] = jnp.where(
-                half == 0, own_code[:, 0:128], own_code[:, 128:256]
+        for half in range(2):
+            to = 4 * half + i
+            here = slice(128 * half, 128 * half + 128)
+            send_ref[to, 0:128, :] = x_ref[i, here, :]
+            far = kv[128 * (1 - half) : 128 * (1 - half) + 128]
+            send_ref[to, 128:160, :] = jnp.concatenate(
+                [far[32 * c : 32 * c + 32] for c in range(4)], 1
             )
-            extra_s[CODE_ROW : CODE_ROW + 1, 128:256] = jnp.where(
-                half == 0, cross_code[:, 0:128], cross_code[:, 128:256]
-            )
-            ref[EX_AT : EX_AT + 16, :] = extra_s[...].astype(BF)
-
-
-def self_fwd_kernel(ids_ref, *refs):
-    pieces, wa_own, wa_oth, kvw_own, kvw_oth = refs[:8], refs[8:12], refs[12:16], refs[16], refs[17]
-    recv_ref, h1_ref, g1_ref, mixed_e, mixed_d, log_e, log_d = refs[18:25]
-    wq, wo, wkv, kv_s, k2, v2, sems = refs[25:]
+            extra_s[CODE_ROW : CODE_ROW + 1, 0:128] = own_code[:, here]
+            extra_s[CODE_ROW : CODE_ROW + 1, 128:256] = cross_code[:, here]
+            send_ref[to, EX_AT : EX_AT + 16, :] = extra_s[...].astype(BF)
+
+
+def self_fwd_kernel(ids_ref, recv_ref, *refs):
+    wa_own, wa_oth, kvw_own, kvw_oth = refs[:4], refs[4:8], refs[8], refs[9]
+    h1_ref, g1_ref, mixed_e, mixed_d, log_e, log_d = refs[10:16]
+    wq, wo, wkv, kv_s, k2, v2, sems = refs[16:]
     sec, m = ids_ref[0], ids_ref[1]
     loads = Loads(sems)
-    come = []
-    for a in range(2):
-        for b in range(4):
-            at = 4 * (sec ^ a) + (m ^ b)
-            come.append(loads.plain(pieces[4 * a + b], recv_ref.at[at]))
     kv_waits = [loads.start(sec == i, kvw_own, kvw_oth, wkv.at[i]) for i in range(2)]
     waits = []
     for layer in range(2):
-        waits += loads.rows(sec == layer, wa_own, wa_oth, 0, wq.at[layer])
-        waits += loads.rows(sec == layer, wa_own, wa_oth, 128, wo.at[layer])
-    wait_all(come)
+        waits += loads.rows(sec == layer, wa_own, wa_oth, 0, wq.at[layer], m)
+        waits += loads.rows(sec == layer, wa_own, wa_oth, 128, wo.at[layer], m)
     wait_all(kv_waits)
     for layer in range(2):
         own_self_kv(recv_ref, layer, sec, wkv[layer], kv_s)
@@ -436,9 +436,7 @@
         ):
             rows = rows_of(recv_ref, layer, t)
             first = norm_of(rows, gain_of(recv_ref, layer, 0))[0].astype(BF)
-            route = routing(
-                first, extra_of(recv_ref, layer, 0), codes_of(recv_ref, layer, t, 0), m
-            )
+            route = routing(first, extra_of(recv_ref, layer, 0), codes_of(recv_ref, layer, t, 0))
             allowed = allowed_rows(t, sec, ends[layer], ends[layer], layer == 1)
             out, mixed, row_log = attend_tile(
                 first, route, wq[layer], wo[layer], k2[layer], v2[layer], allowed
@@ -451,23 +449,18 @@
     lax.fori_loop(0, 2, tile, 0)
 
 
-def enc_ffn_kernel(recv_ref, h1_ref, kvc_ref, *refs):
-    ids_ref, f_own, f_oth = refs[0], refs[1:5], refs[5:9]
-    h2_ref, mem_ref, kvm_ref, w_in, w_out, third_s, sems = refs[9:]
-    low = ids_ref[0] == 0
+def enc_ffn_kernel(
+    ids_ref, recv_ref, h1_ref, kvc_ref, *refs
+):
+    f_own, f_oth = refs[:4], refs[4:8]
+    h2_ref, mem_ref, kvm_ref, w_in, w_out, third_s, sems = refs[8:]
+    low, m = ids_ref[0] == 0, ids_ref[1]
     loads = Loads(sems)
-    waits = [
-        (
-            loads.start(low, f_own[b], f_oth[b], w_in.at[b]),
-            loads.start(low, f_oth[b], f_own[b], w_out.at[b]),
-        )
-        for b in range(4)
-    ]
+    waits = loads.pieces(low, f_own, f_oth, w_in, m) + loads.pieces(low, f_oth, f_own, w_out, m)
     for t in range(2):
         h2_ref[t] = h1_ref[t]
         third_s[t] = norm_of(h1_ref[t], gain_of(recv_ref, 0, 2))[0].astype(BF)
-    for pair in waits:
-        wait_all(pair)
+    wait_all(waits)
 
     def chunk(c, carry):
         pre = nn(flat(third_s), w_in[c])
@@ -484,13 +477,14 @@
         kvm_ref[2 * t + 1] = kv[128:256]
 
 
-def cross_fwd_kernel(ids_ref, recv_ref, g1_ref, kvm_ref, kvo_ref, rc_ref, *refs):
-    wa_own, wa_oth = refs[:4], refs[4:8]
-    g2_ref, mixed_ref, log_ref, wq, wo, kv_s, k2, v2, sems = refs[8:]
-    sec, m = ids_ref[0], ids_ref[1]
+def cross_fwd_kernel(
+    ids_ref, recv_ref, g1_ref, kvm_ref, kvo_ref, rc_ref, cc_own, cc_oth, g2_ref, mixed_ref, log_ref,
+    wq, wo, kv_s, k2, v2, sems,
+):
+    sec = ids_ref[0]
     loads = Loads(sems)
-    waits = loads.rows(sec == 0, wa_own, wa_oth, 256, wq)
-    waits += loads.rows(sec == 0, wa_oth, wa_own, 256, wo)
+    waits = loads.stacked(sec == 0, cc_own, cc_oth, 128, wq)
+    waits += loads.stacked(sec == 0, cc_oth, cc_own, 128, wo)
     cross_kv(kvm_ref, kvo_ref, sec, kv_s)
     widen_kv(kv_s, k2, v2)
     wait_all(waits)
@@ -500,7 +494,7 @@
     def tile(t, carry):
         before = g1_ref[t]
         second = norm_of(before, gain_of(recv_ref, 1, 1))[0].astype(BF)
-        route = routing(second, rc_ref[...], codes_of(recv_ref, 1, t, 128), m)
+        route = routing(second, rc_ref[...], codes_of(recv_ref, 1, t, 128))
         allowed = allowed_rows(t, sec, ends_q, ends_k, False)
         out, mixed, row_log = attend_tile(second, route, wq[...], wo[...], k2[...], v2[...], allowed)
         g2_ref[t] = before + out
@@ -522,18 +516,21 @@
     return hidden
 
 
-def dec_ffn_kernel(ids_ref, recv_ref, g2_ref, mem_ref, *refs):
-    cots, f_own, f_oth = refs[:4], refs[4:8], refs[8:12]
-    outs, dg2_ref, gain_ref, keep_ref, send_ref = refs[12:20], refs[20], refs[21], refs[22], refs[23]
-    w_in, w_out, cot_s, third_s, third_t, cot_t, acc, dthird, sems = refs[24:]
+def dec_ffn_kernel(
+    ids_ref, recv_ref, g2_ref, mem_ref, cc_own, *refs
+):
+    f_own, f_oth = refs[:4], refs[4:8]
+    outs_ref, dg2_ref, gain_ref, keep_ref, send_ref = refs[8:13]
+    w_in, w_out, cot_s, third_s, third_t, cot_t, acc, dthird, sems = refs[13:]
     sec, m = ids_ref[0], ids_ref[1]
     low = sec == 0
     loads = Loads(sems)
-    cot_waits = [loads.plain(cots[b], cot_s.at[m ^ b]) for b in range(4)]
-    waits = loads.blocks(low, f_own, f_oth, w_in) + loads.blocks(low, f_oth, f_own, w_out)
+    cot_waits = [loads.plain(cc_own.at[i, pl.ds(0, 128)], cot_s.at[i]) for i in range(4)]
+    waits = loads.pieces(low, f_own, f_oth, w_in, m) + loads.pieces(low, f_oth, f_own, w_out, m)
     for t in range(2):
         acc[t] = g2_ref[t]
         third_s[t] = norm_of(g2_ref[t], gain_of(recv_ref, 1, 2))[0].astype(BF)
+        outs_ref[2 * t : 2 * t + 2] = mem_ref[t].reshape(2, 128, 512)
     third_t[...] = turned_rows(flat(third_s))
     wait_all(cot_waits)
     cot_t[...] = turned_rows(flat(cot_s))
@@ -551,30 +548,23 @@
     total = jnp.zeros((1, 512), F32)
     gain = gain_of(recv_ref, 1, 2)
     for t in range(2):
+        outs_ref[4 + 2 * t : 6 + 2 * t] = acc[t].astype(BF).reshape(2, 128, 512)
         unused_out, unit, scaled = norm_of(g2_ref[t], gain)
         back, gain_grad = norm_back(dthird[TILE * t : TILE * t + TILE, :], unit, scaled, gain)
         dg2_ref[t] = cot_s[2 * t : 2 * t + 2].reshape(TILE, 512).astype(F32) + back
         total = total + gain_grad
     gain_ref[...] = total
-    for a in range(2):
-        for b in range(4):
-            t, i = (m ^ b) >> 1, (m ^ b) & 1
-            cut = pl.ds(pl.multiple_of(128 * i, 128), 128)
-            outs[4 * a + b][...] = jnp.where(
-                (sec ^ a) == 0, mem_ref[t, cut, :].astype(F32), acc[t, cut, :]
-            ).astype(BF)
 
 
 def cross_back_kernel(
-    ids_ref, recv_ref, g1_ref, dg2_ref, mixed_ref, log_ref, kvm_ref, kvo_ref, rc_ref, *refs
+    ids_ref, recv_ref, g1_ref, dg2_ref, mixed_ref, log_ref, kvm_ref, kvo_ref, rc_ref, cc_own, cc_oth,
+    dg1_ref, gain_ref, own_ref, send_ref, router_ref, keepw_ref, sendw_ref,
+    wq, wo, kv_s, k2, v2, segk, grad_k, grad_v, second_s, gated_s, dz_s, dq_s, dlog_s, sems,
 ):
-    wa_own, wa_oth = refs[:4], refs[4:8]
-    dg1_ref, gain_ref, own_ref, send_ref, router_ref, keepw_ref, sendw_ref = refs[8:15]
-    wq, wo, kv_s, k2, v2, segk, grad_k, grad_v, second_s, gated_s, dz_s, dq_s, dlog_s, sems = refs[15:]
-    sec, m = ids_ref[0], ids_ref[1]
+    sec = ids_ref[0]
     loads = Loads(sems)
-    waits = loads.rows(sec == 0, wa_own, wa_oth, 256, wq)
-    waits += loads.rows(sec == 0, wa_oth, wa_own, 256, wo)
+    waits = loads.stacked(sec == 0, cc_own, cc_oth, 128, wq)
+    waits += loads.stacked(sec == 0, cc_oth, cc_own, 128, wo)
     cross_kv(kvm_ref, kvo_ref, sec, kv_s)
     widen_kv(kv_s, k2, v2)
     ends_k = ends_of(extra_of(recv_ref, 0, 0).astype(F32))
@@ -589,7 +579,7 @@
         second, unit, scaled = norm_of(g1_ref[t], gain)
         second = second.astype(BF)
         second_s[t] = second
-        route = routing(second, rc_ref[...], codes_of(recv_ref, 1, t, 128), m)
+        route = routing(second, rc_ref[...], codes_of(recv_ref, 1, t, 128))
         allowed = allowed_cols(t, sec, ends_q, segk, False)
         grad_rows = attend_back_tile(
             t, dg2_ref[t], second, route, mixed_ref[t], log_ref[t], wq[...], wo[...], rc_ref[...],
@@ -601,21 +591,30 @@
 
     gain_ref[...] = lax.fori_loop(0, 2, tile, jnp.zeros((1, 512), F32))
     fold_kv(grad_k, grad_v, sec, own_ref, send_ref)
-    second_t = turned_rows(flat(second_s))
-    router_ref[...] = nn(second_t, flat(dlog_s))
-    attention_weight_grads(second_t, gated_s, dz_s, dq_s, sec, keepw_ref, sendw_ref)
+    router_ref[...] = router_grads(dlog_s, second_s)
+    attention_weight_grads(
+        turned_rows(flat(second_s)), gated_s, dz_s, dq_s, sec, keepw_ref, sendw_ref, 0
+    )
 
 
 def self_back_kernel(layer, ids_ref, recv_ref, up_ref, mixed_ref, log_ref, *refs):
     wa_own, wa_oth, kvw_own, kvw_oth = refs[:4], refs[4:8], refs[8], refs[9]
-    dfirst_ref, own_ref, send_ref, router_ref, keepw_ref, sendw_ref = refs[10:16]
-    wq, wo, wkv, kv_s, k2, v2, segk, grad_k, grad_v = refs[16:25]
-    first_s, gated_s, dz_s, dq_s, dlog_s, sems = refs[25:]
+    refs = refs[10:]
+    if layer == 1:
+        before, refs = refs[:2], refs[2:]
+    dfirst_ref, own_ref, send_ref, router_ref, keepw_ref, sendw_ref = refs[:6]
+    wq, wo, wkv, kv_s, k2, v2, segk, grad_k, grad_v = refs[6:15]
+    first_s, gated_s, dz_s, dq_s, dlog_s, sems = refs[15:]
     sec, m = ids_ref[0], ids_ref[1]
     mine = sec == layer
     loads = Loads(sems)
     kv_wait = loads.start(mine, kvw_own, kvw_oth, wkv)
-    waits = loads.rows(mine, wa_own, wa_oth, 0, wq) + loads.rows(mine, wa_own, wa_oth, 128, wo)
+    waits = loads.rows(mine, wa_own, wa_oth, 0, wq, m) + loads.rows(mine, wa_own, wa_oth, 128, wo, m)
+    lane = 0
+    if layer == 1:
+        lane = 256
+        for src, dst in zip(before, (keepw_ref, sendw_ref)):
+            waits.append(loads.plain(src, dst.at[:, :, pl.ds(0, 256)]))
     ends = ends_of(extra_of(recv_ref, layer, 0).astype(F32))
     key_segments_t(ends, segk)
     grad_k[...] = jnp.zeros_like(grad_k)
@@ -629,7 +628,7 @@
     def tile(t, carry):
         first = norm_of(rows_of(recv_ref, layer, t), gain_of(recv_ref, layer, 0))[0].astype(BF)
         first_s[t] = first
-        route = routing(first, router_block, codes_of(recv_ref, layer, t, 0), m)
+        route = routing(first, router_block, codes_of(recv_ref, layer, t, 0))
         allowed = allowed_cols(t, sec, ends, segk, layer == 1)
         dfirst_ref[t] = attend_back_tile(
             t, up_ref[t], first, route, mixed_ref[t], log_ref[t], wq[...], wo[...], router_block,
@@ -640,19 +639,22 @@
 
     lax.fori_loop(0, 2, tile, 0)
     fold_kv(grad_k, grad_v, sec, own_ref, send_ref)
-    first_t = turned_rows(flat(first_s))
-    router_ref[...] = nn(first_t, flat(dlog_s))
-    attention_weight_grads(first_t, gated_s, dz_s, dq_s, sec, keepw_ref, sendw_ref)
-
-
-def enc_ffn_back_kernel(ids_ref, recv_ref, h1_ref, h2_ref, own_ref, come_ref, kvc_ref, *refs):
+    router_ref[...] = router_grads(dlog_s, first_s)
+    attention_weight_grads(
+        turned_rows(flat(first_s)), gated_s, dz_s, dq_s, sec, keepw_ref, sendw_ref, lane
+    )
+
+
+def enc_ffn_back_kernel(
+    ids_ref, recv_ref, h1_ref, h2_ref, own_ref, come_ref, kvc_ref, *refs
+):
     f_own, f_oth = refs[:4], refs[4:8]
     dh1_ref, gain_ref, gain2_ref, keep_ref, send_ref = refs[8:13]
     w_in, w_out, third_s, third_t, dy_s, dy_t, dthird, sems = refs[13:]
-    sec = ids_ref[0]
+    sec, m = ids_ref[0], ids_ref[1]
     low = sec == 0
     loads = Loads(sems)
-    waits = loads.blocks(low, f_own, f_oth, w_in) + loads.blocks(low, f_oth, f_own, w_out)
+    waits = loads.pieces(low, f_own, f_oth, w_in, m) + loads.pieces(low, f_oth, f_own, w_out, m)
     total = jnp.zeros((1, 512), F32)
     gain = gain_of(recv_ref, 0, 1)
     for t in range(2):
@@ -685,7 +687,7 @@
     gain2_ref[...] = total
 
 
-def finish_rows(layer, recv_ref, up_ref, df_ref, own_ref, come_ref, wkv, first_s, dx_s):
+def finish_rows(layer, recv_ref, up_ref, df_ref, own_ref, come_ref, wkv, first_s, out_ref, at):
     total = jnp.zeros((1, 512), F32)
     gain = gain_of(recv_ref, layer, 0)
     dkvs = []
@@ -696,7 +698,9 @@
         dkv = dkv.reshape(TILE, 128)
         dkvs.append(dkv)
         back, gain_grad = norm_back(df_ref[t] + nt(dkv, wkv), unit, scaled, gain)
-        dx_s[t] = (up_ref[t] + back).astype(BF)
+        dx = (up_ref[t] + back).astype(BF)
+        for i in range(2):
+            out_ref[at + 2 * t + i, 0:128, :] = dx[128 * i : 128 * i + 128]
         total = total + gain_grad
     grad = nn(turned_rows(flat(first_s)), jnp.concatenate(dkvs, 0))
     return total, grad
@@ -704,8 +708,7 @@
 
 def dec_finish_kernel(
     ids_ref, recv_ref, up_ref, df_ref, own_ref, come_ref, own_c, come_c, mem_ref, kvw_own, kvw_oth,
-    dx_ref, gain_ref, keep_ref, send_ref,
-    wkv, first_s, sems,
+    dx_ref, gain_ref, keep_ref, send_ref, wkv, first_s, sems,
 ):
     sec = ids_ref[0]
     wait = Loads(sems).start(sec == 1, kvw_own, kvw_oth, wkv)
@@ -713,104 +716,101 @@
     split_flat(nn(turned_rows(flat(mem_ref)), dkv_c), sec, keep_ref, send_ref, 128)
     wait()
     gain_ref[...], grad = finish_rows(
-        1, recv_ref, up_ref, df_ref, own_ref, come_ref, wkv[...], first_s, dx_ref
+        1, recv_ref, up_ref, df_ref, own_ref, come_ref, wkv[...], first_s, dx_ref, 0
     )
     split_flat(grad, sec, keep_ref, send_ref, 0)
 
 
 def enc_finish_kernel(
     ids_ref, recv_ref, up_ref, df_ref, own_ref, come_ref, dx1_ref, r0, r1, rc,
-    gain_e1, gain_e2, gain_d0, gain_d1, gain_d2, kvw_own, kvw_oth, *refs
+    gain_e1, gain_e2, gain_d0, gain_d1, gain_d2, kvw_own, kvw_oth,
+    out_ref, wkv, first_s, misc, sems,
 ):
-    outs, keep_ref, send_ref, wkv, first_s, dx_s, sems = refs[:8], *refs[8:]
-    sec, m = ids_ref[0], ids_ref[1]
-    Loads(sems).start(sec == 0, kvw_own, kvw_oth, wkv)()
+    sec = ids_ref[0]
+    wait = Loads(sems).start(sec == 0, kvw_own, kvw_oth, wkv)
+    misc[...] = r0[...] + r1[...] + rc[...]
+    out_ref[4:8, 0:128, :] = dx1_ref[...]
+    wait()
     gain_e0, grad = finish_rows(
-        0, recv_ref, up_ref, df_ref, own_ref, come_ref, wkv[...], first_s, dx_s
-    )
-    split_flat(grad, sec, keep_ref, send_ref, 0)
-    for a in range(2):
-        for b in range(4):
-            t, i = (m ^ b) >> 1, (m ^ b) & 1
-            cut = pl.ds(pl.multiple_of(128 * i, 128), 128)
-            outs[4 * a + b][...] = jnp.where(
-                (sec ^ a) == 0, dx_s[t, cut, :].astype(F32), dx1_ref[t, cut, :].astype(F32)
-            ).astype(BF)
-    gains = (gain_e0, gain_e1[...], gain_e2[...], gain_d0[...], gain_d1[...], gain_d2[...])
-    lanes = lax.broadcasted_iota(jnp.int32, (128, 128), 1)
-    blocks = []
-    for b in range(4):
-        cut = slice(128 * b, 128 * b + 128)
-        misc = r0[cut, :] + r1[cut, :] + rc[cut, :]
-        for i, row in enumerate(gains):
-            misc = misc + jnp.where(lanes == GAIN_LANE + i, row_to_col(row[:, cut]), 0.0)
-        blocks.append(misc)
-    for b in range(2):
-        cut = slice(128 * b, 128 * b + 128)
-        keep_ref[cut, 128:256] = jnp.where(sec == 0, blocks[b], blocks[b + 2]).astype(BF)
-        send_ref[cut, 128:256] = jnp.where(sec == 0, blocks[b + 2], blocks[b]).astype(BF)
-
-
-def add_kernel(counts, *refs):
-    n = len(counts)
-    keeps, comes, outs = refs[:n], refs[n : 2 * n], refs[2 * n :]
-    for b in range(4):
-        lane = 0
-        for keep, come, (pieces, width) in zip(keeps, comes, counts):
-            left = keep[b] if pieces == 4 else keep[...]
-            right = come[b] if pieces == 4 else come[...]
-            outs[b][:, lane : lane + width] = (left.astype(F32) + right.astype(F32)).astype(BF)
-            lane += width
-
-
-def sum_kernel(ids_ref, *refs):
-    groups = (len(refs) - 4) // 4
-    outs = refs[4 * groups :]
-    rows = outs[0].shape[0]
-    d = ids_ref[2]
-    for k in range(4):
-        cut = pl.ds(pl.multiple_of((d ^ k) * rows, rows), rows)
-        lane = 0
-        for g in range(groups):
-            parts = refs[4 * g : 4 * g + 4]
-            total = parts[0][cut, :].astype(F32)
-            for part in parts[1:]:
-                total = total + part[cut, :].astype(F32)
-            width = parts[0].shape[1]
-            outs[k][:, lane : lane + width] = total.astype(BF)
-            lane += width
-
-
-def place_kernel(ids_ref, *refs):
-    pieces, out_ref, buf, sems = refs[:8], refs[8], refs[9], refs[10]
-    sec, m = ids_ref[0], ids_ref[1]
-    loads = Loads(sems)
-    waits = [loads.plain(pieces[i], buf.at[i]) for i in range(8)]
-    wait_all(waits)
-    for a in range(2):
-        for b in range(4):
-            out_ref[m ^ b, sec ^ a] = buf[4 * a + b].astype(out_ref.dtype)
+        0, recv_ref, up_ref, df_ref, own_ref, come_ref, wkv[...], first_s, out_ref, 0
+    )
+    rows = (gain_e0, gain_e1[...], gain_e2[...], gain_d0[...], gain_d1[...], gain_d2[...])
+    for i, row in enumerate(rows):
+        misc[GAIN_ROW + i : GAIN_ROW + i + 1, :] = row
+    both = misc[...]
+    for half in range(2):
+        cut = slice(256 * half, 256 * half + 256)
+        part = grad[cut].astype(BF)
+        small = both[:, cut].astype(BF)
+        block = jnp.concatenate(
+            [
+                jnp.concatenate([part[64 * c : 64 * c + 64] for c in range(4)], 1),
+                jnp.concatenate([small[0:16], small[16:32]], 1),
+            ],
+            0,
+        )
+        for i in range(4):
+            out_ref[4 * half + i, 128:208, :] = block
+
+
+def add_kernel(keep_ref, come_ref, out_ref):
+    out_ref[...] = (keep_ref[...].astype(F32) + come_ref[...].astype(F32)).astype(BF)
+
+
+def add_two_kernel(keep_ref, come_ref, keep_s, come_s, out_ref):
+    out_ref[0, :, 0:256] = (keep_ref[0].astype(F32) + come_ref[0].astype(F32)).astype(BF)
+    out_ref[0, :, 256:512] = (keep_s[...].astype(F32) + come_s[...].astype(F32)).astype(BF)
+
+
+def tail_kernel(dx_ref, att_d, att_e, dx_out, out_ref):
+    for i in range(4):
+        for half in range(2):
+            dx_out[i, half] = dx_ref[4 * half + i, 0:128, :].astype(F32)
+    for ref, lane in ((att_d, 0), (att_e, 512)):
+        total = ref[0].astype(F32)
+        for i in range(1, 4):
+            total = total + ref[i].astype(F32)
+        out_ref[:, lane : lane + 512] = total.astype(BF)
+    small = dx_ref[0, 128:208, :].astype(F32)
+    for i in range(1, 8):
+        small = small + dx_ref[i, 128:208, :].astype(F32)
+    for c in range(4):
+        out_ref[64 * c : 64 * c + 64, 1024:1152] = small[0:64, 128 * c : 128 * c + 128].astype(BF)
+    misc = jnp.concatenate([small[64:80, 0:256], small[64:80, 256:512]], 0)
+    misc = jnp.concatenate([misc, jnp.zeros((96, 256), F32)], 0)
+    out_ref[:, 1152:1280] = misc.T.astype(BF)
 
 
 def shaped(dims, kind):
     return jax.ShapeDtypeStruct(dims, kind)
 
 
-def run(kernel, args, places, outs, scratch, flops):
+def cost_of(micros):
+    return pl.CostEstimate(
+        flops=int(micros * 1.1535e9), bytes_accessed=int(micros * 3.0e6), transcendentals=0
+    )
+
+
+def run(kernel, args, places, outs, scratch, micros, after=()):
     space = {
         "s": pl.BlockSpec(memory_space=pltpu.SMEM),
         "v": pl.BlockSpec(memory_space=pltpu.VMEM),
         "a": pl.BlockSpec(memory_space=pl.ANY),
     }
+    count, extra = len(args), len(after)
+
+    def body(*refs):
+        kernel(*refs[:count], *refs[count + extra :])
+
     return pl.pallas_call(
-        kernel,
+        body,
         out_shape=outs,
-        in_specs=[space[p] for p in places],
+        in_specs=[space[p] for p in places] + [space["a"]] * extra,
         out_specs=jax.tree.map(lambda _: space["v"], outs),
         scratch_shapes=scratch,
         compiler_params=pltpu.CompilerParams(vmem_limit_bytes=VMEM_LIMIT),
-        cost_estimate=pl.CostEstimate(flops=flops, bytes_accessed=8 << 20, transcendentals=0),
-    )(*args)
+        cost_estimate=cost_of(micros),
+    )(*args, *after)
 
 
 def vm(*dims, kind=BF):
@@ -829,62 +829,54 @@
     return across(value, "section", 2, 1)
 
 
-def group_exchange(pieces):
-    return [pieces[0]] + [across(pieces[i], ("section", "mp"), 8, i) for i in range(1, 8)]
-
-
-def mp_exchange(pieces):
-    return [pieces[0]] + [across(pieces[b], "mp", 4, b) for b in range(1, 4)]
-
-
 def gathered(value):
-    return mp_exchange([value] * 4)
-
-
-def dp_sum(pieces):
-    come = [pieces[0]] + [across(pieces[k], "dp", 4, k) for k in range(1, 4)]
-    total = come[0].astype(F32)
-    for piece in come[1:]:
-        total = total + piece.astype(F32)
-    return total
-
-
-def add_shares(keeps, comes):
-    counts = tuple((4 if k.ndim == 3 else 1, k.shape[-1]) for k in keeps)
-    width = sum(c[1] for c in counts)
-    return run(
-        functools.partial(add_kernel, counts),
-        (*keeps, *comes),
-        "v" * (2 * len(keeps)),
-        [shaped((256, width), BF)] * 4,
-        [],
-        10**8,
-    )
-
-
-def sum_over_rows(ids, groups):
-    dp = lax.axis_size("dp")
-    width = sum(g[0].shape[1] for g in groups)
-    if dp == 4:
-        args = [piece for g in groups for piece in g]
-        pieces = run(
-            sum_kernel,
-            (ids, *args),
-            "s" + "v" * len(args),
-            [shaped((64, width), BF)] * 4,
-            [],
-            10**8,
-        )
-        return dp_sum(pieces)
-    totals = []
-    for group in groups:
-        total = group[0].astype(F32)
-        for piece in group[1:]:
-            total = total + piece.astype(F32)
-        totals.append(total)
-    quarter = jnp.concatenate(totals, 1).astype(BF).reshape(dp, 256 // dp, width)
-    come = lax.all_to_all(quarter, "dp", split_axis=0, concat_axis=0, tiled=True)
-    return jnp.sum(come.astype(F32), 0)
+    return [value] + [across(value, "mp", 4, b) for b in range(1, 4)]
+
+
+def to_all(value, axes):
+    return lax.all_to_all(value, axes, split_axis=0, concat_axis=0, tiled=True)
+
+
+def add_shares(keep, come, micros, after=()):
+    whole = pl.BlockSpec((1,) + keep.shape[1:], lambda i: (i, 0, 0))
+    return pl.pallas_call(
+        lambda k, c, *rest: add_kernel(k, c, rest[-1]),
+        out_shape=shaped(keep.shape, BF),
+        grid=(keep.shape[0],),
+        in_specs=[whole, whole] + [pl.BlockSpec(memory_space=pl.ANY)] * len(after),
+        out_specs=whole,
+        cost_estimate=cost_of(micros),
+    )(keep, come, *after)
+
+
+def add_two(keep, come, keep_s, come_s, after):
+    whole = pl.BlockSpec((1, 256, 256), lambda i: (i, 0, 0))
+    small = pl.BlockSpec((256, 256), lambda i: (0, 0))
+    return pl.pallas_call(
+        lambda k, c, ks, cs, *rest: add_two_kernel(k, c, ks, cs, rest[-1]),
+        out_shape=shaped((4, 256, 512), BF),
+        grid=(4,),
+        in_specs=[whole, whole, small, small] + [pl.BlockSpec(memory_space=pl.ANY)] * len(after),
+        out_specs=pl.BlockSpec((1, 256, 512), lambda i: (i, 0, 0)),
+        cost_estimate=cost_of(2.0),
+    )(keep, come, keep_s, come_s, *after)
+
+
+def gated(values, after):
+    anywhere = pl.BlockSpec(memory_space=pl.ANY)
+    count = len(values)
+    return pl.pallas_call(
+        lambda *refs: None,
+        out_shape=[shaped(v.shape, v.dtype) for v in values],
+        in_specs=[anywhere] * (count + len(after)),
+        out_specs=[anywhere] * count,
+        input_output_aliases={i: i for i in range(count)},
+        cost_estimate=cost_of(0.2),
+    )(*values, *after)
+
+
+def shared_out(value):
+    return lax.psum_scatter(value, "mp", scatter_dimension=0, tiled=False)
 
 
 def per_device(
@@ -905,17 +897,20 @@
     output_cross,
     cotangent,
 ):
-    sec, m, d = lax.axis_index("section"), lax.axis_index("mp"), lax.axis_index("dp")
+    sec, m = lax.axis_index("section"), lax.axis_index("mp")
     low = sec == 0
-    ids = jnp.stack([sec, m, d]).astype(jnp.int32)
-    sem = dma(40)
+    ids = jnp.stack([sec, m]).astype(jnp.int32)
+    sem = dma(24)
+    rowgroup = ("section", "mp")
 
     q_rows = query_self[0].transpose(0, 2, 1).reshape(128, 512)
     o_rows = output_self[0].reshape(128, 512)
-    c_rows = jnp.where(
-        low, query_cross.transpose(0, 2, 1).reshape(128, 512), output_cross.reshape(128, 512)
-    )
-    wa_own = gathered(jnp.concatenate([q_rows, o_rows, c_rows], 0))
+    wa = jnp.concatenate([q_rows, o_rows], 0)
+    wa_own = gathered(wa)
+    w_in, w_out = ffn_in[0], ffn_out[0]
+    half_come = swapped(jnp.where(low, w_out, w_in))
+    enc_half = jnp.where(low, w_in, half_come)
+    dec_half = jnp.where(low, half_come, w_out)
     kvw_own = keyval_self[0]
     kvw_oth = swapped(kvw_own)
     router_c = jnp.concatenate([jnp.zeros((8, 512), BF), router_cross.T], 0)
@@ -923,7 +918,6 @@
     packed = run(
         pack_kernel,
         (
-            ids,
             lengths[0, :, 0],
             inputs[0, :, 0],
             gains[0],
@@ -932,22 +926,23 @@
             routes_cross[:, 0].transpose(0, 2, 1),
             router_self[0].T,
         ),
-        "ssvvvvvv",
-        [shaped((176, 512), BF)] * 8,
-        [vm(4, 2, 128, 128), vm(16, 512, kind=F32)],
-        10**9,
-    )
-    pieces = group_exchange(packed)
+        "svvvvvv",
+        shaped((8, 176, 512), BF),
+        [vm(16, 512, kind=F32)],
+        3.4,
+        after=(wa,),
+    )
+    recv = to_all(packed, rowgroup)
     wa_oth = [swapped(piece) for piece in wa_own]
-
-    w_in, w_out = ffn_in[0], ffn_out[0]
-    half_come = swapped(jnp.where(low, w_out, w_in))
-    enc_own = gathered(jnp.where(low, w_in, half_come))
-    enc_oth = [swapped(piece) for piece in enc_own]
-    dec_own = gathered(jnp.where(low, half_come, w_out))
-    dec_oth = [swapped(piece) for piece in dec_own]
-    cot_cut = cotangent[:, 0].reshape(4, 2, 128, 512)
-    cots = mp_exchange([cot_cut[m ^ b, sec] for b in range(4)])
+    (enc_half,) = gated([enc_half], [packed, *wa_own[1:]])
+    enc_own = gathered(enc_half)
+    c_rows = jnp.where(
+        low, query_cross.transpose(0, 2, 1).reshape(128, 512), output_cross.reshape(128, 512)
+    )
+    cot_cut = lax.dynamic_index_in_dim(cotangent[:, 0].reshape(4, 2, 128, 512), sec, 1, False)
+    cc_in = jnp.concatenate([cot_cut, jnp.broadcast_to(c_rows[None], (4, 128, 512))], 1)
+    (cc_in,) = gated([cc_in], [recv])
+    cc_own = to_all(cc_in, "mp")
 
     act = shaped((2, TILE, 512), F32)
     actb = shaped((2, TILE, 512), BF)
@@ -957,9 +952,7 @@
     kv_f = shaped((4, 128, 128), F32)
     row_s = shaped((1, 512), F32)
     ffn_g = shaped((4, 256, 1024), BF)
-    att_g = shaped((4, 256, 256), BF)
-    flat_g = shaped((256, 256), BF)
-    lane_s = shaped((512, 128), F32)
+    router_s = shaped((32, 512), F32)
     wide = [vm(512, 512), vm(512, 512)]
     kv_scratch = [vm(4, 2, 128, 128), vm(1024, 128), vm(1024, 128)]
     back_scratch = [
@@ -968,68 +961,63 @@
     ]
     ffn_w = [vm(4, 512, 512), vm(4, 512, 512)]
 
-    recv, h1, g1, mixed_e, mixed_d, log_e, log_d = run(
+    h1, g1, mixed_e, mixed_d, log_e, log_d = run(
         self_fwd_kernel,
-        (ids, *pieces, *wa_own, *wa_oth, kvw_own, kvw_oth),
-        "s" + "a" * 18,
-        (shaped((8, 176, 512), BF), act, act, mixed_s, mixed_s, log_s, log_s),
+        (ids, recv, *wa_own, *wa_oth, kvw_own, kvw_oth),
+        "sv" + "a" * 10,
+        (act, act, mixed_s, mixed_s, log_s, log_s),
         [vm(2, 512, 512), vm(2, 512, 512), vm(2, 512, 128), vm(4, 2, 128, 128)]
         + [vm(2, 1024, 128), vm(2, 1024, 128), sem],
-        4 * 10**9,
-    )
+        13.6,
+    )
+    enc_own[1:] = gated(enc_own[1:], [h1])
+    enc_oth = [swapped(piece) for piece in enc_own]
+    (dec_half,) = gated([dec_half], [enc_own[1]])
+    dec_own = gathered(dec_half)
+    cc_oth = swapped(cc_own)
     h2, memory, kvm = run(
         enc_ffn_kernel,
-        (recv, h1, keyval_cross, ids, *enc_own, *enc_oth),
-        "vvvs" + "a" * 8,
+        (ids, recv, h1, keyval_cross, *enc_own, *enc_oth),
+        "svvv" + "a" * 8,
         (act, actb, kv_b),
         ffn_w + [vm(2, TILE, 512), sem],
-        4 * 10**9,
+        8.4,
     )
     kvm_oth = swapped(kvm)
     g2, mixed_c, log_c = run(
         cross_fwd_kernel,
-        (ids, recv, g1, kvm, kvm_oth, router_c, *wa_own, *wa_oth),
-        "svvvvv" + "a" * 8,
+        (ids, recv, g1, kvm, kvm_oth, router_c, cc_own, cc_oth),
+        "svvvvvaa",
         (act, mixed_s, log_s),
         wide + kv_scratch + [sem],
-        2 * 10**9,
-    )
-    dec_ffn = run(
+        8.8,
+    )
+    dec_own[1:] = gated(dec_own[1:], [g2])
+    dec_oth = [swapped(piece) for piece in dec_own]
+    outs, dg2, gain_d2, keep_d, send_d = run(
         dec_ffn_kernel,
-        (ids, recv, g2, memory, *cots, *dec_own, *dec_oth),
-        "svvv" + "a" * 12,
-        [shaped((128, 512), BF)] * 8 + [act, row_s, ffn_g, ffn_g],
+        (ids, recv, g2, memory, cc_own, *dec_own, *dec_oth),
+        "svvva" + "a" * 8,
+        (shaped((8, 128, 512), BF), act, row_s, ffn_g, ffn_g),
         ffn_w
         + [vm(4, 128, 512), vm(2, TILE, 512), vm(512, 512), vm(512, 512)]
         + [vm(2, TILE, 512, kind=F32), vm(512, 512, kind=F32), sem],
-        12 * 10**9,
-    )
-    out_pieces, (dg2, gain_d2, keep_d, send_d) = dec_ffn[:8], dec_ffn[8:]
+        15.0,
+    )
     come_d = swapped(send_d)
-    outs_come = group_exchange(out_pieces)
+    outs_come = to_all(outs, rowgroup)
+    att_g = shaped((4, 256, 256), BF)
+    flat_g = shaped((256, 256), BF)
     dg1, gain_d1, own_c, sendkv_c, router_cg, keep_wc, send_wc = run(
         cross_back_kernel,
-        (ids, recv, g1, dg2, mixed_c, log_c, kvm, kvm_oth, router_c, *wa_own, *wa_oth),
-        "svvvvvvvv" + "a" * 8,
-        (act, row_s, kv_f, kv_b, lane_s, att_g, att_g),
+        (ids, recv, g1, dg2, mixed_c, log_c, kvm, kvm_oth, router_c, cc_own, cc_oth),
+        "svvvvvvvvaa",
+        (act, row_s, kv_f, kv_b, router_s, att_g, att_g),
         wide + kv_scratch + back_scratch + [sem],
-        4 * 10**9,
+        13.0,
     )
     comekv_c = swapped(sendkv_c)
-    come_wc = swapped(send_wc)
-    ffn_d_parts = mp_exchange(add_shares([keep_d], [come_d]))
-    self_scratch = wide + [vm(512, 128)] + kv_scratch + back_scratch + [sem]
-    self_outs = (act, kv_f, kv_b, lane_s, att_g, att_g)
-    df1, own_1, sendkv_1, router_1g, keep_w1, send_w1 = run(
-        functools.partial(self_back_kernel, 1),
-        (ids, recv, dg1, mixed_d, log_d, *wa_own, *wa_oth, kvw_own, kvw_oth),
-        "svvvv" + "a" * 10,
-        self_outs,
-        self_scratch,
-        4 * 10**9,
-    )
-    comekv_1 = swapped(sendkv_1)
-    come_w1 = swapped(send_w1)
+    ffn_d = add_shares(keep_d, come_d, 4.0, (dg1, outs_come))
     dh1, gain_e1, gain_e2, keep_e, send_e = run(
         enc_ffn_back_kernel,
         (ids, recv, h1, h2, own_c, comekv_c, keyval_cross, *enc_own, *enc_oth),
@@ -1038,91 +1026,105 @@
         ffn_w
         + [vm(2, TILE, 512), vm(512, 512), vm(2, TILE, 512), vm(512, 512)]
         + [vm(512, 512, kind=F32), sem],
-        12 * 10**9,
-    )
+        13.4,
+        after=(ffn_d,),
+    )
+    ffn_d = shared_out(ffn_d)
     come_e = swapped(send_e)
+    self_scratch = wide + [vm(512, 128)] + kv_scratch + back_scratch + [sem]
+    att_dg = shaped((4, 256, 512), BF)
+    df1, own_1, sendkv_1, router_1g, keep_w1, send_w1 = run(
+        functools.partial(self_back_kernel, 1),
+        (
+            ids, recv, dg1, mixed_d, log_d, *wa_own, *wa_oth, kvw_own, kvw_oth, keep_wc, send_wc,
+        ),
+        "svvvv" + "a" * 12,
+        (act, kv_f, kv_b, router_s, att_dg, att_dg),
+        self_scratch,
+        12.2,
+        after=(dh1,),
+    )
+    comekv_1 = swapped(sendkv_1)
+    come_w1 = swapped(send_w1)
+    ffn_e = add_shares(keep_e, come_e, 4.0, (df1,))
+    att_d = add_shares(keep_w1, come_w1, 2.0, (ffn_e,))
     dx1, gain_d0, keep_s1, send_s1 = run(
         dec_finish_kernel,
         (ids, recv, dg1, df1, own_1, comekv_1, own_c, comekv_c, memory, kvw_own, kvw_oth),
         "svvvvvvvvaa",
-        (actb, row_s, flat_g, flat_g),
+        (shaped((4, 128, 512), BF), row_s, flat_g, flat_g),
         [vm(512, 128), vm(2, TILE, 512), sem],
-        10**9,
-    )
+        5.5,
+        after=(att_d,),
+    )
+    ffn_e = shared_out(ffn_e)
+    att_d = to_all(att_d, "mp")
+    ffn_d = lax.psum_scatter(ffn_d, "dp", scatter_dimension=0, tiled=True).astype(F32)
     come_s1 = swapped(send_s1)
     df0, own_0, sendkv_0, router_0g, keep_w0, send_w0 = run(
         functools.partial(self_back_kernel, 0),
         (ids, recv, dh1, mixed_e, log_e, *wa_own, *wa_oth, kvw_own, kvw_oth),
         "svvvv" + "a" * 10,
-        self_outs,
+        (act, kv_f, kv_b, router_s, att_g, att_g),
         self_scratch,
-        4 * 10**9,
+        11.8,
+        after=(dx1,),
     )
     comekv_0 = swapped(sendkv_0)
     come_w0 = swapped(send_w0)
-    ffn_e_parts = mp_exchange(add_shares([keep_e], [come_e]))
-    att_d_parts = mp_exchange(
-        add_shares([keep_wc, keep_w1, keep_s1], [come_wc, come_w1, come_s1])
-    )
-    finish = run(
+    ffn_e = lax.psum_scatter(ffn_e, "dp", scatter_dimension=0, tiled=True).astype(F32)
+    att_e = to_all(add_two(keep_w0, come_w0, keep_s1, come_s1, (att_d,)), "mp")
+    finished = run(
         enc_finish_kernel,
         (
             ids, recv, dh1, df0, own_0, comekv_0, dx1, router_0g, router_1g, router_cg,
             gain_e1, gain_e2, gain_d0, gain_d1, gain_d2, kvw_own, kvw_oth,
         ),
         "s" + "v" * 14 + "aa",
-        [shaped((128, 512), BF)] * 8 + [flat_g, flat_g],
-        [vm(512, 128), vm(2, TILE, 512), vm(2, TILE, 512), sem],
-        10**9,
-    )
-    dx_pieces, (keep_s0, send_s0) = finish[:8], finish[8:]
-    come_s0 = swapped(send_s0)
-    dx_come = group_exchange(dx_pieces)
-    att_e_parts = mp_exchange(add_shares([keep_w0, keep_s0], [come_w0, come_s0]))
-
-    ffn_dec = sum_over_rows(ids, [ffn_d_parts])
-    att_dec = sum_over_rows(ids, [att_d_parts])
-    ffn_enc = sum_over_rows(ids, [ffn_e_parts])
-    att_enc = sum_over_rows(ids, [att_e_parts])
-
-    def placed(come, kind):
-        whole = run(
-            place_kernel,
-            (ids, *come),
-            "s" + "a" * 8,
-            shaped((4, 2, 128, 512), kind),
-            [vm(8, 128, 512), dma(8)],
-            10**8,
-        )
-        return whole.reshape(1, 4, 1, 256, 512)
-
-    share = att_enc.shape[0]
-
-    def query_of(value, at):
-        return value[:, at : at + 128].reshape(share, 2, 64).transpose(1, 0, 2)
-
-    def output_of(value, at):
-        return value[:, at : at + 128].T.reshape(2, 64, share)
-
-    misc = att_enc[:, 384:512]
+        shaped((8, 208, 512), BF),
+        [vm(512, 128), vm(2, TILE, 512), vm(32, 512, kind=F32), sem],
+        6.0,
+    )
+    dx, small = run(
+        tail_kernel,
+        (to_all(finished, rowgroup), att_d, att_e),
+        "vvv",
+        (shaped((4, 2, 128, 512), F32), shaped((256, 1280), BF)),
+        [],
+        3.0,
+    )
+    dp = lax.axis_size("dp")
+    share = 256 // dp
+    small = to_all(small.reshape(dp, share, 1280), "dp")
+    small = jnp.sum(small.astype(F32), 0)
+
+    outs_come = outs_come.reshape(2, 4, 128, 512).transpose(1, 0, 2, 3)
+
+    def query_of(at):
+        return small[:, at : at + 128].reshape(share, 2, 64).transpose(1, 0, 2)
+
+    def output_of(at):
+        return small[:, at + 128 : at + 256].T.reshape(2, 64, share)
+
+    misc = small[:, 1152:1280].T
 
     def router_of(layer):
-        return misc[:, ROUTER_LANES[layer] : ROUTER_LANES[layer] + 8]
+        return misc[ROUTER_LANES[layer] : ROUTER_LANES[layer] + 8].T
 
     return (
-        placed(outs_come, BF),
-        placed(dx_come, F32),
-        misc[:, GAIN_LANE : GAIN_LANE + 6].T.reshape(2, 3, share),
+        outs_come.reshape(1, 4, 1, 256, 512),
+        dx.reshape(1, 4, 1, 256, 512),
+        misc[GAIN_ROW : GAIN_ROW + 6].reshape(2, 3, share),
         jnp.stack([router_of(0), router_of(1)]),
-        jnp.stack([query_of(att_enc, 0), query_of(att_dec, 256)]),
-        jnp.stack([att_enc[:, 256:384], att_dec[:, 512:640]]),
-        jnp.stack([output_of(att_enc, 128), output_of(att_dec, 384)]),
-        jnp.stack([ffn_enc[:, :512], ffn_dec[:, :512]]),
-        jnp.stack([ffn_enc[:, 512:].T, ffn_dec[:, 512:].T]),
+        jnp.stack([query_of(512), query_of(256)]),
+        jnp.stack([small[:, 1024:1152], small[:, 768:896]]),
+        jnp.stack([output_of(512), output_of(256)]),
+        jnp.stack([ffn_e[:, :512], ffn_d[:, :512]]),
+        jnp.stack([ffn_e[:, 512:].T, ffn_d[:, 512:].T]),
         router_of(2),
-        query_of(att_dec, 0),
-        att_dec[:, 640:768],
-        output_of(att_dec, 128),
+        query_of(0),
+        small[:, 896:1024],
+        output_of(0),
     )
 
 

time: 379 us -> 373 us (0.984)
  starting transfers between devices: 77.6 us -> 41.4 us
  blocking collectives: 0 us -> 26.5 us
  between operations: 1.8 us -> 14.4 us
  Pallas kernels: 142 us -> 131 us
  waiting for transfers between devices: 132 us -> 125 us
  other arithmetic: 6.32 us -> 13.2 us
  local copies, waits for them, and re-layouts: 14 us -> 18.4 us
    ppermute x82 -> x33, waiting for transfers between devices: 132 us -> 66.9 us  [across(): return lax.ppermute(value, axes, [(i, i ^ by) for i in range(size)])]
    ppermute x82 -> x33, starting transfers between devices: 77.6 us -> 16.2 us  [across(): return lax.ppermute(value, axes, [(i, i ^ by) for i in range(size)])]
    all_to_all x0 -> x6, waiting for transfers between devices: none -> 39.6 us  [to_all(): return lax.all_to_all(value, axes, split_axis=0, concat_axis=0, tiled=True)]
    all_to_all x0 -> x1, blocking collectives: none -> 26.5 us  [to_all(): return lax.all_to_all(value, axes, split_axis=0, concat_axis=0, tiled=True)]
    all_to_all x0 -> x6, starting transfers between devices: none -> 25 us  [to_all(): return lax.all_to_all(value, axes, split_axis=0, concat_axis=0, tiled=True)]
    reduce_scatter x0 -> x2, waiting for transfers between devices: none -> 17.4 us  [the longest x1 17.4 us: per_device(): lax.psum_scatter(ffn_e, 'dp', scatter_dimension=0, tiled=True).astype(F32)]
    pallas_call x21, Pallas kernels: 142 us -> 131 us  [the longest x12 115 us: run(): pl.pallas_call(body, out_shape=outs, in_specs=[space[p] for p in places]...]
    unnamed x177 -> x77, local copies, waits for them, and re-layouts: 9.44 us -> 14.5 us
  transfers between devices with their start and end apart: 82 -> 43, of which waited for: 24 -> 21; matrix products, arithmetic and copies ran while one was open for 3% -> 4% of each run, Pallas kernels for 34% -> 29%
where the time goes in v3:
time: 373 us; the launch traced here: 369 us
  Pallas kernels  131 us (35%)
  waiting for transfers between devices  125 us (34%)
  starting transfers between devices  41.4 us (11%)
  blocking collectives  26.5 us (7%)
  local copies, waits for them, and re-layouts  18.4 us (5%)
  between operations  14.4 us (4%)
  other arithmetic  13.2 us (4%)
    pallas_call x12, Pallas kernels, run(): pl.pallas_call(body, out_shape=outs, in_specs=[space[p] for p in places]...  115 us
    ppermute x33, waiting for transfers between devices, across(): return lax.ppermute(value, axes, [(i, i ^ by) for i in range(size)])  66.9 us
    all_to_all x6, waiting for transfers between devices, to_all(): return lax.all_to_all(value, axes, split_axis=0, concat_axis=0, tiled=True)  39.6 us
    all_to_all x1, blocking collectives, to_all(): return lax.all_to_all(value, axes, split_axis=0, concat_axis=0, tiled=True)  26.5 us
    all_to_all x6, starting transfers between devices, to_all(): return lax.all_to_all(value, axes, split_axis=0, concat_axis=0, tiled=True)  25 us
    reduce_scatter x1, waiting for transfers between devices, per_device(): lax.psum_scatter(ffn_e, 'dp', scatter_dimension=0, tiled=True).astype(F32)  17.4 us
    ppermute x33, starting transfers between devices, across(): return lax.ppermute(value, axes, [(i, i ^ by) for i in range(size)])  16.2 us
    unnamed x77, local copies, waits for them, and re-layouts  14.5 us
  transfers between devices with their start and end apart: 43, of which 21 were waited for; matrix products, arithmetic and copies ran while one was open for 4% of the time, Pallas kernels for 29%

profile of v3, /device:TPU:0, one launch (start us, length us, event | category | flops | bytes accessed | tf_op | source)
XLA Modules:
  0.0 369.3 jit_solution(1144909441141698980)
XLA Ops:
  12.3 5.3 %all-to-all-start = ((bf16[8,176,512]{2,1,0:T(8,128)(2,1)}), bf16[8,176,512]{2,1,0:T(8,128)(2,1)S(1)}, u32[]{:S(2)}, u32[]{:S(2)}) async-start(bf16[8,176,512]{2,1,0:T(8,128)(2,1)} %shard_map.255.refs_1_), calls=%async_computation | async-start | bytes 2883584 | tf_op jit(solution)/shard_map/all_to_all | solution.py:837
  25.1 18.3 %collective-permute-done.2.refs_5_.refs_4_.refs_8_ = bf16[256,512]{1,0:T(8,128)(2,1)} collective-permute-done((bf16[256,512]{1,0:T(8,128)(2,1)}, bf16[256,512]{1,0:T(8,128)(2,1)}, u32[]{:S(2)}, u32[]{:S(2)}) %collective-permute-start.2) | collective-permute-done | bytes 262176 | tf_op jit(solution)/shard_map/ppermute | solution.py:825
  43.4 4.2 %collective-permute-done.1.refs_4_.refs_3_.refs_7_ = bf16[256,512]{1,0:T(8,128)(2,1)} collective-permute-done((bf16[256,512]{1,0:T(8,128)(2,1)}, bf16[256,512]{1,0:T(8,128)(2,1)}, u32[]{:S(2)}, u32[]{:S(2)}) %collective-permute-start.1) | collective-permute-done | bytes 262176 | tf_op jit(solution)/shard_map/ppermute | solution.py:825
  59.6 13.5 %shard_map.256 = (f32[2,256,512]{2,1,0:T(8,128)}, f32[2,256,512]{2,1,0:T(8,128)}, f32[2,512,128]{2,1,0:T(8,128)}, f32[2,512,128]{2,1,0:T(8,128)}, f32[2,1,512]{2,1,0:T(1,128)}, /*index=5*/f32[2,1,512]{2,1,0:T(1,128)}) custom-call(s32[2]{0:T(128)} %pad_add_fusion.refs_0_, bf16[8,176,512]{2,1,0:T(8,128)(2,1)} %copy-done.2, ...), custom_call_target="tpu_custom_call" | custom-call | flops 15687600128 | bytes 40800000 | tf_op jit(solution)/shard_map/pallas_call | solution.py:805
  73.1 9.5 %collective-permute-done.11.refs_2_ = bf16[512,512]{1,0:T(8,128)(2,1)S(1)} collective-permute-done((bf16[512,512]{1,0:T(8,128)(2,1)S(1)}, bf16[512,512]{1,0:T(8,128)(2,1)S(1)}, u32[]{:S(2)}, u32[]{:S(2)}) %collective-permute-start.11) | collective-permute-done | bytes 524320 | tf_op jit(solution)/shard_map/ppermute | solution.py:825
  82.6 9.8 %collective-permute-done.10.refs_1_ = bf16[512,512]{1,0:T(8,128)(2,1)S(1)} collective-permute-done((bf16[512,512]{1,0:T(8,128)(2,1)S(1)}, bf16[512,512]{1,0:T(8,128)(2,1)S(1)}, u32[]{:S(2)}, u32[]{:S(2)}) %collective-permute-start.10) | collective-permute-done | bytes 524320 | tf_op jit(solution)/shard_map/ppermute | solution.py:825
  99.4 8.3 %shard_map.259 = (f32[2,256,512]{2,1,0:T(8,128)}, bf16[2,256,512]{2,1,0:T(8,128)(2,1)}, bf16[4,128,128]{2,1,0:T(8,128)(2,1)}) custom-call(s32[2]{0:T(128)} %pad_add_fusion.refs_0_, bf16[8,176,512]{2,1,0:T(8,128)(2,1)} %copy-done.2, f32[2,256,512]{2,1,0:T(8,128)} %get-tuple-element.67.refs_3_.refs_2_, bf16[512,128]{1,0:T(8,128)(2,1)} %refs_6_.1, ...), custom_call_target="tpu_custom_call" | custom-call | flops 9689400320 | bytes 25200000 | tf_op jit(solution)/shard_map/pallas_call | solution.py:805
  112.5 8.9 %shard_map.261 = (f32[2,256,512]{2,1,0:T(8,128)}, f32[2,512,128]{2,1,0:T(8,128)}, f32[2,1,512]{2,1,0:T(1,128)}) custom-call(s32[2]{0:T(128)} %pad_add_fusion.refs_0_, bf16[8,176,512]{2,1,0:T(8,128)(2,1)} %copy-done.2, f32[2,256,512]{2,1,0:T(8,128)} %get-tuple-element.66.refs_2_, bf16[4,128,128]{2,1,0:T(8,128)(2,1)} %get-tuple-element.71.refs_3_.refs_6_, ...), custom_call_target="tpu_custom_call" | custom-call | flops 10150800384 | bytes 26400000 | tf_op jit(solution)/shard_map/pallas_call | solution.py:805
  124.9 10.4 %collective-permute-done.19.refs_1_ = bf16[512,512]{1,0:T(8,128)(2,1)S(1)} collective-permute-done((bf16[512,512]{1,0:T(8,128)(2,1)}, bf16[512,512]{1,0:T(8,128)(2,1)S(1)}, u32[]{:S(2)}, u32[]{:S(2)}) %collective-permute-start.19) | collective-permute-done | bytes 524320 | tf_op jit(solution)/shard_map/ppermute | solution.py:825
  140.6 14.6 %shard_map.264 = (bf16[8,128,512]{2,1,0:T(8,128)(2,1)}, f32[2,256,512]{2,1,0:T(8,128)}, f32[1,512]{1,0:T(1,128)}, bf16[4,256,1024]{2,1,0:T(8,128)(2,1)}, bf16[4,256,1024]{2,1,0:T(8,128)(2,1)}) custom-call(s32[2]{0:T(128)} %pad_add_fusion.refs_0_, bf16[8,176,512]{2,1,0:T(8,128)(2,1)} %copy-done.2, f32[2,256,512]{2,1,0:T(8,128)} %get-tuple-element.72.refs_3_.refs_2_, ...), custom_call_target="tpu_custom_call" | custom-call | flops 17302499328 | bytes 45000000 | tf_op jit(solution)/shard_map/pallas_call | solution.py:805
  159.1 12.7 %shard_map.265 = (f32[2,256,512]{2,1,0:T(8,128)}, f32[1,512]{1,0:T(1,128)}, f32[4,128,128]{2,1,0:T(8,128)}, bf16[4,128,128]{2,1,0:T(8,128)(2,1)}, f32[32,512]{1,...) custom-call(s32[2]{0:T(128)} %pad_add_fusion.refs_0_, bf16[8,176,512]{2,1,0:T(8,128)(2,1)} %copy-done.2, ...), custom_call_target="tpu_custom_call" | custom-call | flops 14995500032 | bytes 39000000 | tf_op jit(solution)/shard_map/pallas_call | solution.py:805
  175.5 4.3 %shard_map.266.refs_15_ = bf16[4,256,1024]{2,1,0:T(8,128)(2,1)} custom-call(bf16[4,256,1024]{2,1,0:T(8,128)(2,1)} %get-tuple-element.84.k, bf16[4,256,1024]{2,1,0:T(8,128)(2,1)} %copy-done.18, f32[2,256,512]{2,1,0:T(8,128)} %get-tuple-element.86.rest_0_.refs_2_, bf16[8,128,512]{2,1,0:T(8,128)(2,1)} %copy-done.3), custom_call_target="tpu_custom_call" | custom-call | flops 4614000128 | bytes 12000000 | tf_op jit(solution)/shard_map/pallas_call | solution.py:842
  182.7 13.9 %shard_map.267 = (f32[2,256,512]{2,1,0:T(8,128)}, f32[1,512]{1,0:T(1,128)}, f32[1,512]{1,0:T(1,128)}, bf16[4,256,1024]{2,1,0:T(8,128)(2,1)}, bf16[4,256,1024]{2,1,0:T(8,128)(2,1)}) custom-call(s32[2]{0:T(128)} %pad_add_fusion.refs_0_, bf16[8,176,512]{2,1,0:T(8,128)(2,1)} %copy-done.2, f32[2,256,512]{2,1,0:T(8,128)} %get-tuple-element.67.refs_3_.refs_2_, ...), custom_call_target="tpu_custom_call" | custom-call | flops 15456900096 | bytes 40200000 | tf_op jit(solution)/shard_map/pallas_call | solution.py:805
  197.0 12.4 %shard_map.268 = (f32[2,256,512]{2,1,0:T(8,128)}, f32[4,128,128]{2,1,0:T(8,128)}, bf16[4,128,128]{2,1,0:T(8,128)(2,1)}, f32[32,512]{1,0:T(8,128)}, bf16[4,256,51...) custom-call(s32[2]{0:T(128)} %pad_add_fusion.refs_0_, bf16[8,176,512]{2,1,0:T(8,128)(2,1)} %copy-done.2, ...), custom_call_target="tpu_custom_call" | custom-call | flops 14072699904 | bytes 36600000 | tf_op jit(solution)/shard_map/pallas_call | solution.py:805
  211.4 4.3 %shard_map.269.rest_0_ = bf16[4,256,1024]{2,1,0:T(8,128)(2,1)} custom-call(bf16[4,256,1024]{2,1,0:T(8,128)(2,1)} %get-tuple-element.99.k, bf16[4,256,1024]{2,1,0:T(8,128)(2,1)} %copy-done.19, f32[2,256,512]{2,1,0:T(8,128)} %get-tuple-element.94.rest_0_.refs_3_), custom_call_target="tpu_custom_call" | custom-call | flops 4614000128 | bytes 12000000 | tf_op jit(solution)/shard_map/pallas_call | solution.py:842
  224.8 5.3 %shard_map.271 = (bf16[4,128,512]{2,1,0:T(8,128)(2,1)}, f32[1,512]{1,0:T(1,128)}, bf16[256,256]{1,0:T(8,128)(2,1)}, bf16[256,256]{1,0:T(8,128)(2,1)}) custom-call(s32[2]{0:T(128)} %pad_add_fusion.refs_0_, bf16[8,176,512]{2,1,0:T(8,128)(2,1)} %copy-done.2, f32[2,256,512]{2,1,0:T(8,128)} %get-tuple-element.86.rest_0_.refs_2_, ...), custom_call_target="tpu_custom_call" | custom-call | flops 6344249856 | bytes 16500000 | tf_op jit(solution)/shard_map/pallas_call | solution.py:805
  230.1 11.9 %shard_map.272 = (f32[2,256,512]{2,1,0:T(8,128)}, f32[4,128,128]{2,1,0:T(8,128)}, bf16[4,128,128]{2,1,0:T(8,128)(2,1)}, f32[32,512]{1,0:T(8,128)}, bf16[4,256,25...) custom-call(s32[2]{0:T(128)} %pad_add_fusion.refs_0_, bf16[8,176,512]{2,1,0:T(8,128)(2,1)} %copy-done.2, ...), custom_call_target="tpu_custom_call" | custom-call | flops 13611299840 | bytes 35400000 | tf_op jit(solution)/shard_map/pallas_call | solution.py:805
  244.3 5.1 %all-to-all-done.4.rest_0_.refs_1_ = bf16[4,256,512]{2,1,0:T(8,128)(2,1)S(1)} async-done(((bf16[4,256,512]{2,1,0:T(8,128)(2,1)}), bf16[4,256,512]{2,1,0:T(8,128)(2,1)S(1)}, u32[]{:S(2)}, u32[]{:S(2)}) %all-to-all-start.4) | async-done | bytes 1048608 | tf_op jit(solution)/shard_map/all_to_all | solution.py:837
  259.7 5.9 %shard_map.273 = bf16[8,208,512]{2,1,0:T(8,128)(2,1)} custom-call(s32[2]{0:T(128)} %pad_add_fusion.refs_0_, bf16[8,176,512]{2,1,0:T(8,128)(2,1)} %copy-done.2, f32[2,256,512]{2,1,0:T(8,128)} %get-tuple-element.87.refs_17_.refs_2_, f32[2,256,512]{2,1,0:T(8,128)} %get-tuple-element.102.refs_3_, f32[4,128,128]{2,1,0:T(8,128)} %get-tuple-element.103.refs_4_, ...), custom_call_target="tpu_custom_call" | custom-call | flops 6920999936 | bytes 18000000 | tf_op jit(solution)/shard_map/pallas_call | solution.py:805
  265.6 9.2 %all-to-all-done.5.refs_2_ = bf16[4,256,512]{2,1,0:T(8,128)(2,1)S(1)} async-done(((bf16[4,256,512]{2,1,0:T(8,128)(2,1)}), bf16[4,256,512]{2,1,0:T(8,128)(2,1)S(1)}, u32[]{:S(2)}, u32[]{:S(2)}) %all-to-all-start.5) | async-done | bytes 1048608 | tf_op jit(solution)/shard_map/all_to_all | solution.py:837
  274.7 26.5 %all_to_all.35.refs_0_ = bf16[8,208,512]{2,1,0:T(8,128)(2,1)} all-to-all(bf16[8,208,512]{2,1,0:T(8,128)(2,1)} %shard_map.273), channel_id=1, replica_groups=mesh['section'=2,'dp'=4,'mp'=4] {'section','mp'}, dimensions={0} | all-to-all | bytes 3407872 | tf_op jit(solution)/shard_map/all_to_all | solution.py:837
  305.0 4.7 %all-to-all-start.6 = ((bf16[4,64,1280]{2,1,0:T(8,128)(2,1)}), bf16[4,64,1280]{2,1,0:T(8,128)(2,1)S(1)}, u32[]{:S(2)}, u32[]{:S(2)}) async-start(bf16[4,64,1280]{2,1,0:T(8,128)(2,1)} %bitcast.98), calls=%async_computation.6 | async-start | bytes 1310720 | tf_op jit(solution)/shard_map/all_to_all | solution.py:837
  311.6 23.3 %all-to-all-done.6 = bf16[4,64,1280]{2,1,0:T(8,128)(2,1)S(1)} async-done(((bf16[4,64,1280]{2,1,0:T(8,128)(2,1)}), bf16[4,64,1280]{2,1,0:T(8,128)(2,1)S(1)}, u32[]{:S(2)}, u32[]{:S(2)}) %all-to-all-start.6) | async-done | bytes 655392 | tf_op jit(solution)/shard_map/all_to_all | solution.py:837
  342.7 17.4 %reduce-scatter.9.cloned.1.call-done = bf16[64,1024]{1,0:T(8,128)(2,1)} async-done(((bf16[256,1024]{1,0:T(8,128)(2,1)}), bf16[64,1024]{1,0:T(8,128)(2,1)}) %reduce-scatter.9.cloned.1.call-update) | async-done | bytes 131088 | tf_op jit(solution)/shard_map/reduce_scatter | solution.py:1075
  (200 shorter events, 94.9 us)
Async XLA Ops:
  12.3 38.0 %all-to-all-start = ((bf16[8,176,512]{2,1,0:T(8,128)(2,1)}), bf16[8,176,512]{2,1,0:T(8,128)(2,1)S(1)}, u32[]{:S(2)}, u32[]{:S(2)}) async-start(bf16[8,176,512]{2,1,0:T(8,128)(2,1)} %shard_map.255.refs_1_), calls=%async_computation | async-start | bytes 2883584 | tf_op jit(solution)/shard_map/all_to_all | solution.py:837
  17.6 37.9 %collective-permute-start.7 = (bf16[512,128]{1,0:T(8,128)(2,1)}, bf16[512,128]{1,0:T(8,128)(2,1)}, u32[]{:S(2)}, u32[]{:S(2)}) collective-permute-start(bf16[512,128]{1,0:T(8,128)(2,1)} %bitcast.111), channel_id=1, source_target_pairs={{0,16},{16,0},{1,17},{17,1},{2,18},{18,2},{3,19},{19,3},{4,20},{20... | collective-permute-start | bytes 393224 | tf_op jit(solution)/shard_map/ppermute | solution.py:825
  18.1 25.3 %collective-permute-start.2 = (bf16[256,512]{1,0:T(8,128)(2,1)}, bf16[256,512]{1,0:T(8,128)(2,1)}, u32[]{:S(2)}, u32[]{:S(2)}) collective-permute-start(bf16[256,512]{1,0:T(8,128)(2,1)} %pad_maximum_fusion.1.refs_7_.refs_2_.refs_5_), channel_id=1, source_target_pairs={{0,3},{1,2},{2,1},{3,0},{4,7},{5,6},{6,5},{7,4},{8,11},{9,10},{10,... | collective-permute-start | bytes 786440 | tf_op jit(solution)/shard_map/ppermute | solution.py:825
  20.7 26.9 %collective-permute-start.1 = (bf16[256,512]{1,0:T(8,128)(2,1)}, bf16[256,512]{1,0:T(8,128)(2,1)}, u32[]{:S(2)}, u32[]{:S(2)}) collective-permute-start(bf16[256,512]{1,0:T(8,128)(2,1)} %pad_maximum_fusion.1.refs_7_.refs_2_.refs_5_), channel_id=1, source_target_pairs={{0,2},{1,3},{2,0},{3,1},{4,6},{5,7},{6,4},{7,5},{8,10},{9,11},{10,... | collective-permute-start | bytes 786440 | tf_op jit(solution)/shard_map/ppermute | solution.py:825
  21.2 26.4 %collective-permute-start = (bf16[256,512]{1,0:T(8,128)(2,1)}, bf16[256,512]{1,0:T(8,128)(2,1)}, u32[]{:S(2)}, u32[]{:S(2)}) collective-permute-start(bf16[256,512]{1,0:T(8,128)(2,1)} %pad_maximum_fusion.1.refs_7_.refs_2_.refs_5_), channel_id=1, source_target_pairs={{0,1},{1,0},{2,3},{3,2},{4,5},{5,4},{6,7},{7,6},{8,9},{9,8},{10,11... | collective-permute-start | bytes 786440 | tf_op jit(solution)/shard_map/ppermute | solution.py:825
  22.4 25.7 %collective-permute-start.8 = (bf16[512,512]{1,0:T(8,128)(2,1)}, bf16[512,512]{1,0:T(8,128)(2,1)}, u32[]{:S(2)}, u32[]{:S(2)}) collective-permute-start(bf16[512,512]{1,0:T(8,128)(2,1)} %bitcast_select_fusion.1), channel_id=1, source_target_pairs={{0,16},{16,0},{1,17},{17,1},{2,18},{18,2},{3,19},{19,3},{4,20},{20... | collective-permute-start | bytes 1572872 | tf_op jit(solution)/shard_map/ppermute | solution.py:825
  51.5 42.4 %all-to-all-start.1 = ((bf16[4,256,512]{2,1,0:T(8,128)(2,1)}), bf16[4,256,512]{2,1,0:T(8,128)(2,1)S(1)}, u32[]{:S(2)}, u32[]{:S(2)}) async-start(bf16[4,256,512]{2,1,0:T(8,128)(2,1)} %shard_map.260), calls=%async_computation.1 | async-start | bytes 2097152 | tf_op jit(solution)/shard_map/all_to_all | solution.py:837
  55.5 38.9 %collective-permute-start.12 = (bf16[512,512]{1,0:T(8,128)(2,1)S(1)}, bf16[512,512]{1,0:T(8,128)(2,1)}, u32[]{:S(2)}, u32[]{:S(2)}) collective-permute-start(bf16[512,512]{1,0:T(8,128)(2,1)S(1)} %copy-done.6), channel_id=1, source_target_pairs={{0,16},{16,0},{1,17},{17,1},{2,18},{18,2},{3,19},{19,3},{4,20},{20... | collective-permute-start | bytes 1572872 | tf_op jit(solution)/shard_map/ppermute | solution.py:825
  56.1 26.6 %collective-permute-start.11 = (bf16[512,512]{1,0:T(8,128)(2,1)S(1)}, bf16[512,512]{1,0:T(8,128)(2,1)S(1)}, u32[]{:S(2)}, u32[]{:S(2)}) collective-permute-start(bf16[512,512]{1,0:T(8,128)(2,1)S(1)} %copy-done.6), channel_id=1, source_target_pairs={{0,3},{1,2},{2,1},{3,0},{4,7},{5,6},{6,5},{7,4},{8,11},{9,10},{10,... | collective-permute-start | bytes 1572872 | tf_op jit(solution)/shard_map/ppermute | solution.py:825
  58.7 33.8 %collective-permute-start.10 = (bf16[512,512]{1,0:T(8,128)(2,1)S(1)}, bf16[512,512]{1,0:T(8,128)(2,1)S(1)}, u32[]{:S(2)}, u32[]{:S(2)}) collective-permute-start(bf16[512,512]{1,0:T(8,128)(2,1)S(1)} %copy-done.6), channel_id=1, source_target_pairs={{0,2},{1,3},{2,0},{3,1},{4,6},{5,7},{6,4},{7,5},{8,10},{9,11},{10,... | collective-permute-start | bytes 1572872 | tf_op jit(solution)/shard_map/ppermute | solution.py:825
  59.2 33.3 %collective-permute-start.9 = (bf16[512,512]{1,0:T(8,128)(2,1)S(1)}, bf16[512,512]{1,0:T(8,128)(2,1)S(1)}, u32[]{:S(2)}, u32[]{:S(2)}) collective-permute-start(bf16[512,512]{1,0:T(8,128)(2,1)S(1)} %copy-done.6), channel_id=1, source_target_pairs={{0,1},{1,0},{2,3},{3,2},{4,5},{5,4},{6,7},{7,6},{8,9},{9,8},{10,11... | collective-permute-start | bytes 1572872 | tf_op jit(solution)/shard_map/ppermute | solution.py:825
  93.9 18.5 %collective-permute-start.17 = (bf16[4,256,512]{2,1,0:T(8,128)(2,1)S(1)}, bf16[4,256,512]{2,1,0:T(8,128)(2,1)}, u32[]{:S(2)}, u32[]{:S(2)}) collective-permute-start(bf16[4,256,512]{2,1,0:T(8,128)(2,1)S(1)} %all-to-all-done.1.refs_6_.refs_4_.refs_9_), channel_id=1, source_target_pairs={{0,16},{16,0},{1,17},{17,1},{2,18},{18,2},{3,19},{19,3},{4,20},{20... | collective-permute-start | bytes 3145736 | tf_op jit(solution)/shard_map/ppermute | solution.py:825
  108.6 28.2 %collective-permute-start.21 = (bf16[512,512]{1,0:T(8,128)(2,1)}, bf16[512,512]{1,0:T(8,128)(2,1)S(1)}, u32[]{:S(2)}, u32[]{:S(2)}) collective-permute-start(bf16[512,512]{1,0:T(8,128)(2,1)} %shard_map.262.refs_5_), channel_id=1, source_target_pairs={{0,16},{16,0},{1,17},{17,1},{2,18},{18,2},{3,19},{19,3},{4,20},{20... | collective-permute-start | bytes 1572872 | tf_op jit(solution)/shard_map/ppermute | solution.py:825
  110.4 24.8 %collective-permute-start.19 = (bf16[512,512]{1,0:T(8,128)(2,1)}, bf16[512,512]{1,0:T(8,128)(2,1)S(1)}, u32[]{:S(2)}, u32[]{:S(2)}) collective-permute-start(bf16[512,512]{1,0:T(8,128)(2,1)} %shard_map.262.refs_5_), channel_id=1, source_target_pairs={{0,2},{1,3},{2,0},{3,1},{4,6},{5,7},{6,4},{7,5},{8,10},{9,11},{10,... | collective-permute-start | bytes 1572872 | tf_op jit(solution)/shard_map/ppermute | solution.py:825
  111.9 23.4 %collective-permute-start.18 = (bf16[512,512]{1,0:T(8,128)(2,1)}, bf16[512,512]{1,0:T(8,128)(2,1)S(1)}, u32[]{:S(2)}, u32[]{:S(2)}) collective-permute-start(bf16[512,512]{1,0:T(8,128)(2,1)} %shard_map.262.refs_5_), channel_id=1, source_target_pairs={{0,1},{1,0},{2,3},{3,2},{4,5},{5,4},{6,7},{7,6},{8,9},{9,8},{10,11... | collective-permute-start | bytes 1572872 | tf_op jit(solution)/shard_map/ppermute | solution.py:825
  155.3 18.6 %collective-permute-start.26 = (bf16[4,256,1024]{2,1,0:T(8,128)(2,1)}, bf16[4,256,1024]{2,1,0:T(8,128)(2,1)S(1)}, u32[]{:S(2)}, u32[]{:S(2)}) collective-permute-start(bf16[4,256,1024]{2,1,0:T(8,128)(2,1)} %get-tuple-element.85), channel_id=1, source_target_pairs={{0,16},{16,0},{1,17},{17,1},{2,18},{18,2},{3,19},{19,3},{4,20},{20... | collective-permute-start | bytes 6291464 | tf_op jit(solution)/shard_map/ppermute | solution.py:825
  155.5 18.4 %all-to-all-start.2 = ((bf16[8,128,512]{2,1,0:T(8,128)(2,1)}), bf16[8,128,512]{2,1,0:T(8,128)(2,1)S(1)}, u32[]{:S(2)}, u32[]{:S(2)}) async-start(bf16[8,128,512]{2,1,0:T(8,128)(2,1)} %get-tuple-element.77), calls=%async_computation.2 | async-start | bytes 2097152 | tf_op jit(solution)/shard_map/all_to_all | solution.py:837
  159.0 150.7 %reduce-scatter.15.cloned.1.call-start = ((), (), s32[]{:S(2)}) async-start(), calls=%async_computation.14 | async-start | bytes 2621440
  179.8 158.4 %reduce-scatter.13.cloned.1.call-start = ((), (), s32[]{:S(2)}) async-start(), calls=%async_computation.13 | async-start | bytes 2621440
  220.4 29.0 %all-to-all-start.4 = ((bf16[4,256,512]{2,1,0:T(8,128)(2,1)}), bf16[4,256,512]{2,1,0:T(8,128)(2,1)S(1)}, u32[]{:S(2)}, u32[]{:S(2)}) async-start(bf16[4,256,512]{2,1,0:T(8,128)(2,1)} %shard_map.270.refs_11_), calls=%async_computation.4 | async-start | bytes 2097152 | tf_op jit(solution)/shard_map/all_to_all | solution.py:837
  254.0 20.8 %all-to-all-start.5 = ((bf16[4,256,512]{2,1,0:T(8,128)(2,1)}), bf16[4,256,512]{2,1,0:T(8,128)(2,1)S(1)}, u32[]{:S(2)}, u32[]{:S(2)}) async-start(bf16[4,256,512]{2,1,0:T(8,128)(2,1)} %shard_map.274), calls=%async_computation.5 | async-start | bytes 2097152 | tf_op jit(solution)/shard_map/all_to_all | solution.py:837
  305.0 29.9 %all-to-all-start.6 = ((bf16[4,64,1280]{2,1,0:T(8,128)(2,1)}), bf16[4,64,1280]{2,1,0:T(8,128)(2,1)S(1)}, u32[]{:S(2)}, u32[]{:S(2)}) async-start(bf16[4,64,1280]{2,1,0:T(8,128)(2,1)} %bitcast.98), calls=%async_computation.6 | async-start | bytes 1310720 | tf_op jit(solution)/shard_map/all_to_all | solution.py:837
  309.7 32.0 %reduce-scatter.11.cloned.1.call-start = ((), (), s32[]{:S(2)}) async-start(), calls=%async_computation.12 | async-start | bytes 655360 | tf_op jit(solution)/shard_map/reduce_scatter | solution.py:1062
  310.5 49.7 %reduce-scatter.9.cloned.1.call-start = ((), (), s32[]{:S(2)}) async-start(), calls=%async_computation.11 | async-start | bytes 655360 | tf_op jit(solution)/shard_map/reduce_scatter | solution.py:1075
  (56 other events, 322.9 us)
Sparse Core Ops, SparseCore 0:
  180.0 35.0 reduce-scatter.14
  218.3 54.9 reduce-scatter.12
  312.8 24.6 reduce-scatter.10
  339.6 20.4 reduce-scatter.8
